TPU v7x, 256 devices: a whole 4x4x8 slice. The times are simulated.
256 devices in a mesh: grid: 16 (over z_hi, x, core), orb: 16 (over z_lo, y).
Axes of the slice: x: 4, y: 4, z: 8 (z_hi: 2, z_lo: 4; z = z_hi * 4 + z_lo), core: 2. Of those that a mesh axis runs over, the one named last changes fastest.
Arguments:
- psi_window: bfloat16 [3072, 16384], P('orb', 'grid'), may hold values from -6 to 6
- phi_window: bfloat16 [3072, 16384], P('orb', 'grid'), may hold values from -6 to 6
- psi_region: bfloat16 [3072, 98304], P('orb', 'grid'), may hold values from -6 to 6
- phi_region: bfloat16 [3072, 98304], P('orb', 'grid'), may hold values from -6 to 6
- points: int32 [12288], P('grid'), may hold values from 0 to 6143, as said below
Outputs:
- fit_rhs: bfloat16 [16384, 16, 768], P('grid', None, 'orb')
Inputs may be any that keep to these rules, and one draw needn't show every extreme that they name: `points`: within each owner's block of 768 entries the indices are distinct; every block holds both 0 and 6143.
All inputs are finite; a program needn't handle non-finite values.
Results may differ from a plain program's by a relative error of at most 0.001.
Values may be sent and summed in bfloat16 or wider, within the bound.
No kernel may reach another device: no remote copies, remote signals or barrier semaphores. Data moves between devices by JAX's collectives and lax.ppermute only.
A program may use at most 128 MiB of HBM per device.

v0:
```python
import jax
import jax.numpy as jnp
from jax import lax
from jax.sharding import PartitionSpec as P


def per_device(psi_window, phi_window, psi_region, phi_region, points):
    psi_points = jnp.take(psi_region, points, axis=1)[:, None, :]
    phi_points = jnp.take(phi_region, points, axis=1)[:, None, :]
    psi_owners, phi_owners = (
        lax.all_gather(psi_points, "grid", axis=1, tiled=True),
        lax.all_gather(phi_points, "grid", axis=1, tiled=True),
    )
    psi_cols, phi_cols = (
        lax.all_to_all(psi_owners, "orb", split_axis=2, concat_axis=0, tiled=True),
        lax.all_to_all(phi_owners, "orb", split_axis=2, concat_axis=0, tiled=True),
    )
    all_orbs = psi_cols.shape[0]
    owners = psi_cols.shape[1]
    share = psi_cols.shape[2]
    psi_flat = psi_cols.reshape(all_orbs, owners * share)
    phi_flat = phi_cols.reshape(all_orbs, owners * share)
    rows = psi_window.shape[1]
    contract = (((0,), (0,)), ((), ()))
    occ_next = lax.dot_general(
        lax.all_gather(psi_window, "orb", axis=0, tiled=True),
        psi_flat,
        contract,
        preferred_element_type=jnp.float32,
    )
    emp_next = lax.dot_general(
        lax.all_gather(phi_window, "orb", axis=0, tiled=True),
        phi_flat,
        contract,
        preferred_element_type=jnp.float32,
    )
    fitted = (occ_next * emp_next / all_orbs).astype(jnp.bfloat16)
    return fitted.reshape(rows, owners, share)


def solution(mesh):
    in_specs = (P("orb", "grid"), P("orb", "grid"), P("orb", "grid"), P("orb", "grid"), P("grid"))
    out_specs = P("grid", None, "orb")
    return jax.shard_map(
        per_device, mesh=mesh, in_specs=in_specs, out_specs=out_specs, check_vma=False
    )
```

profile of v0, /device:TPU:38, one launch (start us, length us, event | category | flops | bytes accessed | tf_op | source)
XLA Modules:
  0.0 630.0 jit_solution(7626322272883664883)
XLA Ops:
  6.5 0.0 all-gather.11.cloned.1.call-start
  6.5 0.7 compare_select_fusion
  7.2 0.7 compare_and_fusion
  7.9 4.5 copy.14
  12.4 3.0 copy.18
  15.5 4.4 gather_fusion
  19.9 3.3 gather_fusion.1
  23.1 2.0 select_bitcast_fusion
  25.2 0.0 all-gather.11.cloned.1.call-update
  25.2 0.0 all-gather.13.cloned.1.call-start
  25.3 0.7 all-gather.13.cloned.1.call-update
  26.0 0.0 all-gather.7.cloned.1.call-start
  26.0 0.7 all-gather.7.cloned.1.call-update
  26.7 92.4 %all-gather.11.cloned.1.call-done = bf16[192,12288]{0,1:T(8,128)(2,1)} async-done(((bf16[192,768]{0,1:T(8,128)(2,1)}), bf16[192,12288]{0,1:T(8,128)(2,1)}) %all-gather.11.cloned.1.call-update) | async-done | bytes 4718608 | tf_op jit(solution)/shard_map/all_gather | solution.py:11
  119.1 9.1 %copy.15 = bf16[192,16,768]{0,1,2:T(8,128)(2,1)} copy(bf16[192,16,768]{0,2,1:T(8,128)(2,1)} %bitcast.28) | data formatting | bytes 9437184 | tf_op jit(solution)/shard_map/all_gather | solution.py:11
  128.2 6.0 all-to-all-start
  134.2 0.0 all-gather.9.cloned.1.call-start
  134.2 0.5 all-gather.9.cloned.1.call-update
  134.7 138.4 %all-gather.13.cloned.1.call-done = bf16[192,12288]{0,1:T(8,128)(2,1)} async-done(((bf16[192,768]{0,1:T(8,128)(2,1)}), bf16[192,12288]{0,1:T(8,128)(2,1)}) %all-gather.13.cloned.1.call-update) | async-done | bytes 4718608 | tf_op jit(solution)/shard_map/all_gather | solution.py:12
  273.1 9.0 %copy.19 = bf16[192,16,768]{0,1,2:T(8,128)(2,1)} copy(bf16[192,16,768]{0,2,1:T(8,128)(2,1)} %bitcast.27) | data formatting | bytes 9437184 | tf_op jit(solution)/shard_map/all_gather | solution.py:12
  282.1 92.8 %all-to-all-done = bf16[192,16,768]{0,1,2:T(8,128)(2,1)} async-done(((bf16[192,16,768]{0,1,2:T(8,128)(2,1)}), bf16[192,16,768]{0,1,2:T(8,128)(2,1)}, u32[]{:S(2)}, u32[]{:S(2)}) %all-to-all-start) | async-done | bytes 4718624 | tf_op jit(solution)/shard_map/all_to_all | solution.py:15
  374.9 8.3 %all-to-all-start.1 = ((bf16[192,16,768]{0,1,2:T(8,128)(2,1)}), bf16[192,16,768]{0,1,2:T(8,128)(2,1)}, u32[]{:S(2)}, u32[]{:S(2)}) async-start(bf16[192,16,768]{0,1,2:T(8,128)(2,1)} %copy.19), calls=%async_computation.1 | async-start | bytes 12582912 | tf_op jit(solution)/shard_map/all_to_all | solution.py:16
  383.2 9.1 %copy.17 = bf16[16,192,16,48]{1,0,3,2:T(8,128)(2,1)} copy(bf16[16,192,16,48]{1,2,3,0:T(8,128)(2,1)} %bitcast.4) | data formatting | bytes 9437184 | tf_op jit(solution)/shard_map/all_to_all | solution.py:15
  392.3 10.7 %reshape.16 = bf16[3072,768]{0,1:T(8,128)(2,1)} reshape(bf16[16,192,16,48]{1,0,3,2:T(8,128)(2,1)} %copy.17) | data formatting | bytes 9437184 | tf_op jit(solution)/shard_map/reshape | solution.py:21
  403.0 182.9 %all-to-all-done.1 = bf16[192,16,768]{0,1,2:T(8,128)(2,1)} async-done(((bf16[192,16,768]{0,1,2:T(8,128)(2,1)}), bf16[192,16,768]{0,1,2:T(8,128)(2,1)}, u32[]{:S(2)}, u32[]{:S(2)}) %all-to-all-start.1) | async-done | bytes 4718624 | tf_op jit(solution)/shard_map/all_to_all | solution.py:16
  585.9 9.0 %copy.21 = bf16[16,192,16,48]{1,0,3,2:T(8,128)(2,1)} copy(bf16[16,192,16,48]{1,2,3,0:T(8,128)(2,1)} %bitcast.9) | data formatting | bytes 9437184 | tf_op jit(solution)/shard_map/all_to_all | solution.py:16
  594.8 10.7 %reshape.17 = bf16[3072,768]{0,1:T(8,128)(2,1)} reshape(bf16[16,192,16,48]{1,0,3,2:T(8,128)(2,1)} %copy.21) | data formatting | bytes 9437184 | tf_op jit(solution)/shard_map/reshape | solution.py:22
  605.5 0.0 all-gather.7.cloned.1.call-done
  605.5 8.5 %fusion = f32[768,1024]{1,0:T(8,128)S(1)} fusion(bf16[3072,768]{0,1:T(8,128)(2,1)} %reshape.16, bf16[3072,1024]{1,0:T(8,128)(2,1)} %all-gather.7.cloned.1.call-done), kind=kOutput, calls=%fused_computation.8 | convolution fusion | flops 4831838208 | bytes 14155776 | tf_op jit(solution)/shard_map/dot_general | solution.py:25
  614.0 0.0 all-gather.9.cloned.1.call-done
  614.0 9.4 %multiply_convert_fusion = bf16[768,1024]{1,0:T(8,128)(2,1)} fusion(f32[768,1024]{1,0:T(8,128)S(1)} %fusion, bf16[3072,768]{0,1:T(8,128)(2,1)} %reshape.17, bf16[3072,1024]{1,0:T(8,128)(2,1)} %all-gather.9.cloned.1.call-done), kind=kOutput, calls=%fused_computation.2 | convolution fusion | flops 4834197504 | bytes 15728640 | tf_op jit(solution)/shard_map/dot_general | solution.py:31
  (1 shorter events, 0.0 us)
Async XLA Ops:
  6.5 112.6 %all-gather.11.cloned.1.call-start = ((), (), s32[]{:S(2)}) async-start(), calls=%async_computation.4 | async-start | bytes 6684672 | tf_op jit(solution)/shard_map/all_gather | solution.py:11
  25.2 247.9 %all-gather.13.cloned.1.call-start = ((), (), s32[]{:S(2)}) async-start(), calls=%async_computation.5 | async-start | bytes 6684672 | tf_op jit(solution)/shard_map/all_gather | solution.py:12
  26.0 579.5 %all-gather.7.cloned.1.call-start = ((), (), s32[]{:S(2)}) async-start(), calls=%async_computation.2 | async-start | bytes 6684672 | tf_op jit(solution)/shard_map/all_gather | solution.py:26
  128.2 246.8 %all-to-all-start = ((bf16[192,16,768]{0,1,2:T(8,128)(2,1)}), bf16[192,16,768]{0,1,2:T(8,128)(2,1)}, u32[]{:S(2)}, u32[]{:S(2)}) async-start(bf16[192,16,768]{0,1,2:T(8,128)(2,1)} %copy.15), calls=%async_computation | async-start | bytes 12582912 | tf_op jit(solution)/shard_map/all_to_all | solution.py:15
  134.2 479.9 %all-gather.9.cloned.1.call-start = ((), (), s32[]{:S(2)}) async-start(), calls=%async_computation.3 | async-start | bytes 6684672 | tf_op jit(solution)/shard_map/all_gather | solution.py:32
  374.9 210.9 %all-to-all-start.1 = ((bf16[192,16,768]{0,1,2:T(8,128)(2,1)}), bf16[192,16,768]{0,1,2:T(8,128)(2,1)}, u32[]{:S(2)}, u32[]{:S(2)}) async-start(bf16[192,16,768]{0,1,2:T(8,128)(2,1)} %copy.19), calls=%async_computation.1 | async-start | bytes 12582912 | tf_op jit(solution)/shard_map/all_to_all | solution.py:16
Sparse Core Ops, SparseCore 0:
  25.3 93.7 all-gather.10
  121.9 151.2 all-gather.12
  274.9 107.1 all-gather.6
  383.8 194.5 all-gather.8
where the time goes:
time: 631 us; the launch traced here: 630 us
  waiting for transfers between devices  508 us (81%)
  local copies, waits for them, and re-layouts  72.6 us (12%)
  matrix products  17.9 us (3%)
  starting transfers between devices  14.4 us (2%)
  between operations  13.2 us (2%)
    all_to_all x1, waiting for transfers between devices, per_device(): lax.all_to_all(phi_owners, 'orb', split_axis=2, concat_axis=0, tiled=True)  183 us
    all_gather x1, waiting for transfers between devices, per_device(): lax.all_gather(phi_points, 'grid', axis=1, tiled=True)  138 us
    all_to_all x1, waiting for transfers between devices, per_device(): lax.all_to_all(psi_owners, 'orb', split_axis=2, concat_axis=0, tiled=True)  92.8 us
    all_gather x1, waiting for transfers between devices, per_device(): lax.all_gather(psi_points, 'grid', axis=1, tiled=True)  92.4 us
  transfers between devices with their start and end apart: 6, of which 4 were waited for; matrix products, arithmetic and copies ran while one was open for 10% of the time, Pallas kernels for 0%

commit v1 on v0

v1 whole, which is shorter than its diff:
```python
import functools

import jax
import jax.numpy as jnp
from jax import lax
from jax.experimental import pallas as pl
from jax.experimental.pallas import tpu as pltpu
from jax.sharding import Mesh, PartitionSpec as P

AXES = ("zhi", "x", "core", "zlo", "y")
SIZES = {"zhi": 2, "x": 4, "core": 2, "zlo": 4, "y": 4}
GRID = ("zhi", "x", "core")
ORB = ("zlo", "y")

NPTS = 768
SHARE = 48
ORBS = 192
REGION = 6144
ROWS = 1024
KSLOT = 4 * ORBS
CHUNK = 1024
VMEM_LIMIT = 56 * 1024 * 1024


def shift(value, axis, step):
    n = SIZES[axis]
    return lax.ppermute(value, axis, [(i, (i + step) % n) for i in range(n)])


def gather_kernel(points_ref, psi_ref, phi_ref, out_ref, acc_ref):
    step = pl.program_id(0)
    columns = lax.broadcasted_iota(jnp.int32, (NPTS, CHUNK), 1) + step * CHUNK
    pick = jnp.where(points_ref[...] == columns, 1.0, 0.0).astype(jnp.bfloat16)
    both = jnp.concatenate([psi_ref[...], phi_ref[...]], axis=0)
    part = lax.dot_general(
        pick, both, (((1,), (1,)), ((), ())), preferred_element_type=jnp.float32
    )

    @pl.when(step == 0)
    def _():
        acc_ref[...] = part

    @pl.when(step > 0)
    def _():
        acc_ref[...] += part

    @pl.when(step == pl.num_programs(0) - 1)
    def _():
        out_ref[...] = acc_ref[...].astype(jnp.bfloat16)


def gather_points(points, psi_region, phi_region):
    steps = REGION // CHUNK
    return pl.pallas_call(
        gather_kernel,
        grid=(steps,),
        in_specs=[
            pl.BlockSpec((NPTS, 1), lambda j: (0, 0)),
            pl.BlockSpec((ORBS, CHUNK), lambda j: (0, j)),
            pl.BlockSpec((ORBS, CHUNK), lambda j: (0, j)),
        ],
        out_specs=pl.BlockSpec((NPTS, 2 * ORBS), lambda j: (0, 0)),
        out_shape=jax.ShapeDtypeStruct((NPTS, 2 * ORBS), jnp.bfloat16),
        scratch_shapes=[pltpu.VMEM((NPTS, 2 * ORBS), jnp.float32)],
        compiler_params=pltpu.CompilerParams(vmem_limit_bytes=VMEM_LIMIT),
        cost_estimate=pl.CostEstimate(
            flops=2 * NPTS * REGION * 2 * ORBS, bytes_accessed=2 * ORBS * REGION * 2, transcendentals=0
        ),
        name="gather_points",
    )(points, psi_region, phi_region)


def gram_kernel(slots, first, last, pos_ref, *refs):
    n_w = 5 * len(slots)
    w_refs, refs = refs[:n_w], refs[n_w:]
    p_refs, refs = refs[:10], refs[10:]
    if not first:
        acc_in, refs = refs[0], refs[1:]
    out_ref, w_buf, p_buf, acc, w_sem, p_sem, a_sem = refs
    x, core, zlo, y = pos_ref[0], pos_ref[1], pos_ref[2], pos_ref[3]

    copies = []
    for s, slot in enumerate(slots):
        mine = []
        own, ym, yp, fm, fp = w_refs[5 * s : 5 * s + 5]
        for j, (ref, e) in enumerate(((own, 0), (ym, 3), (yp, 1))):
            mine.append(pltpu.make_async_copy(ref, w_buf.at[s, :, (y + e) % 4], w_sem.at[s, j]))
        for j, ref in enumerate((fm, fp)):
            mine.append(pltpu.make_async_copy(ref, w_buf.at[s, j, (y + 2) % 4], w_sem.at[s, 3 + j]))
        zsel = (zlo - slot + 4) % 4
        for swap in range(2):
            who = (core + swap) % 2
            own, dm, dp, f1, f2 = p_refs[5 * swap : 5 * swap + 5]
            for zhi in range(2):
                for j, (ref, e) in enumerate(((own, 0), (dm, 3), (dp, 1))):
                    mine.append(
                        pltpu.make_async_copy(
                            ref.at[zhi * 4 + zsel],
                            p_buf.at[s, zhi * 8 + ((x + e) % 4) * 2 + who],
                            p_sem.at[s, swap, zhi, j],
                        )
                    )
                mine.append(
                    pltpu.make_async_copy(
                        (f1, f2)[zhi].at[zsel],
                        p_buf.at[s, zhi * 8 + ((x + 2) % 4) * 2 + who],
                        p_sem.at[s, swap, zhi, 3],
                    )
                )
        for copy in mine:
            copy.start()
        copies.append(mine)
    if not first:
        load = pltpu.make_async_copy(acc_in, acc, a_sem)
        load.start()

    tile = 256
    for s in range(len(slots)):
        for copy in copies[s]:
            copy.wait()
        if s == 0 and not first:
            load.wait()

        def body(n, _):
            cols = pl.ds(pl.multiple_of(n * tile, tile), tile)
            grams = []
            for m in range(2):
                lhs = p_buf[s, :, :, m * KSLOT : (m + 1) * KSLOT].reshape(NPTS, KSLOT)
                rhs = w_buf[s, m, :, :, cols].reshape(KSLOT, tile)
                part = jnp.dot(lhs, rhs, preferred_element_type=jnp.float32)
                if not (first and s == 0):
                    part += acc[m, :, cols]
                grams.append(part)
            if last and s == len(slots) - 1:
                fitted = grams[0] * grams[1] * (1.0 / (16 * ORBS))
                out_ref[:, cols] = fitted.astype(jnp.bfloat16)
            else:
                for m in range(2):
                    acc[m, :, cols] = grams[m]
            return 0

        lax.fori_loop(0, ROWS // tile, body, 0)
    if not last:
        store = pltpu.make_async_copy(acc, out_ref, a_sem)
        store.start()
        store.wait()


def gram(slots, first, last, pos, w_parts, p_parts, acc=None):
    n = len(slots)
    any_spec = pl.BlockSpec(memory_space=pl.ANY)
    operands = list(w_parts) + list(p_parts) + ([] if first else [acc])
    if last:
        out_shape = jax.ShapeDtypeStruct((NPTS, ROWS), jnp.bfloat16)
        out_spec = pl.BlockSpec(memory_space=pltpu.VMEM)
    else:
        out_shape = jax.ShapeDtypeStruct((2, NPTS, ROWS), jnp.float32)
        out_spec = any_spec
    return pl.pallas_call(
        functools.partial(gram_kernel, slots, first, last),
        in_specs=[pl.BlockSpec(memory_space=pltpu.SMEM)] + [any_spec] * len(operands),
        out_specs=out_spec,
        out_shape=out_shape,
        scratch_shapes=[
            pltpu.VMEM((n, 2, 4, ORBS, ROWS), jnp.bfloat16),
            pltpu.VMEM((n, 16, SHARE, 2 * KSLOT), jnp.bfloat16),
            pltpu.VMEM((2, NPTS, ROWS), jnp.float32),
            pltpu.SemaphoreType.DMA((n, 5)),
            pltpu.SemaphoreType.DMA((n, 2, 2, 4)),
            pltpu.SemaphoreType.DMA,
        ],
        compiler_params=pltpu.CompilerParams(vmem_limit_bytes=VMEM_LIMIT),
        cost_estimate=pl.CostEstimate(
            flops=2 * 2 * n * NPTS * KSLOT * ROWS, bytes_accessed=n * 6 * 2**20, transcendentals=0
        ),
        name="gram_last" if last else "gram_first",
    )(pos, *operands)


def per_device(psi_window, phi_window, psi_region, phi_region, points):
    pos = jnp.stack([lax.axis_index(a) for a in ("x", "core", "zlo", "y")]).astype(jnp.int32)

    own = jnp.stack([psi_window, phi_window])
    slots = [own] + [shift(own, "zlo", d) for d in (1, 2, 3)]
    w_parts = []
    for slot in slots:
        below, above = shift(slot, "y", 1), shift(slot, "y", -1)
        far_psi, far_phi = shift(below[0], "y", 1), shift(above[1], "y", -1)
        w_parts.append((slot, below, above, far_psi, far_phi))

    order = points.reshape(4, 4, SHARE).transpose(1, 0, 2).reshape(NPTS, 1)
    picked = gather_points(order, psi_region, phi_region).reshape(4, 4, SHARE, 2 * ORBS)
    by_y = lax.all_to_all(picked, "y", 0, 0, tiled=True)
    cols = by_y.reshape(4, 4, SHARE, 2, ORBS).transpose(1, 2, 3, 0, 4).reshape(4, SHARE, 2 * KSLOT)
    both = jnp.concatenate([cols, cols])
    mine = lax.all_to_all(both, ("zhi", "zlo"), 0, 0, tiled=True)
    below, above = shift(mine, "x", 1), shift(mine, "x", -1)
    far_lo, far_hi = shift(below[:4], "x", 1), shift(above[4:], "x", -1)
    p_parts = [mine, below, above, far_lo, far_hi]
    p_parts += [shift(part, "core", 1) for part in p_parts]

    acc = gram((0, 1, 2), True, False, pos, w_parts[0] + w_parts[1] + w_parts[2], p_parts)
    out = gram((3,), False, True, pos, w_parts[3], p_parts, acc)
    return out.reshape(16, SHARE, ROWS).transpose(2, 0, 1)


def solution(mesh):
    torus = Mesh(mesh.devices.reshape(tuple(SIZES[a] for a in AXES)), AXES)
    in_specs = (P(ORB, GRID), P(ORB, GRID), P(ORB, GRID), P(ORB, GRID), P(GRID))
    out_specs = P(GRID, None, ORB)
    return jax.shard_map(
        per_device, mesh=torus, in_specs=in_specs, out_specs=out_specs, check_vma=False
    )
```

time: 631 us -> 232 us (0.37)
  the two profiles are of different devices: /device:TPU:38 before, /device:TPU:96 now
where the time goes in v1:
time: 232 us
  waiting for transfers between devices  127 us (55%)
  starting transfers between devices  38.1 us (16%)
  Pallas kernels  35.8 us (15%)
  blocking collectives  14.6 us (6%)
  local copies, waits for them, and re-layouts  14 us (6%)
    ppermute x28, waiting for transfers between devices, shift(): return lax.ppermute(value, axis, [(i, (i + step) % n) for i in range(n)])  127 us
    ppermute x28, starting transfers between devices, shift(): return lax.ppermute(value, axis, [(i, (i + step) % n) for i in range(n)])  30.3 us
    pallas_call x2, Pallas kernels, gram(): pl.pallas_call(functools.partial(gram_kernel, slots, first, last), in_spe...  26.9 us
    all_to_all x1, blocking collectives, per_device(): by_y = lax.all_to_all(picked, 'y', 0, 0, tiled=True)  14.6 us
    pallas_call x1, Pallas kernels, gather_points(): pl.pallas_call(gather_kernel, grid=(steps,), in_specs=[pl.BlockSpec((NPTS...  8.97 us
    all_to_all x1, starting transfers between devices, per_device(): mine = lax.all_to_all(both, ('zhi', 'zlo'), 0, 0, tiled=True)  7.8 us
    squeeze x8, local copies, waits for them, and re-layouts, per_device(): far_psi, far_phi = (shift(below[0], 'y', 1), shift(above[1], 'y', -1))  5.19 us
  transfers between devices with their start and end apart: 29, of which 9 were waited for; matrix products, arithmetic and copies ran while one was open for 3% of the time, Pallas kernels for 7%

profile of v1, /device:TPU:96, one launch (start us, length us, event | category | flops | bytes accessed | tf_op | source)
XLA Modules:
  0.0 232.0 jit_solution(5928618642547667905)
XLA Ops:
  0.0 0.8 reshape.18
  0.8 0.9 reshape.24.points_ref
  1.7 9.0 %gather_points.1 = bf16[768,384]{1,0:T(8,128)(2,1)} custom-call(s32[768,1]{1,0:T(8,128)} %reshape.24.points_ref, bf16[192,6144]{1,0:T(8,128)(2,1)} %psi_ref.1, bf16[192,6144]{1,0:T(8,128)(2,1)} %phi_ref.1), custom_call_target="tpu_custom_call" | custom-call | flops 3623878656 | bytes 4718592 | tf_op jit(solution)/shard_map/gather_points/pallas_call | solution.py:54
  10.7 14.6 %all_to_all.10 = bf16[4,4,48,384]{3,2,1,0:T(8,128)(2,1)S(1)} all-to-all(bf16[4,4,48,384]{3,2,1,0:T(8,128)(2,1)} %bitcast.31), channel_id=1, replica_groups=mesh['zhi'=2,'x'=4,'core'=2,'zlo'=4,'y'=4] {'y'}, dimensions={0} | all-to-all | bytes 1179648 | tf_op jit(solution)/shard_map/all_to_all | solution.py:193
  25.7 1.0 copy.8
  26.7 0.9 reshape.22
  27.6 1.1 pad_maximum_fusion
  28.7 7.8 %all-to-all-start.1 = ((bf16[8,48,1536]{2,1,0:T(8,128)(2,1)}), bf16[8,48,1536]{2,1,0:T(8,128)(2,1)S(1)}, u32[]{:S(2)}, u32[]{:S(2)}) async-start(bf16[8,48,1536]{2,1,0:T(8,128)(2,1)} %pad_maximum_fusion), calls=%async_computation.1 | async-start | bytes 2359296 | tf_op jit(solution)/shard_map/all_to_all | solution.py:196
  36.7 0.6 collective-permute-start.14
  37.4 2.7 %collective-permute-start.15 = (bf16[2,192,1024]{2,1,0:T(8,128)(2,1)S(1)}, bf16[2,192,1024]{2,1,0:T(8,128)(2,1)S(1)}, u32[]{:S(2)}, u32[]{:S(2)}) collective-permute-start(bf16[2,192,1024]{2,1,0:T(8,128)(2,1)S(1)} %pad_maximum_fusion.1.refs_0_), channel_id=1, source_target_pairs={{0,3},{1,0},{2,1},{3,2},{4,7},{5,4},{6,5},{7,6},{8,11},{9,8},{10,9... | collective-permute-start | bytes 2359304 | tf_op jit(solution)/shard_map/ppermute | solution.py:27
  40.0 1.9 collective-permute-start.23
  42.5 36.5 %collective-permute-done.18.refs_5_ = bf16[2,192,1024]{2,1,0:T(8,128)(2,1)} collective-permute-done((bf16[2,192,1024]{2,1,0:T(8,128)(2,1)S(1)}, bf16[2,192,1024]{2,1,0:T(8,128)(2,1)}, u32[]{:S(2)}, u32[]{:S(2)}) %collective-permute-start.18) | collective-permute-done | bytes 786464 | tf_op jit(solution)/shard_map/ppermute | solution.py:27
  79.1 0.6 collective-permute-start.19
  79.6 2.7 %collective-permute-start.20 = (bf16[2,192,1024]{2,1,0:T(8,128)(2,1)}, bf16[2,192,1024]{2,1,0:T(8,128)(2,1)}, u32[]{:S(2)}, u32[]{:S(2)}) collective-permute-start(bf16[2,192,1024]{2,1,0:T(8,128)(2,1)} %collective-permute-done.18.refs_5_), channel_id=1, source_target_pairs={{0,3},{1,0},{2,1},{3,2},{4,7},{5,4},{6,5},{7,6},{8,11},{9,8},{10,9... | collective-permute-start | bytes 2359304 | tf_op jit(solution)/shard_map/ppermute | solution.py:27
  82.5 46.0 %collective-permute-done.23.refs_10_ = bf16[2,192,1024]{2,1,0:T(8,128)(2,1)} collective-permute-done((bf16[2,192,1024]{2,1,0:T(8,128)(2,1)S(1)}, bf16[2,192,1024]{2,1,0:T(8,128)(2,1)}, u32[]{:S(2)}, u32[]{:S(2)}) %collective-permute-start.23) | collective-permute-done | bytes 786464 | tf_op jit(solution)/shard_map/ppermute | solution.py:27
  128.5 1.2 collective-permute-start.17
  129.6 0.9 collective-permute-start.24
  130.6 1.7 collective-permute-start.5
  132.3 7.3 %collective-permute-done.17.refs_4_ = bf16[192,1024]{1,0:T(8,128)(2,1)} collective-permute-done((bf16[192,1024]{1,0:T(8,128)(2,1)S(1)}, bf16[192,1024]{1,0:T(8,128)(2,1)}, u32[]{:S(2)}, u32[]{:S(2)}) %collective-permute-start.17) | collective-permute-done | bytes 393248 | tf_op jit(solution)/shard_map/ppermute | solution.py:27
  139.6 2.7 %collective-permute-start.6 = (bf16[8,48,1536]{2,1,0:T(8,128)(2,1)S(1)}, bf16[8,48,1536]{2,1,0:T(8,128)(2,1)S(1)}, u32[]{:S(2)}, u32[]{:S(2)}) collective-permute-start(bf16[8,48,1536]{2,1,0:T(8,128)(2,1)S(1)} %all-to-all-done.1.refs_15_.refs_5_), channel_id=1, source_target_pairs={{0,96},{32,0},{64,32},{96,64},{1,97},{33,1},{65,33},{97,65},{2,98}... | collective-permute-start | bytes 3538952 | tf_op jit(solution)/shard_map/ppermute | solution.py:27
  142.3 2.4 %collective-permute-start.25 = (bf16[2,192,1024]{2,1,0:T(8,128)(2,1)}, bf16[2,192,1024]{2,1,0:T(8,128)(2,1)S(1)}, u32[]{:S(2)}, u32[]{:S(2)}) collective-permute-start(bf16[2,192,1024]{2,1,0:T(8,128)(2,1)} %collective-permute-done.23.refs_10_), channel_id=1, source_target_pairs={{0,3},{1,0},{2,1},{3,2},{4,7},{5,4},{6,5},{7,6},{8,11},{9,8},{10,9... | collective-permute-start | bytes 2359304 | tf_op jit(solution)/shard_map/ppermute | solution.py:27
  144.7 1.0 slice_bitcast_fusion.3
  145.7 1.0 slice_bitcast_fusion.2
  146.7 4.9 %collective-permute-done.24.refs_11_ = bf16[2,192,1024]{2,1,0:T(8,128)(2,1)} collective-permute-done((bf16[2,192,1024]{2,1,0:T(8,128)(2,1)}, bf16[2,192,1024]{2,1,0:T(8,128)(2,1)}, u32[]{:S(2)}, u32[]{:S(2)}) %collective-permute-start.24) | collective-permute-done | bytes 786464 | tf_op jit(solution)/shard_map/ppermute | solution.py:27
  151.6 1.0 slice_bitcast_fusion.1
  152.6 10.4 %collective-permute-done.25.refs_12_ = bf16[2,192,1024]{2,1,0:T(8,128)(2,1)S(1)} collective-permute-done((bf16[2,192,1024]{2,1,0:T(8,128)(2,1)}, bf16[2,192,1024]{2,1,0:T(8,128)(2,1)S(1)}, u32[]{:S(2)}, u32[]{:S(2)}) %collective-permute-start.25) | collective-permute-done | bytes 786464 | tf_op jit(solution)/shard_map/ppermute | solution.py:27
  163.0 0.6 collective-permute-start.21
  163.6 4.8 %collective-permute-done.1.refs_1_ = bf16[2,192,1024]{2,1,0:T(8,128)(2,1)S(1)} collective-permute-done((bf16[2,192,1024]{2,1,0:T(8,128)(2,1)}, bf16[2,192,1024]{2,1,0:T(8,128)(2,1)S(1)}, u32[]{:S(2)}, u32[]{:S(2)}) %collective-permute-start.1) | collective-permute-done | bytes 786464 | tf_op jit(solution)/shard_map/ppermute | solution.py:27
  168.4 2.1 collective-permute-start.26
  170.5 1.3 collective-permute-start.27
  171.8 0.9 slice.42
  172.7 0.9 slice.43
  173.6 6.3 %collective-permute-done.2.refs_2_ = bf16[2,192,1024]{2,1,0:T(8,128)(2,1)S(1)} collective-permute-done((bf16[2,192,1024]{2,1,0:T(8,128)(2,1)S(1)}, bf16[2,192,1024]{2,1,0:T(8,128)(2,1)S(1)}, u32[]{:S(2)}, u32[]{:S(2)}) %collective-permute-start.2) | collective-permute-done | bytes 786464 | tf_op jit(solution)/shard_map/ppermute | solution.py:27
  179.9 3.2 %collective-permute-start.8 = (bf16[4,48,1536]{2,1,0:T(8,128)(2,1)}, bf16[4,48,1536]{2,1,0:T(8,128)(2,1)}, u32[]{:S(2)}, u32[]{:S(2)}) collective-permute-start(bf16[4,48,1536]{2,1,0:T(8,128)(2,1)} %slice.43), channel_id=1, source_target_pairs={{0,96},{32,0},{64,32},{96,64},{1,97},{33,1},{65,33},{97,65},{2,98}... | collective-permute-start | bytes 1769480 | tf_op jit(solution)/shard_map/ppermute | solution.py:27
  183.1 5.2 %collective-permute-done.22.refs_9_ = bf16[192,1024]{1,0:T(8,128)(2,1)S(1)} collective-permute-done((bf16[192,1024]{1,0:T(8,128)(2,1)S(1)}, bf16[192,1024]{1,0:T(8,128)(2,1)S(1)}, u32[]{:S(2)}, u32[]{:S(2)}) %collective-permute-start.22) | collective-permute-done | bytes 393248 | tf_op jit(solution)/shard_map/ppermute | solution.py:27
  188.3 0.6 collective-permute-start.10
  188.9 5.7 %collective-permute-done.27.refs_14_ = bf16[192,1024]{1,0:T(8,128)(2,1)S(1)} collective-permute-done((bf16[192,1024]{1,0:T(8,128)(2,1)S(1)}, bf16[192,1024]{1,0:T(8,128)(2,1)S(1)}, u32[]{:S(2)}, u32[]{:S(2)}) %collective-permute-start.27) | collective-permute-done | bytes 393248 | tf_op jit(solution)/shard_map/ppermute | solution.py:27
  194.6 0.7 copy-done.20
  195.9 0.6 pad_add_fusion.pos_ref
  196.5 1.0 slice_bitcast_fusion.7
  197.5 1.0 slice_bitcast_fusion.6
  198.5 0.6 collective-permute-start.3
  199.2 3.3 %collective-permute-start.4 = (bf16[192,1024]{1,0:T(8,128)(2,1)S(1)}, bf16[192,1024]{1,0:T(8,128)(2,1)S(1)}, u32[]{:S(2)}, u32[]{:S(2)}) collective-permute-start(bf16[192,1024]{1,0:T(8,128)(2,1)S(1)} %slice_bitcast_fusion.6), channel_id=1, source_target_pairs={{0,3},{1,0},{2,1},{3,2},{4,7},{5,4},{6,5},{7,6},{8,11},{9,8},{10,9... | collective-permute-start | bytes 1179656 | tf_op jit(solution)/shard_map/ppermute | solution.py:27
  202.6 0.8 copy-done.9
  203.4 17.1 %gram_first.1.refs_15_ = f32[2,768,1024]{2,1,0:T(8,128)} custom-call(s32[4]{0:T(128)} %pad_add_fusion.pos_ref, bf16[2,192,1024]{2,1,0:T(8,128)(2,1)} %copy-done.7, bf16[2,192,1024]{2,1,0:T(8,128)(2,1)} %copy-done.14, bf16[2,192,1024]{2,1,0:T(8,128)(2,1)} %copy-done.15, bf16[192,1024]{1,0:T(8,128)(2,1)} %collective-permute-done.16.refs_3_, ...), custom_call_target="tpu_custom_call" | custom-call | flops 7247757312 | bytes 18874368 | tf_op jit(solution)/shard_map/gram_first/pallas_call | solution.py:159
  220.5 0.7 copy-done.12
  221.3 0.7 copy-done.13
  222.0 9.8 %gram_last.1 = bf16[768,1024]{1,0:T(8,128)(2,1)} custom-call(s32[4]{0:T(128)} %pad_add_fusion.pos_ref, bf16[2,192,1024]{2,1,0:T(8,128)(2,1)} %copy-done.5, bf16[2,192,1024]{2,1,0:T(8,128)(2,1)} %copy-done.3, bf16[2,192,1024]{2,1,0:T(8,128)(2,1)} %copy-done.4, bf16[192,1024]{1,0:T(8,128)(2,1)} %copy-done.12, bf16[192,1024]{1,0:T(8,128)(2,1)} %copy-done.13, ...), custom_call_target="tpu_custom_call" | custom-call | flops 2415919104 | bytes 6291456 | tf_op jit(solution)/shard_map/gram_last/pallas_call | solution.py:159
  (75 shorter events, 2.0 us)
Async XLA Ops:
  28.7 7.8 %copy-start.10 = (bf16[192,1024]{1,0:T(8,128)(2,1)S(1)}, bf16[192,1024]{1,0:T(8,128)(2,1)}, u32[]{:S(2)}) copy-start(bf16[192,1024]{1,0:T(8,128)(2,1)} %param.6) | copy-start | bytes 1179652
  28.7 7.8 %copy-start.11 = (bf16[192,1024]{1,0:T(8,128)(2,1)S(1)}, bf16[192,1024]{1,0:T(8,128)(2,1)}, u32[]{:S(2)}) copy-start(bf16[192,1024]{1,0:T(8,128)(2,1)} %param.5) | copy-start | bytes 1179652
  28.7 101.8 %all-to-all-start.1 = ((bf16[8,48,1536]{2,1,0:T(8,128)(2,1)}), bf16[8,48,1536]{2,1,0:T(8,128)(2,1)S(1)}, u32[]{:S(2)}, u32[]{:S(2)}) async-start(bf16[8,48,1536]{2,1,0:T(8,128)(2,1)} %pad_maximum_fusion), calls=%async_computation.1 | async-start | bytes 2359296 | tf_op jit(solution)/shard_map/all_to_all | solution.py:196
  36.6 93.9 %copy-start.7 = (bf16[2,192,1024]{2,1,0:T(8,128)(2,1)}, bf16[2,192,1024]{2,1,0:T(8,128)(2,1)S(1)}, u32[]{:S(2)}) copy-start(bf16[2,192,1024]{2,1,0:T(8,128)(2,1)S(1)} %pad_maximum_fusion.1.refs_0_) | copy-start | bytes 2359300
  36.6 42.4 %collective-permute-start.18 = (bf16[2,192,1024]{2,1,0:T(8,128)(2,1)S(1)}, bf16[2,192,1024]{2,1,0:T(8,128)(2,1)}, u32[]{:S(2)}, u32[]{:S(2)}) collective-permute-start(bf16[2,192,1024]{2,1,0:T(8,128)(2,1)S(1)} %pad_maximum_fusion.1.refs_0_), channel_id=1, source_target_pairs={{0,4},{4,8},{8,12},{12,0},{1,5},{5,9},{9,13},{13,1},{2,6},{6,10},{... | collective-permute-start | bytes 2359304 | tf_op jit(solution)/shard_map/ppermute | solution.py:27
  36.7 42.9 %collective-permute-start.14 = (bf16[2,192,1024]{2,1,0:T(8,128)(2,1)S(1)}, bf16[2,192,1024]{2,1,0:T(8,128)(2,1)S(1)}, u32[]{:S(2)}, u32[]{:S(2)}) collective-permute-start(bf16[2,192,1024]{2,1,0:T(8,128)(2,1)S(1)} %pad_maximum_fusion.1.refs_0_), channel_id=1, source_target_pairs={{0,1},{1,2},{2,3},{3,0},{4,5},{5,6},{6,7},{7,4},{8,9},{9,10},{10,1... | collective-permute-start | bytes 2359304 | tf_op jit(solution)/shard_map/ppermute | solution.py:27
  37.4 45.0 %collective-permute-start.15 = (bf16[2,192,1024]{2,1,0:T(8,128)(2,1)S(1)}, bf16[2,192,1024]{2,1,0:T(8,128)(2,1)S(1)}, u32[]{:S(2)}, u32[]{:S(2)}) collective-permute-start(bf16[2,192,1024]{2,1,0:T(8,128)(2,1)S(1)} %pad_maximum_fusion.1.refs_0_), channel_id=1, source_target_pairs={{0,3},{1,0},{2,1},{3,2},{4,7},{5,4},{6,5},{7,6},{8,11},{9,8},{10,9... | collective-permute-start | bytes 2359304 | tf_op jit(solution)/shard_map/ppermute | solution.py:27
  40.0 88.4 %collective-permute-start.23 = (bf16[2,192,1024]{2,1,0:T(8,128)(2,1)S(1)}, bf16[2,192,1024]{2,1,0:T(8,128)(2,1)}, u32[]{:S(2)}, u32[]{:S(2)}) collective-permute-start(bf16[2,192,1024]{2,1,0:T(8,128)(2,1)S(1)} %pad_maximum_fusion.1.refs_0_), channel_id=1, source_target_pairs={{0,8},{4,12},{8,0},{12,4},{1,9},{5,13},{9,1},{13,5},{2,10},{6,14},... | collective-permute-start | bytes 2359304 | tf_op jit(solution)/shard_map/ppermute | solution.py:27
  42.0 87.7 %collective-permute-start = (bf16[2,192,1024]{2,1,0:T(8,128)(2,1)S(1)}, bf16[2,192,1024]{2,1,0:T(8,128)(2,1)S(1)}, u32[]{:S(2)}, u32[]{:S(2)}) collective-permute-start(bf16[2,192,1024]{2,1,0:T(8,128)(2,1)S(1)} %pad_maximum_fusion.1.refs_0_), channel_id=1, source_target_pairs={{0,12},{4,0},{8,4},{12,8},{1,13},{5,1},{9,5},{13,9},{2,14},{6,2},{... | collective-permute-start | bytes 2359304 | tf_op jit(solution)/shard_map/ppermute | solution.py:27
  79.1 63.3 %collective-permute-start.19 = (bf16[2,192,1024]{2,1,0:T(8,128)(2,1)}, bf16[2,192,1024]{2,1,0:T(8,128)(2,1)}, u32[]{:S(2)}, u32[]{:S(2)}) collective-permute-start(bf16[2,192,1024]{2,1,0:T(8,128)(2,1)} %collective-permute-done.18.refs_5_), channel_id=1, source_target_pairs={{0,1},{1,2},{2,3},{3,0},{4,5},{5,6},{6,7},{7,4},{8,9},{9,10},{10,1... | collective-permute-start | bytes 2359304 | tf_op jit(solution)/shard_map/ppermute | solution.py:27
  79.6 50.9 %copy-start.14 = (bf16[2,192,1024]{2,1,0:T(8,128)(2,1)}, bf16[2,192,1024]{2,1,0:T(8,128)(2,1)S(1)}, u32[]{:S(2)}) copy-start(bf16[2,192,1024]{2,1,0:T(8,128)(2,1)S(1)} %collective-permute-done.14.refs_1_) | copy-start | bytes 2359300
  79.6 65.1 %collective-permute-start.20 = (bf16[2,192,1024]{2,1,0:T(8,128)(2,1)}, bf16[2,192,1024]{2,1,0:T(8,128)(2,1)}, u32[]{:S(2)}, u32[]{:S(2)}) collective-permute-start(bf16[2,192,1024]{2,1,0:T(8,128)(2,1)} %collective-permute-done.18.refs_5_), channel_id=1, source_target_pairs={{0,3},{1,0},{2,1},{3,2},{4,7},{5,4},{6,5},{7,6},{8,11},{9,8},{10,9... | collective-permute-start | bytes 2359304 | tf_op jit(solution)/shard_map/ppermute | solution.py:27
  82.3 48.2 %copy-start.15 = (bf16[2,192,1024]{2,1,0:T(8,128)(2,1)}, bf16[2,192,1024]{2,1,0:T(8,128)(2,1)S(1)}, u32[]{:S(2)}) copy-start(bf16[2,192,1024]{2,1,0:T(8,128)(2,1)S(1)} %collective-permute-done.15.refs_2_) | copy-start | bytes 2359300
  82.4 48.2 %collective-permute-start.16 = (bf16[192,1024]{1,0:T(8,128)(2,1)S(1)}, bf16[192,1024]{1,0:T(8,128)(2,1)}, u32[]{:S(2)}, u32[]{:S(2)}) collective-permute-start(bf16[192,1024]{1,0:T(8,128)(2,1)S(1)} %slice_bitcast_fusion.5), channel_id=1, source_target_pairs={{0,1},{1,2},{2,3},{3,0},{4,5},{5,6},{6,7},{7,4},{8,9},{9,10},{10,1... | collective-permute-start | bytes 1179656 | tf_op jit(solution)/shard_map/ppermute | solution.py:27
  128.5 11.1 %collective-permute-start.17 = (bf16[192,1024]{1,0:T(8,128)(2,1)S(1)}, bf16[192,1024]{1,0:T(8,128)(2,1)}, u32[]{:S(2)}, u32[]{:S(2)}) collective-permute-start(bf16[192,1024]{1,0:T(8,128)(2,1)S(1)} %slice_bitcast_fusion.4), channel_id=1, source_target_pairs={{0,3},{1,0},{2,1},{3,2},{4,7},{5,4},{6,5},{7,6},{8,11},{9,8},{10,9... | collective-permute-start | bytes 1179656 | tf_op jit(solution)/shard_map/ppermute | solution.py:27
  129.6 0.9 copy-start.5
  129.6 22.0 %collective-permute-start.24 = (bf16[2,192,1024]{2,1,0:T(8,128)(2,1)}, bf16[2,192,1024]{2,1,0:T(8,128)(2,1)}, u32[]{:S(2)}, u32[]{:S(2)}) collective-permute-start(bf16[2,192,1024]{2,1,0:T(8,128)(2,1)} %collective-permute-done.23.refs_10_), channel_id=1, source_target_pairs={{0,1},{1,2},{2,3},{3,0},{4,5},{5,6},{6,7},{7,4},{8,9},{9,10},{10,1... | collective-permute-start | bytes 2359304 | tf_op jit(solution)/shard_map/ppermute | solution.py:27
  130.5 57.7 %copy-start = (bf16[8,48,1536]{2,1,0:T(8,128)(2,1)}, bf16[8,48,1536]{2,1,0:T(8,128)(2,1)S(1)}, u32[]{:S(2)}) copy-start(bf16[8,48,1536]{2,1,0:T(8,128)(2,1)S(1)} %all-to-all-done.1.refs_15_.refs_5_) | copy-start | bytes 3538948
  130.6 21.1 %copy-start.6 = (bf16[2,192,1024]{2,1,0:T(8,128)(2,1)S(1)}, bf16[2,192,1024]{2,1,0:T(8,128)(2,1)}, u32[]{:S(2)}) copy-start(bf16[2,192,1024]{2,1,0:T(8,128)(2,1)} %copy-done.5) | copy-start | bytes 2359300
  130.6 37.8 %collective-permute-start.5 = (bf16[8,48,1536]{2,1,0:T(8,128)(2,1)S(1)}, bf16[8,48,1536]{2,1,0:T(8,128)(2,1)S(1)}, u32[]{:S(2)}, u32[]{:S(2)}) collective-permute-start(bf16[8,48,1536]{2,1,0:T(8,128)(2,1)S(1)} %all-to-all-done.1.refs_15_.refs_5_), channel_id=1, source_target_pairs={{0,32},{32,64},{64,96},{96,0},{1,33},{33,65},{65,97},{97,1},{2,34}... | collective-permute-start | bytes 3538952 | tf_op jit(solution)/shard_map/ppermute | solution.py:27
  139.6 30.9 %collective-permute-start.6 = (bf16[8,48,1536]{2,1,0:T(8,128)(2,1)S(1)}, bf16[8,48,1536]{2,1,0:T(8,128)(2,1)S(1)}, u32[]{:S(2)}, u32[]{:S(2)}) collective-permute-start(bf16[8,48,1536]{2,1,0:T(8,128)(2,1)S(1)} %all-to-all-done.1.refs_15_.refs_5_), channel_id=1, source_target_pairs={{0,96},{32,0},{64,32},{96,64},{1,97},{33,1},{65,33},{97,65},{2,98}... | collective-permute-start | bytes 3538952 | tf_op jit(solution)/shard_map/ppermute | solution.py:27
  142.3 20.7 %collective-permute-start.25 = (bf16[2,192,1024]{2,1,0:T(8,128)(2,1)}, bf16[2,192,1024]{2,1,0:T(8,128)(2,1)S(1)}, u32[]{:S(2)}, u32[]{:S(2)}) collective-permute-start(bf16[2,192,1024]{2,1,0:T(8,128)(2,1)} %collective-permute-done.23.refs_10_), channel_id=1, source_target_pairs={{0,3},{1,0},{2,1},{3,2},{4,7},{5,4},{6,5},{7,6},{8,11},{9,8},{10,9... | collective-permute-start | bytes 2359304 | tf_op jit(solution)/shard_map/ppermute | solution.py:27
  144.7 23.7 %collective-permute-start.1 = (bf16[2,192,1024]{2,1,0:T(8,128)(2,1)}, bf16[2,192,1024]{2,1,0:T(8,128)(2,1)S(1)}, u32[]{:S(2)}, u32[]{:S(2)}) collective-permute-start(bf16[2,192,1024]{2,1,0:T(8,128)(2,1)} %copy-done.5), channel_id=1, source_target_pairs={{0,1},{1,2},{2,3},{3,0},{4,5},{5,6},{6,7},{7,4},{8,9},{9,10},{10,1... | collective-permute-start | bytes 2359304 | tf_op jit(solution)/shard_map/ppermute | solution.py:27
  151.6 28.2 %collective-permute-start.2 = (bf16[2,192,1024]{2,1,0:T(8,128)(2,1)S(1)}, bf16[2,192,1024]{2,1,0:T(8,128)(2,1)S(1)}, u32[]{:S(2)}, u32[]{:S(2)}) collective-permute-start(bf16[2,192,1024]{2,1,0:T(8,128)(2,1)S(1)} %copy-done.6), channel_id=1, source_target_pairs={{0,3},{1,0},{2,1},{3,2},{4,7},{5,4},{6,5},{7,6},{8,11},{9,8},{10,9... | collective-permute-start | bytes 2359304 | tf_op jit(solution)/shard_map/ppermute | solution.py:27
  163.0 7.5 %copy-start.16 = (bf16[2,192,1024]{2,1,0:T(8,128)(2,1)}, bf16[2,192,1024]{2,1,0:T(8,128)(2,1)S(1)}, u32[]{:S(2)}) copy-start(bf16[2,192,1024]{2,1,0:T(8,128)(2,1)S(1)} %collective-permute-done.25.refs_12_) | copy-start | bytes 2359300
  163.0 16.9 %collective-permute-start.21 = (bf16[192,1024]{1,0:T(8,128)(2,1)S(1)}, bf16[192,1024]{1,0:T(8,128)(2,1)S(1)}, u32[]{:S(2)}, u32[]{:S(2)}) collective-permute-start(bf16[192,1024]{1,0:T(8,128)(2,1)S(1)} %slice_bitcast_fusion.3), channel_id=1, source_target_pairs={{0,1},{1,2},{2,3},{3,0},{4,5},{5,6},{6,7},{7,4},{8,9},{9,10},{10,1... | collective-permute-start | bytes 1179656 | tf_op jit(solution)/shard_map/ppermute | solution.py:27
  168.4 2.2 copy-start.3
  168.4 19.9 %collective-permute-start.22 = (bf16[192,1024]{1,0:T(8,128)(2,1)S(1)}, bf16[192,1024]{1,0:T(8,128)(2,1)S(1)}, u32[]{:S(2)}, u32[]{:S(2)}) collective-permute-start(bf16[192,1024]{1,0:T(8,128)(2,1)S(1)} %slice_bitcast_fusion.2), channel_id=1, source_target_pairs={{0,3},{1,0},{2,1},{3,2},{4,7},{5,4},{6,5},{7,6},{8,11},{9,8},{10,9... | collective-permute-start | bytes 1179656 | tf_op jit(solution)/shard_map/ppermute | solution.py:27
  168.4 19.9 %copy-start.1 = (bf16[8,48,1536]{2,1,0:T(8,128)(2,1)}, bf16[8,48,1536]{2,1,0:T(8,128)(2,1)S(1)}, u32[]{:S(2)}) copy-start(bf16[8,48,1536]{2,1,0:T(8,128)(2,1)S(1)} %collective-permute-done.5.refs_16_.refs_6_) | copy-start | bytes 3538948
  168.4 19.9 %collective-permute-start.26 = (bf16[192,1024]{1,0:T(8,128)(2,1)S(1)}, bf16[192,1024]{1,0:T(8,128)(2,1)S(1)}, u32[]{:S(2)}, u32[]{:S(2)}) collective-permute-start(bf16[192,1024]{1,0:T(8,128)(2,1)S(1)} %slice_bitcast_fusion.1), channel_id=1, source_target_pairs={{0,1},{1,2},{2,3},{3,0},{4,5},{5,6},{6,7},{7,4},{8,9},{9,10},{10,1... | collective-permute-start | bytes 1179656 | tf_op jit(solution)/shard_map/ppermute | solution.py:27
  170.5 24.0 %copy-start.2 = (bf16[8,48,1536]{2,1,0:T(8,128)(2,1)}, bf16[8,48,1536]{2,1,0:T(8,128)(2,1)S(1)}, u32[]{:S(2)}) copy-start(bf16[8,48,1536]{2,1,0:T(8,128)(2,1)S(1)} %collective-permute-done.6.refs_17_.refs_7_) | copy-start | bytes 3538948
  170.5 24.0 %collective-permute-start.27 = (bf16[192,1024]{1,0:T(8,128)(2,1)S(1)}, bf16[192,1024]{1,0:T(8,128)(2,1)S(1)}, u32[]{:S(2)}, u32[]{:S(2)}) collective-permute-start(bf16[192,1024]{1,0:T(8,128)(2,1)S(1)} %slice_bitcast_fusion), channel_id=1, source_target_pairs={{0,3},{1,0},{2,1},{3,2},{4,7},{5,4},{6,5},{7,6},{8,11},{9,8},{10,9... | collective-permute-start | bytes 1179656 | tf_op jit(solution)/shard_map/ppermute | solution.py:27
  179.9 14.7 %copy-start.4 = (bf16[2,192,1024]{2,1,0:T(8,128)(2,1)}, bf16[2,192,1024]{2,1,0:T(8,128)(2,1)S(1)}, u32[]{:S(2)}) copy-start(bf16[2,192,1024]{2,1,0:T(8,128)(2,1)S(1)} %collective-permute-done.2.refs_2_) | copy-start | bytes 2359300
  179.9 15.5 %collective-permute-start.7 = (bf16[4,48,1536]{2,1,0:T(8,128)(2,1)}, bf16[4,48,1536]{2,1,0:T(8,128)(2,1)}, u32[]{:S(2)}, u32[]{:S(2)}) collective-permute-start(bf16[4,48,1536]{2,1,0:T(8,128)(2,1)} %slice.42), channel_id=1, source_target_pairs={{0,32},{32,64},{64,96},{96,0},{1,33},{33,65},{65,97},{97,1},{2,34}... | collective-permute-start | bytes 1769480 | tf_op jit(solution)/shard_map/ppermute | solution.py:27
  179.9 14.7 %copy-start.17 = (bf16[192,1024]{1,0:T(8,128)(2,1)}, bf16[192,1024]{1,0:T(8,128)(2,1)S(1)}, u32[]{:S(2)}) copy-start(bf16[192,1024]{1,0:T(8,128)(2,1)S(1)} %collective-permute-done.21.refs_8_) | copy-start | bytes 1179652
  179.9 15.5 %collective-permute-start.8 = (bf16[4,48,1536]{2,1,0:T(8,128)(2,1)}, bf16[4,48,1536]{2,1,0:T(8,128)(2,1)}, u32[]{:S(2)}, u32[]{:S(2)}) collective-permute-start(bf16[4,48,1536]{2,1,0:T(8,128)(2,1)} %slice.43), channel_id=1, source_target_pairs={{0,96},{32,0},{64,32},{96,64},{1,97},{33,1},{65,33},{97,65},{2,98}... | collective-permute-start | bytes 1769480 | tf_op jit(solution)/shard_map/ppermute | solution.py:27
  188.3 6.3 %copy-start.18 = (bf16[192,1024]{1,0:T(8,128)(2,1)}, bf16[192,1024]{1,0:T(8,128)(2,1)S(1)}, u32[]{:S(2)}) copy-start(bf16[192,1024]{1,0:T(8,128)(2,1)S(1)} %collective-permute-done.22.refs_9_) | copy-start | bytes 1179652
  188.3 10.2 %collective-permute-start.9 = (bf16[8,48,1536]{2,1,0:T(8,128)(2,1)S(1)}, bf16[8,48,1536]{2,1,0:T(8,128)(2,1)}, u32[]{:S(2)}, u32[]{:S(2)}) collective-permute-start(bf16[8,48,1536]{2,1,0:T(8,128)(2,1)S(1)} %all-to-all-done.1.refs_15_.refs_5_), channel_id=1, source_target_pairs={{0,16},{16,0},{1,17},{17,1},{2,18},{18,2},{3,19},{19,3},{4,20},{20... | collective-permute-start | bytes 3538952 | tf_op jit(solution)/shard_map/ppermute | solution.py:27
  188.3 6.3 %copy-start.19 = (bf16[192,1024]{1,0:T(8,128)(2,1)}, bf16[192,1024]{1,0:T(8,128)(2,1)S(1)}, u32[]{:S(2)}) copy-start(bf16[192,1024]{1,0:T(8,128)(2,1)S(1)} %collective-permute-done.26.refs_13_) | copy-start | bytes 1179652
  188.3 14.2 %collective-permute-start.10 = (bf16[8,48,1536]{2,1,0:T(8,128)(2,1)S(1)}, bf16[8,48,1536]{2,1,0:T(8,128)(2,1)}, u32[]{:S(2)}, u32[]{:S(2)}) collective-permute-start(bf16[8,48,1536]{2,1,0:T(8,128)(2,1)S(1)} %collective-permute-done.5.refs_16_.refs_6_), channel_id=1, source_target_pairs={{0,16},{16,0},{1,17},{17,1},{2,18},{18,2},{3,19},{19,3},{4,20},{20... | collective-permute-start | bytes 3538952 | tf_op jit(solution)/shard_map/ppermute | solution.py:27
  194.6 0.8 copy-start.20
  194.6 8.0 %collective-permute-start.11 = (bf16[8,48,1536]{2,1,0:T(8,128)(2,1)S(1)}, bf16[8,48,1536]{2,1,0:T(8,128)(2,1)}, u32[]{:S(2)}, u32[]{:S(2)}) collective-permute-start(bf16[8,48,1536]{2,1,0:T(8,128)(2,1)S(1)} %collective-permute-done.6.refs_17_.refs_7_), channel_id=1, source_target_pairs={{0,16},{16,0},{1,17},{17,1},{2,18},{18,2},{3,19},{19,3},{4,20},{20... | collective-permute-start | bytes 3538952 | tf_op jit(solution)/shard_map/ppermute | solution.py:27
  195.3 3.8 %collective-permute-start.12 = (bf16[4,48,1536]{2,1,0:T(8,128)(2,1)}, bf16[4,48,1536]{2,1,0:T(8,128)(2,1)S(1)}, u32[]{:S(2)}, u32[]{:S(2)}) collective-permute-start(bf16[4,48,1536]{2,1,0:T(8,128)(2,1)} %collective-permute-done.7.refs_18_.refs_8_), channel_id=1, source_target_pairs={{0,16},{16,0},{1,17},{17,1},{2,18},{18,2},{3,19},{19,3},{4,20},{20... | collective-permute-start | bytes 1769480 | tf_op jit(solution)/shard_map/ppermute | solution.py:27
  195.4 7.2 %collective-permute-start.13 = (bf16[4,48,1536]{2,1,0:T(8,128)(2,1)}, bf16[4,48,1536]{2,1,0:T(8,128)(2,1)S(1)}, u32[]{:S(2)}, u32[]{:S(2)}) collective-permute-start(bf16[4,48,1536]{2,1,0:T(8,128)(2,1)} %collective-permute-done.8.refs_19_.refs_9_), channel_id=1, source_target_pairs={{0,16},{16,0},{1,17},{17,1},{2,18},{18,2},{3,19},{19,3},{4,20},{20... | collective-permute-start | bytes 1769480 | tf_op jit(solution)/shard_map/ppermute | solution.py:27
  198.5 22.0 %collective-permute-start.3 = (bf16[192,1024]{1,0:T(8,128)(2,1)S(1)}, bf16[192,1024]{1,0:T(8,128)(2,1)S(1)}, u32[]{:S(2)}, u32[]{:S(2)}) collective-permute-start(bf16[192,1024]{1,0:T(8,128)(2,1)S(1)} %slice_bitcast_fusion.7), channel_id=1, source_target_pairs={{0,1},{1,2},{2,3},{3,0},{4,5},{5,6},{6,7},{7,4},{8,9},{9,10},{10,1... | collective-permute-start | bytes 1179656 | tf_op jit(solution)/shard_map/ppermute | solution.py:27
  199.2 3.4 %copy-start.8 = (bf16[4,48,1536]{2,1,0:T(8,128)(2,1)}, bf16[4,48,1536]{2,1,0:T(8,128)(2,1)S(1)}, u32[]{:S(2)}) copy-start(bf16[4,48,1536]{2,1,0:T(8,128)(2,1)S(1)} %collective-permute-done.12.refs_23_.refs_13_) | copy-start | bytes 1769476
  199.2 21.3 %collective-permute-start.4 = (bf16[192,1024]{1,0:T(8,128)(2,1)S(1)}, bf16[192,1024]{1,0:T(8,128)(2,1)S(1)}, u32[]{:S(2)}, u32[]{:S(2)}) collective-permute-start(bf16[192,1024]{1,0:T(8,128)(2,1)S(1)} %slice_bitcast_fusion.6), channel_id=1, source_target_pairs={{0,3},{1,0},{2,1},{3,2},{4,7},{5,4},{6,5},{7,6},{8,11},{9,8},{10,9... | collective-permute-start | bytes 1179656 | tf_op jit(solution)/shard_map/ppermute | solution.py:27
  202.5 0.9 copy-start.9
  (2 other events, 1.5 us)

commit v2 on v1

v2 whole, which is shorter than its diff:
```python
import functools

import jax
import jax.numpy as jnp
from jax import lax
from jax.experimental import pallas as pl
from jax.experimental.pallas import tpu as pltpu
from jax.sharding import Mesh, PartitionSpec as P

AXES = ("zhi", "x", "core", "zlo", "y")
SIZES = {"zhi": 2, "x": 4, "core": 2, "zlo": 4, "y": 4}
GRID = ("zhi", "x", "core")
ORB = ("zlo", "y")

NPTS = 768
SHARE = 48
ORBS = 192
HALF = ORBS // 2
REGION = 6144
ROWS = 1024
KSLOT = 4 * ORBS
CHUNK = 1024
TILE = 512
GROUPS = ((0,), (1, 2, 3))
MIB = 1024 * 1024

PAIRS = [(0, 1), (1, 0), (2, 3), (3, 2)]
MIRROR = [(0, 3), (1, 2), (2, 1), (3, 0)]


def shift(value, axis, step):
    n = SIZES[axis]
    return lax.ppermute(value, axis, [(i, (i + step) % n) for i in range(n)])


def after(value, *others):
    return lax.optimization_barrier((value,) + others)[0]


def gather_kernel(points_ref, psi_ref, phi_ref, out_ref, acc_ref):
    step = pl.program_id(0)
    columns = lax.broadcasted_iota(jnp.int32, (NPTS, CHUNK), 1) + step * CHUNK
    pick = jnp.where(points_ref[...] == columns, 1.0, 0.0).astype(jnp.bfloat16)
    both = jnp.concatenate([psi_ref[...], phi_ref[...]], axis=0)
    part = lax.dot_general(
        pick, both, (((1,), (1,)), ((), ())), preferred_element_type=jnp.float32
    )

    @pl.when(step == 0)
    def _():
        acc_ref[...] = part

    @pl.when(step > 0)
    def _():
        acc_ref[...] += part

    @pl.when(step == pl.num_programs(0) - 1)
    def _():
        out_ref[...] = acc_ref[...].astype(jnp.bfloat16)


def gather_points(points, psi_region, phi_region):
    steps = REGION // CHUNK
    return pl.pallas_call(
        gather_kernel,
        grid=(steps,),
        in_specs=[
            pl.BlockSpec((NPTS, 1), lambda j: (0, 0)),
            pl.BlockSpec((ORBS, CHUNK), lambda j: (0, j)),
            pl.BlockSpec((ORBS, CHUNK), lambda j: (0, j)),
        ],
        out_specs=pl.BlockSpec((NPTS, 2 * ORBS), lambda j: (0, 0)),
        out_shape=jax.ShapeDtypeStruct((NPTS, 2 * ORBS), jnp.bfloat16),
        scratch_shapes=[pltpu.VMEM((NPTS, 2 * ORBS), jnp.float32)],
        compiler_params=pltpu.CompilerParams(vmem_limit_bytes=56 * MIB),
        cost_estimate=pl.CostEstimate(
            flops=2 * NPTS * REGION * 2 * ORBS, bytes_accessed=2 * ORBS * REGION * 2, transcendentals=0
        ),
        name="gather_points",
    )(points, psi_region, phi_region)


def spread_kernel(in_ref, out_ref):
    for y in range(4):
        for m in range(2):
            out_ref[m, :, :, y * ORBS : (y + 1) * ORBS] = in_ref[y, :, :, m * ORBS : (m + 1) * ORBS]


def join_orbitals(by_y):
    return pl.pallas_call(
        spread_kernel,
        in_specs=[pl.BlockSpec(memory_space=pltpu.VMEM)],
        out_specs=pl.BlockSpec(memory_space=pltpu.VMEM),
        out_shape=jax.ShapeDtypeStruct((2, 4, SHARE, KSLOT), jnp.bfloat16),
        compiler_params=pltpu.CompilerParams(vmem_limit_bytes=8 * MIB),
        name="join_orbitals",
    )(by_y)


def gram_kernel(pieces, n_w, pos_ref, *refs):
    w_refs, p_refs = refs[:n_w], refs[n_w : n_w + 10]
    out_ref, w_buf, p_buf, acc, w_sem, p_sem = refs[n_w + 10 :]
    x, core, zlo, y = pos_ref[0], pos_ref[1], pos_ref[2], pos_ref[3]
    pair = zlo + 1 - 2 * (zlo % 2)
    which = [zlo, pair, 3 - zlo, 3 - pair]

    def loads(s):
        mine = []
        for j, (ref, source, m, e, rows) in enumerate(pieces[s]):
            mine.append(
                pltpu.make_async_copy(
                    w_refs[ref].at[source], w_buf.at[s, m, (y + e) % 4, rows], w_sem.at[s, j]
                )
            )
        for swap in range(2):
            who = (core + swap) % 2
            five = p_refs[5 * swap : 5 * swap + 5]
            for j, e in enumerate((0, 3, 1)):
                mine.append(
                    pltpu.make_async_copy(
                        five[j].at[:, which[s]], p_buf.at[s, :, (x + e) % 4, who], p_sem.at[s, swap, j]
                    )
                )
            for m in range(2):
                mine.append(
                    pltpu.make_async_copy(
                        five[3 + m].at[:, which[s]],
                        p_buf.at[s, :, (x + 2) % 4, who, m],
                        p_sem.at[s, swap, 3 + m],
                    )
                )
        return mine

    copies = [loads(s) for s in range(4)]
    for copy in copies[0]:
        copy.start()
    for i, group in enumerate(GROUPS):
        for s in group:
            for copy in copies[s]:
                copy.wait()
            if s == 0:
                for later in copies[1:]:
                    for copy in later:
                        copy.start()
        last = i == len(GROUPS) - 1

        def body(n, _):
            cols = pl.ds(pl.multiple_of(n * TILE, TILE), TILE)
            grams = []
            for m in range(2):
                lhs = jnp.concatenate([p_buf[s, :, :, :, m].reshape(NPTS, KSLOT) for s in group], axis=1)
                rhs = w_buf[group[0] : group[-1] + 1, m, :, :, cols].reshape(len(group) * KSLOT, TILE)
                part = jnp.dot(lhs, rhs, preferred_element_type=jnp.float32)
                grams.append(part if i == 0 else part + acc[m, :, cols])
            if last:
                fitted = grams[0] * grams[1] * (1.0 / (16 * ORBS))
                out_ref[:, cols] = fitted.astype(jnp.bfloat16)
            else:
                for m in range(2):
                    acc[m, :, cols] = grams[m]
            return 0

        lax.fori_loop(0, ROWS // TILE, body, 0)


def gram(pos, parts, p_parts):
    arrays, pieces = [], []
    for slot in parts:
        mine = []
        for array, *place in slot:
            found = [i for i, a in enumerate(arrays) if a is array]
            if not found:
                found = [len(arrays)]
                arrays.append(array)
            mine.append((found[0], *place))
        pieces.append(mine)
    any_spec = pl.BlockSpec(memory_space=pl.ANY)
    p_parts = [p.reshape((2, 4) + p.shape[1:]) for p in p_parts]
    return pl.pallas_call(
        functools.partial(gram_kernel, pieces, len(arrays)),
        in_specs=[pl.BlockSpec(memory_space=pltpu.SMEM)] + [any_spec] * (len(arrays) + 10),
        out_specs=pl.BlockSpec(memory_space=pltpu.VMEM),
        out_shape=jax.ShapeDtypeStruct((NPTS, ROWS), jnp.bfloat16),
        scratch_shapes=[
            pltpu.VMEM((4, 2, 4, ORBS, ROWS), jnp.bfloat16),
            pltpu.VMEM((4, 2, 4, 2, 2, SHARE, KSLOT), jnp.bfloat16),
            pltpu.VMEM((2, NPTS, ROWS), jnp.float32),
            pltpu.SemaphoreType.DMA((4, max(len(slot) for slot in pieces))),
            pltpu.SemaphoreType.DMA((4, 2, 5)),
        ],
        compiler_params=pltpu.CompilerParams(vmem_limit_bytes=48 * MIB),
        cost_estimate=pl.CostEstimate(
            flops=2 * 2 * 4 * NPTS * KSLOT * ROWS, bytes_accessed=24 * MIB, transcendentals=0
        ),
        name="gram",
    )(pos, *arrays, *p_parts)


def per_device(psi_window, phi_window, psi_region, phi_region, points):
    pos = jnp.stack([lax.axis_index(a) for a in ("x", "core", "zlo", "y")]).astype(jnp.int32)
    both, full, one, two = slice(0, 2), slice(0, ORBS), slice(1, 3), slice(0, 2)
    parts = [[] for _ in range(4)]

    own = jnp.stack([psi_window, phi_window])
    below, above = shift(own, "y", 1), shift(own, "y", -1)
    near = lax.ppermute(own, "zlo", PAIRS)
    mirror = lax.ppermute(own, "zlo", MIRROR)
    parts[0] += [(own, both, both, 0, full), (below, both, both, 3, full), (above, both, both, 1, full)]

    def ring(s, slot, below, above):
        up = shift(jnp.concatenate([below[0:1], slot]), "y", 1)
        down = shift(jnp.concatenate([slot, above[1:2]]), "y", -1)
        parts[s - 1] += [(up, 0, 0, 2, full), (down, 2, 1, 2, full)]
        parts[s] += [(slot, both, both, 0, full), (up, one, both, 3, full), (down, two, both, 1, full)]
        return up[1:], down[:2]

    order = points.reshape(4, 4, SHARE).transpose(1, 0, 2).reshape(NPTS, 1)
    picked = gather_points(order, psi_region, phi_region).reshape(4, 4, SHARE, 2 * ORBS)
    cols = join_orbitals(lax.all_to_all(picked, "y", 0, 0, tiled=True))
    cols = after(cols, below, above, near, mirror)

    below, above = ring(1, near, below, above)
    cols = cols.transpose(1, 0, 2, 3)
    mine = lax.all_to_all(jnp.concatenate([cols, cols]), ("zhi", "zlo"), 0, 0, tiled=True)
    mine = after(mine, below, above, mirror)

    below, above = ring(2, mirror, below, above)
    cross = lax.ppermute(mirror, "zlo", PAIRS)
    left, right = shift(mine, "x", 1), shift(mine, "x", -1)
    left = after(left, below, above, cross)
    below, above = ring(3, cross, below, above)
    far_psi, far_phi = shift(left[:, 0], "x", 1), shift(right[:, 1], "x", -1)
    far_psi = after(far_psi, below, above)

    up, down = shift(below[0], "y", 1), shift(above[1], "y", -1)
    parts[3] += [(up, Ellipsis, 0, 2, full), (down, Ellipsis, 1, 2, full)]
    p_parts = [mine, left, right, far_psi, far_phi]
    p_parts += [shift(part, "core", 1) for part in p_parts]

    out = gram(pos, parts, p_parts)
    return out.reshape(16, SHARE, ROWS).transpose(2, 0, 1)


def solution(mesh):
    torus = Mesh(mesh.devices.reshape(tuple(SIZES[a] for a in AXES)), AXES)
    in_specs = (P(ORB, GRID), P(ORB, GRID), P(ORB, GRID), P(ORB, GRID), P(GRID))
    out_specs = P(GRID, None, ORB)
    return jax.shard_map(
        per_device, mesh=torus, in_specs=in_specs, out_specs=out_specs, check_vma=False
    )
```

time: 232 us -> 185 us (0.80)
  the two profiles are of different devices: /device:TPU:96 before, /device:TPU:1 now
where the time goes in v2:
time: 185 us
  waiting for transfers between devices  86.2 us (47%)
  starting transfers between devices  36.7 us (20%)
  Pallas kernels  26.6 us (14%)
  blocking collectives  14.8 us (8%)
  local copies, waits for them, and re-layouts  11.9 us (6%)
  other arithmetic  8.11 us (4%)
    ppermute x19, waiting for transfers between devices, shift(): return lax.ppermute(value, axis, [(i, (i + step) % n) for i in range(n)])  72.2 us
    ppermute x19, starting transfers between devices, shift(): return lax.ppermute(value, axis, [(i, (i + step) % n) for i in range(n)])  24.8 us
    pallas_call x1, Pallas kernels, gram(): pl.pallas_call(functools.partial(gram_kernel, pieces, len(arrays)), in_sp...  17.5 us
    all_to_all x1, blocking collectives, per_device(): cols = join_orbitals(lax.all_to_all(picked, 'y', 0, 0, tiled=True))  14.8 us
    pallas_call x1, Pallas kernels, gather_points(): pl.pallas_call(gather_kernel, grid=(steps,), in_specs=[pl.BlockSpec((NPTS...  8.97 us
    ppermute x1, waiting for transfers between devices, per_device(): near = lax.ppermute(own, 'zlo', PAIRS)  7.29 us
    concatenate x3, other arithmetic, ring(): down = shift(jnp.concatenate([slot, above[1:2]]), 'y', -1)  6.75 us
    all_to_all x1, waiting for transfers between devices, per_device(): lax.all_to_all(jnp.concatenate([cols, cols]), ('zhi', 'zlo'), 0, 0, tiled...  6.73 us
  transfers between devices with their start and end apart: 23, of which 9 were waited for; matrix products, arithmetic and copies ran while one was open for 7% of the time, Pallas kernels for 5%

profile of v2, /device:TPU:1, one launch (start us, length us, event | category | flops | bytes accessed | tf_op | source)
XLA Modules:
  0.0 184.6 jit_solution(18032199150924980453)
XLA Ops:
  0.0 1.2 pad_maximum_fusion.7.refs_0_
  1.2 5.3 %collective-permute-start.5 = (bf16[2,192,1024]{2,1,0:T(8,128)(2,1)S(1)}, bf16[2,192,1024]{2,1,0:T(8,128)(2,1)}, u32[]{:S(2)}, u32[]{:S(2)}) collective-permute-start(bf16[2,192,1024]{2,1,0:T(8,128)(2,1)S(1)} %pad_maximum_fusion.7.refs_0_), channel_id=1, source_target_pairs={{0,12},{4,8},{8,4},{12,0},{1,13},{5,9},{9,5},{13,1},{2,14},{6,10},... | collective-permute-start | bytes 2359304 | tf_op jit(solution)/shard_map/ppermute | solution.py:207
  6.5 2.7 %collective-permute-start.1 = (bf16[2,192,1024]{2,1,0:T(8,128)(2,1)S(1)}, bf16[2,192,1024]{2,1,0:T(8,128)(2,1)S(1)}, u32[]{:S(2)}, u32[]{:S(2)}) collective-permute-start(bf16[2,192,1024]{2,1,0:T(8,128)(2,1)S(1)} %pad_maximum_fusion.7.refs_0_), channel_id=1, source_target_pairs={{0,3},{1,0},{2,1},{3,2},{4,7},{5,4},{6,5},{7,6},{8,11},{9,8},{10,9... | collective-permute-start | bytes 2359304 | tf_op jit(solution)/shard_map/ppermute | solution.py:33
  9.2 0.1 reshape.42
  9.3 0.9 reshape.56.points_ref
  10.2 9.0 %gather_points.1 = bf16[768,384]{1,0:T(8,128)(2,1)} custom-call(s32[768,1]{1,0:T(8,128)} %reshape.56.points_ref, bf16[192,6144]{1,0:T(8,128)(2,1)} %psi_ref.1, bf16[192,6144]{1,0:T(8,128)(2,1)} %phi_ref.1), custom_call_target="tpu_custom_call" | custom-call | flops 3623878656 | bytes 4718592 | tf_op jit(solution)/shard_map/gather_points/pallas_call | solution.py:64
  19.2 14.8 %all_to_all.10.in_ref = bf16[4,4,48,384]{3,2,1,0:T(8,128)(2,1)S(1)} all-to-all(bf16[4,4,48,384]{3,2,1,0:T(8,128)(2,1)} %bitcast.33), channel_id=1, replica_groups=mesh['zhi'=2,'x'=4,'core'=2,'zlo'=4,'y'=4] {'y'}, dimensions={0} | all-to-all | bytes 1179648 | tf_op jit(solution)/shard_map/all_to_all | solution.py:219
  34.0 0.2 join_orbitals.1
  34.1 7.3 %collective-permute-done.2.refs_5_ = bf16[2,192,1024]{2,1,0:T(8,128)(2,1)S(1)} collective-permute-done((bf16[2,192,1024]{2,1,0:T(8,128)(2,1)S(1)}, bf16[2,192,1024]{2,1,0:T(8,128)(2,1)S(1)}, u32[]{:S(2)}, u32[]{:S(2)}) %collective-permute-start.2) | collective-permute-done | bytes 786464 | tf_op jit(solution)/shard_map/ppermute | solution.py:206
  41.5 0.8 copy-done.2
  42.3 2.6 %pad_maximum_fusion.1 = (bf16[3,192,1024]{2,1,0:T(8,128)(2,1)}, bf16[3,192,1024]{2,1,0:T(8,128)(2,1)S(1)}) fusion(bf16[1,192,1024]{2,1,0:T(8,128)(2,1)S(1)} %slice.53, bf16[2,192,1024]{2,1,0:T(8,128)(2,1)} %copy-done.2, bf16[1,192,1024]{2,1,0:T(8,128)(2,1)S(1)} %slice.52), kind=kLoop, calls=%fused_computation.1 | loop fusion | flops 1179648 | bytes 3932160 | tf_op jit(solution)/shard_map/concatenate | solution.py:212
  44.9 2.7 %collective-permute-start.4 = (bf16[3,192,1024]{2,1,0:T(8,128)(2,1)}, bf16[3,192,1024]{2,1,0:T(8,128)(2,1)}, u32[]{:S(2)}, u32[]{:S(2)}) collective-permute-start(bf16[3,192,1024]{2,1,0:T(8,128)(2,1)} %get-tuple-element.15), channel_id=1, source_target_pairs={{0,3},{1,0},{2,1},{3,2},{4,7},{5,4},{6,5},{7,6},{8,11},{9,8},{10,9... | collective-permute-start | bytes 3538952 | tf_op jit(solution)/shard_map/ppermute | solution.py:33
  47.7 0.1 pad_maximum_fusion.6
  47.8 1.1 copy.22
  48.9 6.6 %all-to-all-start.1 = ((bf16[8,2,48,768]{3,2,1,0:T(8,128)(2,1)}), bf16[8,2,48,768]{3,2,1,0:T(8,128)(2,1)}, u32[]{:S(2)}, u32[]{:S(2)}) async-start(bf16[8,2,48,768]{3,2,1,0:T(8,128)(2,1)} %copy.22), calls=%async_computation.1 | async-start | bytes 2359296 | tf_op jit(solution)/shard_map/all_to_all | solution.py:224
  55.5 17.3 %collective-permute-done.4.refs_4_ = bf16[3,192,1024]{2,1,0:T(8,128)(2,1)} collective-permute-done((bf16[3,192,1024]{2,1,0:T(8,128)(2,1)}, bf16[3,192,1024]{2,1,0:T(8,128)(2,1)}, u32[]{:S(2)}, u32[]{:S(2)}) %collective-permute-start.4) | collective-permute-done | bytes 1179680 | tf_op jit(solution)/shard_map/ppermute | solution.py:33
  72.8 1.0 slice.55
  73.9 1.9 %collective-permute-done.3.refs_3_ = bf16[3,192,1024]{2,1,0:T(8,128)(2,1)} collective-permute-done((bf16[3,192,1024]{2,1,0:T(8,128)(2,1)S(1)}, bf16[3,192,1024]{2,1,0:T(8,128)(2,1)}, u32[]{:S(2)}, u32[]{:S(2)}) %collective-permute-start.3) | collective-permute-done | bytes 1179680 | tf_op jit(solution)/shard_map/ppermute | solution.py:33
  75.7 1.0 slice.54
  76.7 2.6 %pad_maximum_fusion.3 = (bf16[3,192,1024]{2,1,0:T(8,128)(2,1)}, bf16[3,192,1024]{2,1,0:T(8,128)(2,1)S(1)}) fusion(bf16[1,192,1024]{2,1,0:T(8,128)(2,1)S(1)} %slice.55, bf16[2,192,1024]{2,1,0:T(8,128)(2,1)} %collective-permute-done.5.refs_8_, bf16[1,192,1024]{2,1,0:T(8,128)(2,1)S(1)} %slice.54), kind=kLoop, calls=%fused_computation.3 | loop fusion | flops 1179648 | bytes 3932160 | tf_op jit(solution)/shard_map/concatenate | solution.py:212
  79.3 1.6 collective-permute-start.7
  80.9 6.7 %all-to-all-done.1 = bf16[8,2,48,768]{3,2,1,0:T(8,128)(2,1)} async-done(((bf16[8,2,48,768]{3,2,1,0:T(8,128)(2,1)}), bf16[8,2,48,768]{3,2,1,0:T(8,128)(2,1)}, u32[]{:S(2)}, u32[]{:S(2)}) %all-to-all-start.1) | async-done | bytes 1179680 | tf_op jit(solution)/shard_map/all_to_all | solution.py:224
  87.6 1.2 collective-permute-start.13
  88.8 1.5 collective-permute-start.14
  90.3 15.1 %collective-permute-done.7.refs_7_ = bf16[3,192,1024]{2,1,0:T(8,128)(2,1)} collective-permute-done((bf16[3,192,1024]{2,1,0:T(8,128)(2,1)}, bf16[3,192,1024]{2,1,0:T(8,128)(2,1)}, u32[]{:S(2)}, u32[]{:S(2)}) %collective-permute-start.7) | collective-permute-done | bytes 1179680 | tf_op jit(solution)/shard_map/ppermute | solution.py:33
  105.4 2.6 %collective-permute-start.17 = (bf16[8,2,48,768]{3,2,1,0:T(8,128)(2,1)}, bf16[8,2,48,768]{3,2,1,0:T(8,128)(2,1)S(1)}, u32[]{:S(2)}, u32[]{:S(2)}) collective-permute-start(bf16[8,2,48,768]{3,2,1,0:T(8,128)(2,1)} %all-to-all-done.1), channel_id=1, source_target_pairs={{0,16},{16,0},{1,17},{17,1},{2,18},{18,2},{3,19},{19,3},{4,20},{20... | collective-permute-start | bytes 3538952 | tf_op jit(solution)/shard_map/ppermute | solution.py:33
  108.0 1.0 slice.57
  109.1 1.0 slice.56
  110.1 1.6 pad_maximum_fusion.5
  111.7 2.9 %collective-permute-start.10 = (bf16[3,192,1024]{2,1,0:T(8,128)(2,1)S(1)}, bf16[3,192,1024]{2,1,0:T(8,128)(2,1)S(1)}, u32[]{:S(2)}, u32[]{:S(2)}) collective-permute-start(bf16[3,192,1024]{2,1,0:T(8,128)(2,1)S(1)} %get-tuple-element.11), channel_id=1, source_target_pairs={{0,3},{1,0},{2,1},{3,2},{4,7},{5,4},{6,5},{7,6},{8,11},{9,8},{10,9... | collective-permute-start | bytes 3538952 | tf_op jit(solution)/shard_map/ppermute | solution.py:33
  114.5 1.5 collective-permute-done.13
  116.1 1.1 slice_bitcast_fusion.1
  117.2 0.1 collective-permute-start.15
  117.3 1.1 slice_bitcast_fusion
  118.4 2.7 %collective-permute-start.16 = (bf16[8,48,768]{2,1,0:T(8,128)(2,1)S(1)}, bf16[8,48,768]{2,1,0:T(8,128)(2,1)S(1)}, u32[]{:S(2)}, u32[]{:S(2)}) collective-permute-start(bf16[8,48,768]{2,1,0:T(8,128)(2,1)S(1)} %slice_bitcast_fusion), channel_id=1, source_target_pairs={{0,96},{32,0},{64,32},{96,64},{1,97},{33,1},{65,33},{97,65},{2,98}... | collective-permute-start | bytes 1769480 | tf_op jit(solution)/shard_map/ppermute | solution.py:33
  121.1 2.0 %collective-permute-start.19 = (bf16[8,2,48,768]{3,2,1,0:T(8,128)(2,1)}, bf16[8,2,48,768]{3,2,1,0:T(8,128)(2,1)}, u32[]{:S(2)}, u32[]{:S(2)}) collective-permute-start(bf16[8,2,48,768]{3,2,1,0:T(8,128)(2,1)} %collective-permute-done.14), channel_id=1, source_target_pairs={{0,16},{16,0},{1,17},{17,1},{2,18},{18,2},{3,19},{19,3},{4,20},{20... | collective-permute-start | bytes 3538952 | tf_op jit(solution)/shard_map/ppermute | solution.py:33
  123.2 16.8 %collective-permute-done.10.refs_10_ = bf16[3,192,1024]{2,1,0:T(8,128)(2,1)S(1)} collective-permute-done((bf16[3,192,1024]{2,1,0:T(8,128)(2,1)S(1)}, bf16[3,192,1024]{2,1,0:T(8,128)(2,1)S(1)}, u32[]{:S(2)}, u32[]{:S(2)}) %collective-permute-start.10) | collective-permute-done | bytes 1179680 | tf_op jit(solution)/shard_map/ppermute | solution.py:33
  139.9 0.8 collective-permute-start.18
  140.8 3.5 %collective-permute-start.12 = (bf16[192,1024]{1,0:T(8,128)(2,1)S(1)}, bf16[192,1024]{1,0:T(8,128)(2,1)S(1)}, u32[]{:S(2)}, u32[]{:S(2)}) collective-permute-start(bf16[192,1024]{1,0:T(8,128)(2,1)S(1)} %slice_bitcast_fusion.2), channel_id=1, source_target_pairs={{0,3},{1,0},{2,1},{3,2},{4,7},{5,4},{6,5},{7,6},{8,11},{9,8},{10,9... | collective-permute-start | bytes 1179656 | tf_op jit(solution)/shard_map/ppermute | solution.py:33
  144.2 0.3 collective-permute-start.20
  144.5 0.2 collective-permute-start.21
  144.8 0.8 slice_bitcast_fusion.3
  145.5 7.3 %collective-permute-done.12.refs_13_ = bf16[192,1024]{1,0:T(8,128)(2,1)S(1)} collective-permute-done((bf16[192,1024]{1,0:T(8,128)(2,1)S(1)}, bf16[192,1024]{1,0:T(8,128)(2,1)S(1)}, u32[]{:S(2)}, u32[]{:S(2)}) %collective-permute-start.12) | collective-permute-done | bytes 393248 | tf_op jit(solution)/shard_map/ppermute | solution.py:33
  152.8 0.7 copy-done
  153.5 0.1 pad_add_fusion.pos_ref
  153.6 12.3 %collective-permute-done.11.refs_12_ = bf16[192,1024]{1,0:T(8,128)(2,1)} collective-permute-done((bf16[192,1024]{1,0:T(8,128)(2,1)}, bf16[192,1024]{1,0:T(8,128)(2,1)}, u32[]{:S(2)}, u32[]{:S(2)}) %collective-permute-start.11) | collective-permute-done | bytes 393248 | tf_op jit(solution)/shard_map/ppermute | solution.py:33
  166.0 1.0 copy-done.1
  167.0 17.5 %gram.1 = bf16[768,1024]{1,0:T(8,128)(2,1)} custom-call(s32[4]{0:T(128)S(1)} %pad_add_fusion.pos_ref, bf16[2,192,1024]{2,1,0:T(8,128)(2,1)S(1)} %pad_maximum_fusion.7.refs_0_, bf16[2,192,1024]{2,1,0:T(8,128)(2,1)S(1)} %collective-permute-done.refs_1_, bf16[2,192,1024]{2,1,0:T(8,128)(2,1)S(1)} %collective-permute-done.1.refs_2_, ...), custom_call_target="tpu_custom_call" | custom-call | flops 9663676416 | bytes 25165824 | tf_op jit(solution)/shard_map/gram/pallas_call | solution.py:179
  (36 shorter events, 0.2 us)
Async XLA Ops:
  0.0 9.2 %copy-start.5 = (s32[768]{0:T(1024)S(1)}, s32[768]{0:T(1024)}, u32[]{:S(2)}) copy-start(s32[768]{0:T(1024)} %param.9) | copy-start | bytes 9220
  1.2 32.9 %collective-permute-start.5 = (bf16[2,192,1024]{2,1,0:T(8,128)(2,1)S(1)}, bf16[2,192,1024]{2,1,0:T(8,128)(2,1)}, u32[]{:S(2)}, u32[]{:S(2)}) collective-permute-start(bf16[2,192,1024]{2,1,0:T(8,128)(2,1)S(1)} %pad_maximum_fusion.7.refs_0_), channel_id=1, source_target_pairs={{0,12},{4,8},{8,4},{12,0},{1,13},{5,9},{9,5},{13,1},{2,14},{6,10},... | collective-permute-start | bytes 2359304 | tf_op jit(solution)/shard_map/ppermute | solution.py:207
  6.5 35.0 %collective-permute-start.2 = (bf16[2,192,1024]{2,1,0:T(8,128)(2,1)S(1)}, bf16[2,192,1024]{2,1,0:T(8,128)(2,1)S(1)}, u32[]{:S(2)}, u32[]{:S(2)}) collective-permute-start(bf16[2,192,1024]{2,1,0:T(8,128)(2,1)S(1)} %pad_maximum_fusion.7.refs_0_), channel_id=1, source_target_pairs={{0,4},{4,0},{8,12},{12,8},{1,5},{5,1},{9,13},{13,9},{2,6},{6,2},{1... | collective-permute-start | bytes 2359304 | tf_op jit(solution)/shard_map/ppermute | solution.py:206
  6.5 35.0 %collective-permute-start.1 = (bf16[2,192,1024]{2,1,0:T(8,128)(2,1)S(1)}, bf16[2,192,1024]{2,1,0:T(8,128)(2,1)S(1)}, u32[]{:S(2)}, u32[]{:S(2)}) collective-permute-start(bf16[2,192,1024]{2,1,0:T(8,128)(2,1)S(1)} %pad_maximum_fusion.7.refs_0_), channel_id=1, source_target_pairs={{0,3},{1,0},{2,1},{3,2},{4,7},{5,4},{6,5},{7,6},{8,11},{9,8},{10,9... | collective-permute-start | bytes 2359304 | tf_op jit(solution)/shard_map/ppermute | solution.py:33
  9.2 32.2 %collective-permute-start = (bf16[2,192,1024]{2,1,0:T(8,128)(2,1)S(1)}, bf16[2,192,1024]{2,1,0:T(8,128)(2,1)S(1)}, u32[]{:S(2)}, u32[]{:S(2)}) collective-permute-start(bf16[2,192,1024]{2,1,0:T(8,128)(2,1)S(1)} %pad_maximum_fusion.7.refs_0_), channel_id=1, source_target_pairs={{0,1},{1,2},{2,3},{3,0},{4,5},{5,6},{6,7},{7,4},{8,9},{9,10},{10,1... | collective-permute-start | bytes 2359304 | tf_op jit(solution)/shard_map/ppermute | solution.py:33
  41.4 0.9 copy-start.2
  44.9 27.9 %collective-permute-start.4 = (bf16[3,192,1024]{2,1,0:T(8,128)(2,1)}, bf16[3,192,1024]{2,1,0:T(8,128)(2,1)}, u32[]{:S(2)}, u32[]{:S(2)}) collective-permute-start(bf16[3,192,1024]{2,1,0:T(8,128)(2,1)} %get-tuple-element.15), channel_id=1, source_target_pairs={{0,3},{1,0},{2,1},{3,2},{4,7},{5,4},{6,5},{7,6},{8,11},{9,8},{10,9... | collective-permute-start | bytes 3538952 | tf_op jit(solution)/shard_map/ppermute | solution.py:33
  47.7 28.0 %collective-permute-start.3 = (bf16[3,192,1024]{2,1,0:T(8,128)(2,1)S(1)}, bf16[3,192,1024]{2,1,0:T(8,128)(2,1)}, u32[]{:S(2)}, u32[]{:S(2)}) collective-permute-start(bf16[3,192,1024]{2,1,0:T(8,128)(2,1)S(1)} %get-tuple-element.16), channel_id=1, source_target_pairs={{0,1},{1,2},{2,3},{3,0},{4,5},{5,6},{6,7},{7,4},{8,9},{9,10},{10,1... | collective-permute-start | bytes 3538952 | tf_op jit(solution)/shard_map/ppermute | solution.py:33
  48.9 38.8 %all-to-all-start.1 = ((bf16[8,2,48,768]{3,2,1,0:T(8,128)(2,1)}), bf16[8,2,48,768]{3,2,1,0:T(8,128)(2,1)}, u32[]{:S(2)}, u32[]{:S(2)}) async-start(bf16[8,2,48,768]{3,2,1,0:T(8,128)(2,1)} %copy.22), calls=%async_computation.1 | async-start | bytes 2359296 | tf_op jit(solution)/shard_map/all_to_all | solution.py:224
  79.3 26.1 %collective-permute-start.7 = (bf16[3,192,1024]{2,1,0:T(8,128)(2,1)}, bf16[3,192,1024]{2,1,0:T(8,128)(2,1)}, u32[]{:S(2)}, u32[]{:S(2)}) collective-permute-start(bf16[3,192,1024]{2,1,0:T(8,128)(2,1)} %get-tuple-element.13), channel_id=1, source_target_pairs={{0,3},{1,0},{2,1},{3,2},{4,7},{5,4},{6,5},{7,6},{8,11},{9,8},{10,9... | collective-permute-start | bytes 3538952 | tf_op jit(solution)/shard_map/ppermute | solution.py:33
  80.9 28.2 %collective-permute-start.6 = (bf16[3,192,1024]{2,1,0:T(8,128)(2,1)S(1)}, bf16[3,192,1024]{2,1,0:T(8,128)(2,1)}, u32[]{:S(2)}, u32[]{:S(2)}) collective-permute-start(bf16[3,192,1024]{2,1,0:T(8,128)(2,1)S(1)} %get-tuple-element.14), channel_id=1, source_target_pairs={{0,1},{1,2},{2,3},{3,0},{4,5},{5,6},{6,7},{7,4},{8,9},{9,10},{10,1... | collective-permute-start | bytes 3538952 | tf_op jit(solution)/shard_map/ppermute | solution.py:33
  80.9 29.2 %collective-permute-start.8 = (bf16[2,192,1024]{2,1,0:T(8,128)(2,1)}, bf16[2,192,1024]{2,1,0:T(8,128)(2,1)}, u32[]{:S(2)}, u32[]{:S(2)}) collective-permute-start(bf16[2,192,1024]{2,1,0:T(8,128)(2,1)} %collective-permute-done.5.refs_8_), channel_id=1, source_target_pairs={{0,4},{4,0},{8,12},{12,8},{1,5},{5,1},{9,13},{13,9},{2,6},{6,2},{1... | collective-permute-start | bytes 2359304 | tf_op jit(solution)/shard_map/ppermute | solution.py:228
  87.6 28.4 %collective-permute-start.13 = (bf16[8,2,48,768]{3,2,1,0:T(8,128)(2,1)}, bf16[8,2,48,768]{3,2,1,0:T(8,128)(2,1)}, u32[]{:S(2)}, u32[]{:S(2)}) collective-permute-start(bf16[8,2,48,768]{3,2,1,0:T(8,128)(2,1)} %all-to-all-done.1), channel_id=1, source_target_pairs={{0,32},{32,64},{64,96},{96,0},{1,33},{33,65},{65,97},{97,1},{2,34}... | collective-permute-start | bytes 3538952 | tf_op jit(solution)/shard_map/ppermute | solution.py:33
  88.8 28.4 %collective-permute-start.14 = (bf16[8,2,48,768]{3,2,1,0:T(8,128)(2,1)}, bf16[8,2,48,768]{3,2,1,0:T(8,128)(2,1)}, u32[]{:S(2)}, u32[]{:S(2)}) collective-permute-start(bf16[8,2,48,768]{3,2,1,0:T(8,128)(2,1)} %all-to-all-done.1), channel_id=1, source_target_pairs={{0,96},{32,0},{64,32},{96,64},{1,97},{33,1},{65,33},{97,65},{2,98}... | collective-permute-start | bytes 3538952 | tf_op jit(solution)/shard_map/ppermute | solution.py:33
  105.4 15.7 %collective-permute-start.17 = (bf16[8,2,48,768]{3,2,1,0:T(8,128)(2,1)}, bf16[8,2,48,768]{3,2,1,0:T(8,128)(2,1)S(1)}, u32[]{:S(2)}, u32[]{:S(2)}) collective-permute-start(bf16[8,2,48,768]{3,2,1,0:T(8,128)(2,1)} %all-to-all-done.1), channel_id=1, source_target_pairs={{0,16},{16,0},{1,17},{17,1},{2,18},{18,2},{3,19},{19,3},{4,20},{20... | collective-permute-start | bytes 3538952 | tf_op jit(solution)/shard_map/ppermute | solution.py:33
  111.7 28.3 %collective-permute-start.10 = (bf16[3,192,1024]{2,1,0:T(8,128)(2,1)S(1)}, bf16[3,192,1024]{2,1,0:T(8,128)(2,1)S(1)}, u32[]{:S(2)}, u32[]{:S(2)}) collective-permute-start(bf16[3,192,1024]{2,1,0:T(8,128)(2,1)S(1)} %get-tuple-element.11), channel_id=1, source_target_pairs={{0,3},{1,0},{2,1},{3,2},{4,7},{5,4},{6,5},{7,6},{8,11},{9,8},{10,9... | collective-permute-start | bytes 3538952 | tf_op jit(solution)/shard_map/ppermute | solution.py:33
  114.5 29.7 %collective-permute-start.9 = (bf16[3,192,1024]{2,1,0:T(8,128)(2,1)S(1)}, bf16[3,192,1024]{2,1,0:T(8,128)(2,1)S(1)}, u32[]{:S(2)}, u32[]{:S(2)}) collective-permute-start(bf16[3,192,1024]{2,1,0:T(8,128)(2,1)S(1)} %get-tuple-element.12), channel_id=1, source_target_pairs={{0,1},{1,2},{2,3},{3,0},{4,5},{5,6},{6,7},{7,4},{8,9},{9,10},{10,1... | collective-permute-start | bytes 3538952 | tf_op jit(solution)/shard_map/ppermute | solution.py:33
  117.2 23.6 %collective-permute-start.15 = (bf16[8,48,768]{2,1,0:T(8,128)(2,1)S(1)}, bf16[8,48,768]{2,1,0:T(8,128)(2,1)S(1)}, u32[]{:S(2)}, u32[]{:S(2)}) collective-permute-start(bf16[8,48,768]{2,1,0:T(8,128)(2,1)S(1)} %slice_bitcast_fusion.1), channel_id=1, source_target_pairs={{0,32},{32,64},{64,96},{96,0},{1,33},{33,65},{65,97},{97,1},{2,34}... | collective-permute-start | bytes 1769480 | tf_op jit(solution)/shard_map/ppermute | solution.py:33
  118.4 26.1 %collective-permute-start.16 = (bf16[8,48,768]{2,1,0:T(8,128)(2,1)S(1)}, bf16[8,48,768]{2,1,0:T(8,128)(2,1)S(1)}, u32[]{:S(2)}, u32[]{:S(2)}) collective-permute-start(bf16[8,48,768]{2,1,0:T(8,128)(2,1)S(1)} %slice_bitcast_fusion), channel_id=1, source_target_pairs={{0,96},{32,0},{64,32},{96,64},{1,97},{33,1},{65,33},{97,65},{2,98}... | collective-permute-start | bytes 1769480 | tf_op jit(solution)/shard_map/ppermute | solution.py:33
  121.1 32.4 %copy-start.6 = (bf16[8,2,48,768]{3,2,1,0:T(8,128)(2,1)}, bf16[8,2,48,768]{3,2,1,0:T(8,128)(2,1)S(1)}, u32[]{:S(2)}) copy-start(bf16[8,2,48,768]{3,2,1,0:T(8,128)(2,1)S(1)} %collective-permute-done.17) | copy-start | bytes 3538948
  121.1 44.9 %collective-permute-start.19 = (bf16[8,2,48,768]{3,2,1,0:T(8,128)(2,1)}, bf16[8,2,48,768]{3,2,1,0:T(8,128)(2,1)}, u32[]{:S(2)}, u32[]{:S(2)}) collective-permute-start(bf16[8,2,48,768]{3,2,1,0:T(8,128)(2,1)} %collective-permute-done.14), channel_id=1, source_target_pairs={{0,16},{16,0},{1,17},{17,1},{2,18},{18,2},{3,19},{19,3},{4,20},{20... | collective-permute-start | bytes 3538952 | tf_op jit(solution)/shard_map/ppermute | solution.py:33
  139.9 12.9 %copy-start.3 = (bf16[3,192,1024]{2,1,0:T(8,128)(2,1)}, bf16[3,192,1024]{2,1,0:T(8,128)(2,1)S(1)}, u32[]{:S(2)}) copy-start(bf16[3,192,1024]{2,1,0:T(8,128)(2,1)S(1)} %collective-permute-done.10.refs_10_) | copy-start | bytes 3538948
  139.9 26.1 %collective-permute-start.18 = (bf16[8,2,48,768]{3,2,1,0:T(8,128)(2,1)}, bf16[8,2,48,768]{3,2,1,0:T(8,128)(2,1)}, u32[]{:S(2)}, u32[]{:S(2)}) collective-permute-start(bf16[8,2,48,768]{3,2,1,0:T(8,128)(2,1)} %collective-permute-done.13), channel_id=1, source_target_pairs={{0,16},{16,0},{1,17},{17,1},{2,18},{18,2},{3,19},{19,3},{4,20},{20... | collective-permute-start | bytes 3538952 | tf_op jit(solution)/shard_map/ppermute | solution.py:33
  140.8 12.0 %collective-permute-start.12 = (bf16[192,1024]{1,0:T(8,128)(2,1)S(1)}, bf16[192,1024]{1,0:T(8,128)(2,1)S(1)}, u32[]{:S(2)}, u32[]{:S(2)}) collective-permute-start(bf16[192,1024]{1,0:T(8,128)(2,1)S(1)} %slice_bitcast_fusion.2), channel_id=1, source_target_pairs={{0,3},{1,0},{2,1},{3,2},{4,7},{5,4},{6,5},{7,6},{8,11},{9,8},{10,9... | collective-permute-start | bytes 1179656 | tf_op jit(solution)/shard_map/ppermute | solution.py:33
  144.2 9.3 %copy-start.4 = (bf16[3,192,1024]{2,1,0:T(8,128)(2,1)}, bf16[3,192,1024]{2,1,0:T(8,128)(2,1)S(1)}, u32[]{:S(2)}) copy-start(bf16[3,192,1024]{2,1,0:T(8,128)(2,1)S(1)} %collective-permute-done.9.refs_9_) | copy-start | bytes 3538948
  144.2 21.7 %collective-permute-start.20 = (bf16[8,48,768]{2,1,0:T(8,128)(2,1)S(1)}, bf16[8,48,768]{2,1,0:T(8,128)(2,1)}, u32[]{:S(2)}, u32[]{:S(2)}) collective-permute-start(bf16[8,48,768]{2,1,0:T(8,128)(2,1)S(1)} %collective-permute-done.15), channel_id=1, source_target_pairs={{0,16},{16,0},{1,17},{17,1},{2,18},{18,2},{3,19},{19,3},{4,20},{20... | collective-permute-start | bytes 1769480 | tf_op jit(solution)/shard_map/ppermute | solution.py:33
  144.5 21.4 %collective-permute-start.21 = (bf16[8,48,768]{2,1,0:T(8,128)(2,1)S(1)}, bf16[8,48,768]{2,1,0:T(8,128)(2,1)}, u32[]{:S(2)}, u32[]{:S(2)}) collective-permute-start(bf16[8,48,768]{2,1,0:T(8,128)(2,1)S(1)} %collective-permute-done.16), channel_id=1, source_target_pairs={{0,16},{16,0},{1,17},{17,1},{2,18},{18,2},{3,19},{19,3},{4,20},{20... | collective-permute-start | bytes 1769480 | tf_op jit(solution)/shard_map/ppermute | solution.py:33
  152.8 0.7 copy-start
  153.5 12.4 %collective-permute-start.11 = (bf16[192,1024]{1,0:T(8,128)(2,1)}, bf16[192,1024]{1,0:T(8,128)(2,1)}, u32[]{:S(2)}, u32[]{:S(2)}) collective-permute-start(bf16[192,1024]{1,0:T(8,128)(2,1)} %slice_bitcast_fusion.3), channel_id=1, source_target_pairs={{0,1},{1,2},{2,3},{3,0},{4,5},{5,6},{6,7},{7,4},{8,9},{9,10},{10,1... | collective-permute-start | bytes 1179656 | tf_op jit(solution)/shard_map/ppermute | solution.py:33
  166.0 1.0 copy-start.1

commit v3 on v2

v3 whole, which is shorter than its diff:
```python
import functools

import jax
import jax.numpy as jnp
from jax import lax
from jax.experimental import pallas as pl
from jax.experimental.pallas import tpu as pltpu
from jax.sharding import Mesh, PartitionSpec as P

AXES = ("zhi", "x", "core", "zlo", "y")
SIZES = {"zhi": 2, "x": 4, "core": 2, "zlo": 4, "y": 4}
GRID = ("zhi", "x", "core")
ORB = ("zlo", "y")

NPTS = 768
SHARE = 48
ORBS = 192
HALF = ORBS // 2
REGION = 6144
ROWS = 1024
KSLOT = 4 * ORBS
CHUNK = 1024
TILE = 256
GRAM_VMEM = 24
MIB = 1024 * 1024

PAIRS = [(0, 1), (1, 0), (2, 3), (3, 2)]
MIDDLE = [(1, 2), (2, 1)]
OUTWARD = [(1, 0), (2, 3)]


def shift(value, axis, step):
    n = SIZES[axis]
    return lax.ppermute(value, axis, [(i, (i + step) % n) for i in range(n)])


def after(value, *others):
    return lax.optimization_barrier((value,) + others)[0]


def together(*values):
    return lax.optimization_barrier(values)


def gather_kernel(points_ref, psi_ref, phi_ref, out_ref, acc_ref):
    step = pl.program_id(0)
    columns = lax.broadcasted_iota(jnp.int32, (NPTS, CHUNK), 1) + step * CHUNK
    pick = jnp.where(points_ref[...] == columns, 1.0, 0.0).astype(jnp.bfloat16)
    both = jnp.concatenate([psi_ref[...], phi_ref[...]], axis=0)
    part = lax.dot_general(
        pick, both, (((1,), (1,)), ((), ())), preferred_element_type=jnp.float32
    )

    @pl.when(step == 0)
    def _():
        acc_ref[...] = part

    @pl.when(step > 0)
    def _():
        acc_ref[...] += part

    @pl.when(step == pl.num_programs(0) - 1)
    def _():
        out_ref[...] = acc_ref[...].astype(jnp.bfloat16)


def gather_points(points, psi_region, phi_region):
    steps = REGION // CHUNK
    return pl.pallas_call(
        gather_kernel,
        grid=(steps,),
        in_specs=[
            pl.BlockSpec((NPTS, 1), lambda j: (0, 0)),
            pl.BlockSpec((ORBS, CHUNK), lambda j: (0, j)),
            pl.BlockSpec((ORBS, CHUNK), lambda j: (0, j)),
        ],
        out_specs=pl.BlockSpec((NPTS, 2 * ORBS), lambda j: (0, 0)),
        out_shape=jax.ShapeDtypeStruct((NPTS, 2 * ORBS), jnp.bfloat16),
        scratch_shapes=[pltpu.VMEM((NPTS, 2 * ORBS), jnp.float32)],
        compiler_params=pltpu.CompilerParams(vmem_limit_bytes=56 * MIB),
        cost_estimate=pl.CostEstimate(
            flops=2 * NPTS * REGION * 2 * ORBS, bytes_accessed=2 * ORBS * REGION * 2, transcendentals=0
        ),
        name="gather_points",
    )(points, psi_region, phi_region)


def join_kernel(pos_ref, in_ref, out_ref):
    y = pos_ref[3]
    for e in range(4):
        for m in range(2):
            out_ref[:, m, :, e * ORBS : (e + 1) * ORBS] = in_ref[(y + e) % 4, :, :, m * ORBS : (m + 1) * ORBS]


def join_orbitals(pos, by_y):
    vmem = pl.BlockSpec(memory_space=pltpu.VMEM)
    return pl.pallas_call(
        join_kernel,
        in_specs=[pl.BlockSpec(memory_space=pltpu.SMEM), vmem],
        out_specs=vmem,
        out_shape=jax.ShapeDtypeStruct((4, 2, SHARE, KSLOT), jnp.bfloat16),
        compiler_params=pltpu.CompilerParams(vmem_limit_bytes=8 * MIB),
        name="join_orbitals",
    )(pos, by_y)


def gram_kernel(slots, rows, pieces, n_w, n_p, n_acc, pos_ref, *refs):
    w_refs, p_refs, acc_refs = refs[:n_w], refs[n_w : n_w + n_p], refs[n_w + n_p : n_w + n_p + n_acc]
    out_ref, *scratch = refs[n_w + n_p + n_acc :]
    acc = scratch[0] if scratch else out_ref
    x, core, zlo = pos_ref[0], pos_ref[1], pos_ref[2]
    pair = zlo + 1 - 2 * (zlo % 2)
    which = [zlo, pair, 2 - zlo // 2, 3 - 3 * (zlo // 2)]

    for i, s in enumerate(slots):

        def body(n, _):
            cols = pl.ds(pl.multiple_of(n * TILE, TILE), TILE)
            grams = []
            for m in range(2):
                lhs = []
                for zhi, e, swap in rows:
                    z = zhi * 4 + which[s]
                    if e == 2:
                        lhs.append(p_refs[2 * swap + m][z] if n_p == 4 else p_refs[6 + 2 * swap + m][z])
                    else:
                        lhs.append(p_refs[3 * swap + (0, 2, None, 1)[e]][z, m])
                lhs = jnp.concatenate(lhs, axis=0)
                rhs = jnp.concatenate([w_refs[ref][*index, :, cols] for ref, index in pieces[i][m]], axis=0)
                part = jnp.dot(lhs, rhs, preferred_element_type=jnp.float32)
                if n_acc:
                    part = part + jnp.concatenate([ref[m, :, cols] for ref in acc_refs], axis=0)
                elif i > 0:
                    part = part + acc[m, :, cols]
                grams.append(part)
            if n_acc:
                fitted = (grams[0] * grams[1] * (1.0 / (16 * ORBS))).astype(jnp.bfloat16)
                for j, (zhi, e, swap) in enumerate(rows):
                    out_ref[zhi, (x + e) % 4, (core + swap) % 2, :, cols] = fitted[j * SHARE : (j + 1) * SHARE]
            else:
                for m in range(2):
                    acc[m, :, cols] = grams[m]
            return 0

        lax.fori_loop(0, ROWS // TILE, body, 0)


NEAR_ROWS = [(zhi, e, swap) for zhi in range(2) for e in (0, 1, 3) for swap in range(2)]
FAR_ROWS = [(zhi, 2, swap) for zhi in range(2) for swap in range(2)]


def gram(name, pos, rows, slots, parts, p_parts, accs=()):
    arrays, pieces = [], []
    for s in slots:
        mine = []
        for four in parts[s]:
            row = []
            for array, index in four:
                found = [i for i, a in enumerate(arrays) if a is array]
                if not found:
                    found = [len(arrays)]
                    arrays.append(array)
                row.append((found[0], index))
            mine.append(row)
        pieces.append(mine)
    if accs:
        shape = jax.ShapeDtypeStruct((2, 4, 2, SHARE, ROWS), jnp.bfloat16)
    else:
        shape = jax.ShapeDtypeStruct((2, len(rows) * SHARE, ROWS), jnp.float32)
    vmem = pl.BlockSpec(memory_space=pltpu.VMEM)
    operands = [*arrays, *p_parts, *accs]
    return pl.pallas_call(
        functools.partial(gram_kernel, slots, rows, pieces, len(arrays), len(p_parts), len(accs)),
        in_specs=[pl.BlockSpec(memory_space=pltpu.SMEM)] + [vmem] * len(operands),
        out_specs=vmem,
        out_shape=shape,
        compiler_params=pltpu.CompilerParams(vmem_limit_bytes=GRAM_VMEM * MIB),
        cost_estimate=pl.CostEstimate(
            flops=4 * len(slots) * len(rows) * SHARE * KSLOT * ROWS, bytes_accessed=8 * MIB, transcendentals=0
        ),
        name=name,
    )(pos, *operands)


def per_device(psi_window, phi_window, psi_region, phi_region, points):
    pos = jnp.stack([lax.axis_index(a) for a in ("x", "core", "zlo", "y")]).astype(jnp.int32)

    def sides(slot):
        return shift(slot, "y", 1), shift(slot, "y", -1)

    def across(below, above):
        return shift(below[0], "y", 1), shift(above[1], "y", -1)

    inner = (pos[2] == 1) | (pos[2] == 2)

    def passed_on(value):
        return jnp.where(inner, value, lax.ppermute(value, "zlo", OUTWARD))

    own = jnp.stack([psi_window, phi_window])
    near = lax.ppermute(own, "zlo", PAIRS)
    other = lax.ppermute(own, "zlo", MIDDLE)
    side0 = sides(own)
    order = points.reshape(4, 4, SHARE).transpose(1, 0, 2).reshape(NPTS, 1)
    picked = gather_points(order, psi_region, phi_region).reshape(4, 4, SHARE, 2 * ORBS)
    by_y = lax.all_to_all(picked, "y", 0, 0, tiled=True)
    near, other, *side0, by_y = together(near, other, *side0, by_y)
    side1 = sides(near)
    third = passed_on(other)
    last = lax.ppermute(near, "zlo", MIDDLE)
    cols = join_orbitals(pos, by_y)
    cols = after(cols, third, last, *side1)

    mine = lax.all_to_all(jnp.concatenate([cols, cols]), ("zhi", "zlo"), 0, 0, tiled=True)
    far0 = across(*side0)
    far1 = across(*side1)
    mine, third, *far01 = together(mine, third, *far0, *far1)
    far0, far1 = far01[:2], far01[2:]

    left, right = shift(mine, "x", 1), shift(mine, "x", -1)
    side2 = sides(third)
    last = passed_on(last)
    far2 = across(*side2)
    left, right, last, *far2 = together(left, right, last, *far2)

    side3 = sides(last)
    swapped = [shift(part, "core", 1) for part in (mine, left, right)]
    to_right, to_left = together(left[:, 0], right[:, 1], *swapped)[:2]
    far = [shift(to_right, "x", 1), shift(to_left, "x", -1)]

    parts = []
    for slot, (below, above), ahead in ((own, side0, far0), (near, side1, far1), (third, side2, far2)):
        parts.append([[(slot, (m,)), (above, (m,)), (ahead[m], ()), (below, (m,))] for m in range(2)])
    near_p = [mine, left, right, *swapped]
    near_acc = gram("gram_near", pos, NEAR_ROWS, (0, 1, 2), parts, near_p)
    below, above, near_acc = together(*side3, near_acc)
    far3 = across(below, above)
    far_p = far + [shift(part, "core", 1) for part in far]
    far_acc = gram("gram_far", pos, FAR_ROWS, (0, 1, 2), parts, far_p)
    parts.append([[(last, (m,)), (above, (m,)), (far3[m], ()), (below, (m,))] for m in range(2)])
    out = gram("gram_last", pos, NEAR_ROWS + FAR_ROWS, (3,), parts, near_p + far_p, (near_acc, far_acc))
    return out.reshape(16, SHARE, ROWS).transpose(2, 0, 1)


def solution(mesh):
    torus = Mesh(mesh.devices.reshape(tuple(SIZES[a] for a in AXES)), AXES)
    in_specs = (P(ORB, GRID), P(ORB, GRID), P(ORB, GRID), P(ORB, GRID), P(GRID))
    out_specs = P(GRID, None, ORB)
    return jax.shard_map(
        per_device, mesh=torus, in_specs=in_specs, out_specs=out_specs, check_vma=False
    )
```

time: 185 us -> 167 us (0.903)
  waiting for transfers between devices: 86.2 us -> 49.4 us
  starting transfers between devices: 36.7 us -> 57.5 us
  other arithmetic: 8.11 us -> 3.74 us
  Pallas kernels: 26.6 us -> 29.6 us
    ppermute x19 -> x25, waiting for transfers between devices: 72.2 us -> 23.4 us  [shift(): return lax.ppermute(value, axis, [(i, (i + step) % n) for i in range(n)])]
    ppermute x2 -> x4, waiting for transfers between devices: 0.01 us -> 15.5 us  [the longest x2 15.5 us: passed_on(): return jnp.where(inner, value, lax.ppermute(value, 'zlo', OUTWARD))]
    ppermute x19 -> x25, starting transfers between devices: 24.8 us -> 38.9 us  [shift(): return lax.ppermute(value, axis, [(i, (i + step) % n) for i in range(n)])]
    ppermute x1, waiting for transfers between devices: 7.29 us -> 0.01 us  [per_device(): near = lax.ppermute(own, 'zlo', PAIRS)]
    concatenate x3 -> x0, other arithmetic: 6.75 us -> none  [ring(): down = shift(jnp.concatenate([slot, above[1:2]]), 'y', -1)]
    slice x6 -> x0, local copies, waits for them, and re-layouts: 4.14 us -> none  [the longest x3 2.07 us: ring(): up = shift(jnp.concatenate([below[0:1], slot]), 'y', 1)]
    unnamed x14 -> x24, local copies, waits for them, and re-layouts: 2.58 us -> 6.45 us
    all_to_all x1, waiting for transfers between devices: 6.73 us -> 10.5 us  [per_device(): lax.all_to_all(jnp.concatenate([cols, cols]), ('zhi', 'zlo'), 0, 0, tiled...]
  transfers between devices with their start and end apart: 23 -> 31, of which waited for: 9 -> 8; matrix products, arithmetic and copies ran while one was open for 7% -> 4% of each run, Pallas kernels for 5% -> 15%
where the time goes in v3:
time: 167 us; the launch traced here: 166 us
  starting transfers between devices  57.5 us (34%)
  waiting for transfers between devices  49.4 us (30%)
  Pallas kernels  29.6 us (18%)
  blocking collectives  14.5 us (9%)
  local copies, waits for them, and re-layouts  11.1 us (7%)
  other arithmetic  3.74 us (2%)
    ppermute x25, starting transfers between devices, shift(): return lax.ppermute(value, axis, [(i, (i + step) % n) for i in range(n)])  38.9 us
    ppermute x25, waiting for transfers between devices, shift(): return lax.ppermute(value, axis, [(i, (i + step) % n) for i in range(n)])  23.4 us
    pallas_call x3, Pallas kernels, gram(): pl.pallas_call(functools.partial(gram_kernel, slots, rows, pieces, len(ar...  19.9 us
    ppermute x2, waiting for transfers between devices, passed_on(): return jnp.where(inner, value, lax.ppermute(value, 'zlo', OUTWARD))  15.5 us
    all_to_all x1, blocking collectives, per_device(): by_y = lax.all_to_all(picked, 'y', 0, 0, tiled=True)  14.5 us
    all_to_all x1, waiting for transfers between devices, per_device(): lax.all_to_all(jnp.concatenate([cols, cols]), ('zhi', 'zlo'), 0, 0, tiled...  10.5 us
    all_to_all x1, starting transfers between devices, per_device(): lax.all_to_all(jnp.concatenate([cols, cols]), ('zhi', 'zlo'), 0, 0, tiled...  10.2 us
    pallas_call x1, Pallas kernels, gather_points(): pl.pallas_call(gather_kernel, grid=(steps,), in_specs=[pl.BlockSpec((NPTS...  8.99 us
  transfers between devices with their start and end apart: 31, of which 8 were waited for; matrix products, arithmetic and copies ran while one was open for 4% of the time, Pallas kernels for 15%

profile of v3, /device:TPU:1, one launch (start us, length us, event | category | flops | bytes accessed | tf_op | source)
XLA Modules:
  0.0 166.1 jit_solution(3770004442170828899)
XLA Ops:
  0.0 1.2 pad_maximum_fusion.1.refs_0_
  1.2 2.6 %collective-permute-start = (bf16[2,192,1024]{2,1,0:T(8,128)(2,1)S(1)}, bf16[2,192,1024]{2,1,0:T(8,128)(2,1)}, u32[]{:S(2)}, u32[]{:S(2)}) collective-permute-start(bf16[2,192,1024]{2,1,0:T(8,128)(2,1)S(1)} %pad_maximum_fusion.1.refs_0_), channel_id=1, source_target_pairs={{0,4},{4,0},{8,12},{12,8},{1,5},{5,1},{9,13},{13,9},{2,6},{6,2},{1... | collective-permute-start | bytes 2359304 | tf_op jit(solution)/shard_map/ppermute | solution.py:200
  3.8 1.5 collective-permute-start.1
  5.3 1.3 collective-permute-start.2
  6.6 1.4 collective-permute-start.3
  8.1 0.9 reshape.16.points_ref
  9.0 9.0 %gather_points.1 = bf16[768,384]{1,0:T(8,128)(2,1)} custom-call(s32[768,1]{1,0:T(8,128)} %reshape.16.points_ref, bf16[192,6144]{1,0:T(8,128)(2,1)} %psi_ref.1, bf16[192,6144]{1,0:T(8,128)(2,1)} %phi_ref.1), custom_call_target="tpu_custom_call" | custom-call | flops 3623878656 | bytes 4718592 | tf_op jit(solution)/shard_map/gather_points/pallas_call | solution.py:69
  18.0 14.5 %all_to_all.10.in_ref = bf16[4,4,48,384]{3,2,1,0:T(8,128)(2,1)} all-to-all(bf16[4,4,48,384]{3,2,1,0:T(8,128)(2,1)} %bitcast.31), channel_id=1, replica_groups=mesh['zhi'=2,'x'=4,'core'=2,'zlo'=4,'y'=4] {'y'}, dimensions={0} | all-to-all | bytes 1179648 | tf_op jit(solution)/shard_map/all_to_all | solution.py:205
  32.5 0.9 copy-done
  33.4 1.3 collective-permute-start.4
  34.7 0.9 collective-permute-start.6
  35.6 1.9 %collective-permute-start.7 = (bf16[2,192,1024]{2,1,0:T(8,128)(2,1)}, bf16[2,192,1024]{2,1,0:T(8,128)(2,1)}, u32[]{:S(2)}, u32[]{:S(2)}) collective-permute-start(bf16[2,192,1024]{2,1,0:T(8,128)(2,1)} %collective-permute-done.refs_5_), channel_id=1, source_target_pairs={{0,3},{1,0},{2,1},{3,2},{4,7},{5,4},{6,5},{7,6},{8,11},{9,8},{10,9... | collective-permute-start | bytes 2359304 | tf_op jit(solution)/shard_map/ppermute | solution.py:34
  37.5 1.5 collective-permute-start.5
  39.1 1.1 copy-done.2
  40.9 12.9 %collective-permute-done.4 = bf16[2,192,1024]{2,1,0:T(8,128)(2,1)} collective-permute-done((bf16[2,192,1024]{2,1,0:T(8,128)(2,1)}, bf16[2,192,1024]{2,1,0:T(8,128)(2,1)}, u32[]{:S(2)}, u32[]{:S(2)}) %collective-permute-start.4) | collective-permute-done | bytes 786464 | tf_op jit(solution)/shard_map/ppermute | solution.py:197
  53.8 1.2 broadcast_select_fusion.1.refs_10_
  55.1 1.1 pad_maximum_fusion
  56.2 10.2 %all-to-all-start.1 = ((bf16[8,2,48,768]{3,2,1,0:T(8,128)(2,1)}), bf16[8,2,48,768]{3,2,1,0:T(8,128)(2,1)S(1)}, u32[]{:S(2)}, u32[]{:S(2)}) async-start(bf16[8,2,48,768]{3,2,1,0:T(8,128)(2,1)} %pad_maximum_fusion), calls=%async_computation.1 | async-start | bytes 2359296 | tf_op jit(solution)/shard_map/all_to_all | solution.py:213
  66.5 1.0 slice_bitcast_fusion.8
  67.6 2.7 %collective-permute-start.9 = (bf16[192,1024]{1,0:T(8,128)(2,1)S(1)}, bf16[192,1024]{1,0:T(8,128)(2,1)S(1)}, u32[]{:S(2)}, u32[]{:S(2)}) collective-permute-start(bf16[192,1024]{1,0:T(8,128)(2,1)S(1)} %slice_bitcast_fusion.8), channel_id=1, source_target_pairs={{0,3},{1,0},{2,1},{3,2},{4,7},{5,4},{6,5},{7,6},{8,11},{9,8},{10,9... | collective-permute-start | bytes 1179656 | tf_op jit(solution)/shard_map/ppermute | solution.py:34
  70.3 1.0 slice_bitcast_fusion.5
  71.4 1.0 slice_bitcast_fusion.4
  72.4 2.7 %collective-permute-start.11 = (bf16[192,1024]{1,0:T(8,128)(2,1)S(1)}, bf16[192,1024]{1,0:T(8,128)(2,1)S(1)}, u32[]{:S(2)}, u32[]{:S(2)}) collective-permute-start(bf16[192,1024]{1,0:T(8,128)(2,1)S(1)} %slice_bitcast_fusion.4), channel_id=1, source_target_pairs={{0,3},{1,0},{2,1},{3,2},{4,7},{5,4},{6,5},{7,6},{8,11},{9,8},{10,9... | collective-permute-start | bytes 1179656 | tf_op jit(solution)/shard_map/ppermute | solution.py:34
  76.7 7.0 %collective-permute-done.10.refs_7_ = bf16[192,1024]{1,0:T(8,128)(2,1)S(1)} collective-permute-done((bf16[192,1024]{1,0:T(8,128)(2,1)S(1)}, bf16[192,1024]{1,0:T(8,128)(2,1)S(1)}, u32[]{:S(2)}, u32[]{:S(2)}) %collective-permute-start.10) | collective-permute-done | bytes 393248 | tf_op jit(solution)/shard_map/ppermute | solution.py:34
  83.7 0.8 copy-done.7
  84.5 0.8 copy-done.9
  85.2 10.5 %all-to-all-done.1.refs_15_.refs_5_ = bf16[8,2,48,768]{3,2,1,0:T(8,128)(2,1)S(1)} async-done(((bf16[8,2,48,768]{3,2,1,0:T(8,128)(2,1)}), bf16[8,2,48,768]{3,2,1,0:T(8,128)(2,1)S(1)}, u32[]{:S(2)}, u32[]{:S(2)}) %all-to-all-start.1) | async-done | bytes 1179680 | tf_op jit(solution)/shard_map/all_to_all | solution.py:213
  95.7 2.7 %collective-permute-start.17 = (bf16[2,192,1024]{2,1,0:T(8,128)(2,1)S(1)}, bf16[2,192,1024]{2,1,0:T(8,128)(2,1)S(1)}, u32[]{:S(2)}, u32[]{:S(2)}) collective-permute-start(bf16[2,192,1024]{2,1,0:T(8,128)(2,1)S(1)} %broadcast_select_fusion.1.refs_10_), channel_id=1, source_target_pairs={{0,3},{1,0},{2,1},{3,2},{4,7},{5,4},{6,5},{7,6},{8,11},{9,8},{10,9... | collective-permute-start | bytes 2359304 | tf_op jit(solution)/shard_map/ppermute | solution.py:34
  98.5 1.2 collective-permute-start.12
  99.7 1.5 collective-permute-start.13
  101.2 1.5 collective-permute-start.14
  102.7 10.0 %collective-permute-done.15.refs_13_ = bf16[2,192,1024]{2,1,0:T(8,128)(2,1)S(1)} collective-permute-done((bf16[2,192,1024]{2,1,0:T(8,128)(2,1)S(1)}, bf16[2,192,1024]{2,1,0:T(8,128)(2,1)S(1)}, u32[]{:S(2)}, u32[]{:S(2)}) %collective-permute-start.15) | collective-permute-done | bytes 786464 | tf_op jit(solution)/shard_map/ppermute | solution.py:34
  112.9 2.7 %collective-permute-start.18 = (bf16[192,1024]{1,0:T(8,128)(2,1)S(1)}, bf16[192,1024]{1,0:T(8,128)(2,1)S(1)}, u32[]{:S(2)}, u32[]{:S(2)}) collective-permute-start(bf16[192,1024]{1,0:T(8,128)(2,1)S(1)} %slice_bitcast_fusion.2), channel_id=1, source_target_pairs={{0,3},{1,0},{2,1},{3,2},{4,7},{5,4},{6,5},{7,6},{8,11},{9,8},{10,9... | collective-permute-start | bytes 1179656 | tf_op jit(solution)/shard_map/ppermute | solution.py:34
  115.6 2.6 %collective-permute-done.14 = bf16[2,192,1024]{2,1,0:T(8,128)(2,1)S(1)} collective-permute-done((bf16[2,192,1024]{2,1,0:T(8,128)(2,1)}, bf16[2,192,1024]{2,1,0:T(8,128)(2,1)S(1)}, u32[]{:S(2)}, u32[]{:S(2)}) %collective-permute-start.14) | collective-permute-done | bytes 786464 | tf_op jit(solution)/shard_map/ppermute | solution.py:197
  118.3 5.4 %collective-permute-start.21 = (bf16[8,2,48,768]{3,2,1,0:T(8,128)(2,1)S(1)}, bf16[8,2,48,768]{3,2,1,0:T(8,128)(2,1)S(1)}, u32[]{:S(2)}, u32[]{:S(2)}) collective-permute-start(bf16[8,2,48,768]{3,2,1,0:T(8,128)(2,1)S(1)} %all-to-all-done.1.refs_15_.refs_5_), channel_id=1, source_target_pairs={{0,16},{16,0},{1,17},{17,1},{2,18},{18,2},{3,19},{19,3},{4,20},{20... | collective-permute-start | bytes 3538952 | tf_op jit(solution)/shard_map/ppermute | solution.py:34
  123.7 4.5 %collective-permute-start.22 = (bf16[8,2,48,768]{3,2,0,1:T(8,128)(2,1)S(1)}, bf16[8,2,48,768]{3,2,0,1:T(8,128)(2,1)S(1)}, u32[]{:S(2)}, u32[]{:S(2)}) collective-permute-start(bf16[8,2,48,768]{3,2,0,1:T(8,128)(2,1)S(1)} %collective-permute-done.12), channel_id=1, source_target_pairs={{0,16},{16,0},{1,17},{17,1},{2,18},{18,2},{3,19},{19,3},{4,20},{20... | collective-permute-start | bytes 3538952 | tf_op jit(solution)/shard_map/ppermute | solution.py:34
  128.4 2.7 %collective-permute-start.20 = (bf16[2,192,1024]{2,1,0:T(8,128)(2,1)S(1)}, bf16[2,192,1024]{2,1,0:T(8,128)(2,1)S(1)}, u32[]{:S(2)}, u32[]{:S(2)}) collective-permute-start(bf16[2,192,1024]{2,1,0:T(8,128)(2,1)S(1)} %broadcast_select_fusion.refs_0_), channel_id=1, source_target_pairs={{0,3},{1,0},{2,1},{3,2},{4,7},{5,4},{6,5},{7,6},{8,11},{9,8},{10,9... | collective-permute-start | bytes 2359304 | tf_op jit(solution)/shard_map/ppermute | solution.py:34
  131.1 1.3 collective-permute-done.23
  132.4 1.1 collective-permute-start.26
  133.6 1.5 collective-permute-start.27
  135.5 1.0 copy-done.1
  136.9 9.3 %gram_near.1.refs_15_ = f32[2,576,1024]{2,1,0:T(8,128)S(1)} custom-call(s32[4]{0:T(128)S(1)} %pad_add_fusion.pos_ref, bf16[2,192,1024]{2,1,0:T(8,128)(2,1)S(1)} %pad_maximum_fusion.1.refs_0_, bf16[2,192,1024]{2,1,0:T(8,128)(2,1)S(1)} %copy-done.1, bf16[192,1024]{1,0:T(8,128)(2,1)S(1)} %copy-done.4, bf16[2,192,1024]{2,1,0:T(8,128)(2,1)S(1)} %collective-permute-done.2.refs_3_, ...), custom_call_target="tpu_custom_call" | custom-call | flops 5435817984 | bytes 8388608 | tf_op jit(solution)/shard_map/gram_near/pallas_call | solution.py:172
  146.3 2.0 %collective-permute-done.19.refs_3_ = bf16[2,192,1024]{2,1,0:T(8,128)(2,1)S(1)} collective-permute-done((bf16[2,192,1024]{2,1,0:T(8,128)(2,1)S(1)}, bf16[2,192,1024]{2,1,0:T(8,128)(2,1)S(1)}, u32[]{:S(2)}, u32[]{:S(2)}) %collective-permute-start.19) | collective-permute-done | bytes 786464 | tf_op jit(solution)/shard_map/ppermute | solution.py:34
  148.3 1.2 collective-permute-start.28
  149.8 2.7 %collective-permute-start.25 = (bf16[192,1024]{1,0:T(8,128)(2,1)S(1)}, bf16[192,1024]{1,0:T(8,128)(2,1)S(1)}, u32[]{:S(2)}, u32[]{:S(2)}) collective-permute-start(bf16[192,1024]{1,0:T(8,128)(2,1)S(1)} %slice_bitcast_fusion.6), channel_id=1, source_target_pairs={{0,3},{1,0},{2,1},{3,2},{4,7},{5,4},{6,5},{7,6},{8,11},{9,8},{10,9... | collective-permute-start | bytes 1179656 | tf_op jit(solution)/shard_map/ppermute | solution.py:34
  152.5 5.7 %gram_far.1.refs_16_ = f32[2,192,1024]{2,1,0:T(8,128)S(1)} custom-call(s32[4]{0:T(128)S(1)} %pad_add_fusion.pos_ref, bf16[2,192,1024]{2,1,0:T(8,128)(2,1)S(1)} %pad_maximum_fusion.1.refs_0_, bf16[2,192,1024]{2,1,0:T(8,128)(2,1)S(1)} %copy-done.1, bf16[192,1024]{1,0:T(8,128)(2,1)S(1)} %copy-done.4, bf16[2,192,1024]{2,1,0:T(8,128)(2,1)S(1)} %collective-permute-done.2.refs_3_, ...), custom_call_target="tpu_custom_call" | custom-call | flops 1811939328 | bytes 8388608 | tf_op jit(solution)/shard_map/gram_far/pallas_call | solution.py:172
  158.3 3.0 %collective-permute-done.24.refs_2_ = bf16[192,1024]{1,0:T(8,128)(2,1)S(1)} collective-permute-done((bf16[192,1024]{1,0:T(8,128)(2,1)S(1)}, bf16[192,1024]{1,0:T(8,128)(2,1)S(1)}, u32[]{:S(2)}, u32[]{:S(2)}) %collective-permute-start.24) | collective-permute-done | bytes 393248 | tf_op jit(solution)/shard_map/ppermute | solution.py:34
  161.2 4.9 %gram_last.1 = bf16[2,4,2,48,1024]{4,3,2,1,0:T(8,128)(2,1)} custom-call(s32[4]{0:T(128)S(1)} %pad_add_fusion.pos_ref, bf16[2,192,1024]{2,1,0:T(8,128)(2,1)S(1)} %broadcast_select_fusion.refs_0_, bf16[2,192,1024]{2,1,0:T(8,128)(2,1)S(1)} %collective-permute-done.20.refs_1_, bf16[192,1024]{1,0:T(8,128)(2,1)S(1)} %collective-permute-done.24.refs_2_, ...), custom_call_target="tpu_custom_call" | custom-call | flops 2415919104 | bytes 8388608 | tf_op jit(solution)/shard_map/gram_last/pallas_call | solution.py:172
  (66 shorter events, 4.2 us)
Async XLA Ops:
  0.0 8.0 %copy-start.11 = (s32[768]{0:T(1024)S(1)}, s32[768]{0:T(1024)}, u32[]{:S(2)}) copy-start(s32[768]{0:T(1024)} %param.9) | copy-start | bytes 9220
  1.2 31.3 %collective-permute-start = (bf16[2,192,1024]{2,1,0:T(8,128)(2,1)S(1)}, bf16[2,192,1024]{2,1,0:T(8,128)(2,1)}, u32[]{:S(2)}, u32[]{:S(2)}) collective-permute-start(bf16[2,192,1024]{2,1,0:T(8,128)(2,1)S(1)} %pad_maximum_fusion.1.refs_0_), channel_id=1, source_target_pairs={{0,4},{4,0},{8,12},{12,8},{1,5},{5,1},{9,13},{13,9},{2,6},{6,2},{1... | collective-permute-start | bytes 2359304 | tf_op jit(solution)/shard_map/ppermute | solution.py:200
  3.8 28.8 %collective-permute-start.1 = (bf16[2,192,1024]{2,1,0:T(8,128)(2,1)S(1)}, bf16[2,192,1024]{2,1,0:T(8,128)(2,1)}, u32[]{:S(2)}, u32[]{:S(2)}) collective-permute-start(bf16[2,192,1024]{2,1,0:T(8,128)(2,1)S(1)} %pad_maximum_fusion.1.refs_0_), channel_id=1, source_target_pairs={{4,8},{8,4},{5,9},{9,5},{6,10},{10,6},{7,11},{11,7},{20,24},{24,20... | collective-permute-start | bytes 2359304 | tf_op jit(solution)/shard_map/ppermute | solution.py:201
  5.3 27.2 %collective-permute-start.2 = (bf16[2,192,1024]{2,1,0:T(8,128)(2,1)S(1)}, bf16[2,192,1024]{2,1,0:T(8,128)(2,1)S(1)}, u32[]{:S(2)}, u32[]{:S(2)}) collective-permute-start(bf16[2,192,1024]{2,1,0:T(8,128)(2,1)S(1)} %pad_maximum_fusion.1.refs_0_), channel_id=1, source_target_pairs={{0,1},{1,2},{2,3},{3,0},{4,5},{5,6},{6,7},{7,4},{8,9},{9,10},{10,1... | collective-permute-start | bytes 2359304 | tf_op jit(solution)/shard_map/ppermute | solution.py:34
  6.6 25.9 %collective-permute-start.3 = (bf16[2,192,1024]{2,1,0:T(8,128)(2,1)S(1)}, bf16[2,192,1024]{2,1,0:T(8,128)(2,1)S(1)}, u32[]{:S(2)}, u32[]{:S(2)}) collective-permute-start(bf16[2,192,1024]{2,1,0:T(8,128)(2,1)S(1)} %pad_maximum_fusion.1.refs_0_), channel_id=1, source_target_pairs={{0,3},{1,0},{2,1},{3,2},{4,7},{5,4},{6,5},{7,6},{8,11},{9,8},{10,9... | collective-permute-start | bytes 2359304 | tf_op jit(solution)/shard_map/ppermute | solution.py:34
  32.5 0.9 copy-start
  33.4 20.4 %collective-permute-start.4 = (bf16[2,192,1024]{2,1,0:T(8,128)(2,1)}, bf16[2,192,1024]{2,1,0:T(8,128)(2,1)}, u32[]{:S(2)}, u32[]{:S(2)}) collective-permute-start(bf16[2,192,1024]{2,1,0:T(8,128)(2,1)} %collective-permute-done.1), channel_id=1, source_target_pairs={{4,0},{8,12},{5,1},{9,13},{6,2},{10,14},{7,3},{11,15},{20,16},{24,... | collective-permute-start | bytes 2359304 | tf_op jit(solution)/shard_map/ppermute | solution.py:197
  34.7 20.3 %collective-permute-start.6 = (bf16[2,192,1024]{2,1,0:T(8,128)(2,1)}, bf16[2,192,1024]{2,1,0:T(8,128)(2,1)}, u32[]{:S(2)}, u32[]{:S(2)}) collective-permute-start(bf16[2,192,1024]{2,1,0:T(8,128)(2,1)} %collective-permute-done.refs_5_), channel_id=1, source_target_pairs={{0,1},{1,2},{2,3},{3,0},{4,5},{5,6},{6,7},{7,4},{8,9},{9,10},{10,1... | collective-permute-start | bytes 2359304 | tf_op jit(solution)/shard_map/ppermute | solution.py:34
  35.6 19.4 %collective-permute-start.7 = (bf16[2,192,1024]{2,1,0:T(8,128)(2,1)}, bf16[2,192,1024]{2,1,0:T(8,128)(2,1)}, u32[]{:S(2)}, u32[]{:S(2)}) collective-permute-start(bf16[2,192,1024]{2,1,0:T(8,128)(2,1)} %collective-permute-done.refs_5_), channel_id=1, source_target_pairs={{0,3},{1,0},{2,1},{3,2},{4,7},{5,4},{6,5},{7,6},{8,11},{9,8},{10,9... | collective-permute-start | bytes 2359304 | tf_op jit(solution)/shard_map/ppermute | solution.py:34
  37.5 17.6 %collective-permute-start.5 = (bf16[2,192,1024]{2,1,0:T(8,128)(2,1)}, bf16[2,192,1024]{2,1,0:T(8,128)(2,1)}, u32[]{:S(2)}, u32[]{:S(2)}) collective-permute-start(bf16[2,192,1024]{2,1,0:T(8,128)(2,1)} %collective-permute-done.refs_5_), channel_id=1, source_target_pairs={{4,8},{8,4},{5,9},{9,5},{6,10},{10,6},{7,11},{11,7},{20,24},{24,20... | collective-permute-start | bytes 2359304 | tf_op jit(solution)/shard_map/ppermute | solution.py:209
  39.1 1.1 copy-start.2
  56.2 39.5 %all-to-all-start.1 = ((bf16[8,2,48,768]{3,2,1,0:T(8,128)(2,1)}), bf16[8,2,48,768]{3,2,1,0:T(8,128)(2,1)S(1)}, u32[]{:S(2)}, u32[]{:S(2)}) async-start(bf16[8,2,48,768]{3,2,1,0:T(8,128)(2,1)} %pad_maximum_fusion), calls=%async_computation.1 | async-start | bytes 2359296 | tf_op jit(solution)/shard_map/all_to_all | solution.py:213
  66.4 8.7 %collective-permute-start.8 = (bf16[192,1024]{1,0:T(8,128)(2,1)S(1)}, bf16[192,1024]{1,0:T(8,128)(2,1)S(1)}, u32[]{:S(2)}, u32[]{:S(2)}) collective-permute-start(bf16[192,1024]{1,0:T(8,128)(2,1)S(1)} %slice_bitcast_fusion.9), channel_id=1, source_target_pairs={{0,1},{1,2},{2,3},{3,0},{4,5},{5,6},{6,7},{7,4},{8,9},{9,10},{10,1... | collective-permute-start | bytes 1179656 | tf_op jit(solution)/shard_map/ppermute | solution.py:34
  67.6 8.4 %collective-permute-start.9 = (bf16[192,1024]{1,0:T(8,128)(2,1)S(1)}, bf16[192,1024]{1,0:T(8,128)(2,1)S(1)}, u32[]{:S(2)}, u32[]{:S(2)}) collective-permute-start(bf16[192,1024]{1,0:T(8,128)(2,1)S(1)} %slice_bitcast_fusion.8), channel_id=1, source_target_pairs={{0,3},{1,0},{2,1},{3,2},{4,7},{5,4},{6,5},{7,6},{8,11},{9,8},{10,9... | collective-permute-start | bytes 1179656 | tf_op jit(solution)/shard_map/ppermute | solution.py:34
  71.3 12.4 %collective-permute-start.10 = (bf16[192,1024]{1,0:T(8,128)(2,1)S(1)}, bf16[192,1024]{1,0:T(8,128)(2,1)S(1)}, u32[]{:S(2)}, u32[]{:S(2)}) collective-permute-start(bf16[192,1024]{1,0:T(8,128)(2,1)S(1)} %slice_bitcast_fusion.5), channel_id=1, source_target_pairs={{0,1},{1,2},{2,3},{3,0},{4,5},{5,6},{6,7},{7,4},{8,9},{9,10},{10,1... | collective-permute-start | bytes 1179656 | tf_op jit(solution)/shard_map/ppermute | solution.py:34
  72.4 12.0 %collective-permute-start.11 = (bf16[192,1024]{1,0:T(8,128)(2,1)S(1)}, bf16[192,1024]{1,0:T(8,128)(2,1)S(1)}, u32[]{:S(2)}, u32[]{:S(2)}) collective-permute-start(bf16[192,1024]{1,0:T(8,128)(2,1)S(1)} %slice_bitcast_fusion.4), channel_id=1, source_target_pairs={{0,3},{1,0},{2,1},{3,2},{4,7},{5,4},{6,5},{7,6},{8,11},{9,8},{10,9... | collective-permute-start | bytes 1179656 | tf_op jit(solution)/shard_map/ppermute | solution.py:34
  75.2 0.7 copy-start.3
  75.9 0.7 copy-start.5
  83.7 0.8 copy-start.7
  84.5 0.8 copy-start.9
  95.7 17.0 %collective-permute-start.15 = (bf16[2,192,1024]{2,1,0:T(8,128)(2,1)S(1)}, bf16[2,192,1024]{2,1,0:T(8,128)(2,1)S(1)}, u32[]{:S(2)}, u32[]{:S(2)}) collective-permute-start(bf16[2,192,1024]{2,1,0:T(8,128)(2,1)S(1)} %broadcast_select_fusion.1.refs_10_), channel_id=1, source_target_pairs={{0,1},{1,2},{2,3},{3,0},{4,5},{5,6},{6,7},{7,4},{8,9},{9,10},{10,1... | collective-permute-start | bytes 2359304 | tf_op jit(solution)/shard_map/ppermute | solution.py:34
  95.7 17.1 %collective-permute-start.17 = (bf16[2,192,1024]{2,1,0:T(8,128)(2,1)S(1)}, bf16[2,192,1024]{2,1,0:T(8,128)(2,1)S(1)}, u32[]{:S(2)}, u32[]{:S(2)}) collective-permute-start(bf16[2,192,1024]{2,1,0:T(8,128)(2,1)S(1)} %broadcast_select_fusion.1.refs_10_), channel_id=1, source_target_pairs={{0,3},{1,0},{2,1},{3,2},{4,7},{5,4},{6,5},{7,6},{8,11},{9,8},{10,9... | collective-permute-start | bytes 2359304 | tf_op jit(solution)/shard_map/ppermute | solution.py:34
  98.5 25.2 %collective-permute-start.12 = (bf16[8,2,48,768]{3,2,0,1:T(8,128)(2,1)S(1)}, bf16[8,2,48,768]{3,2,0,1:T(8,128)(2,1)S(1)}, u32[]{:S(2)}, u32[]{:S(2)}) collective-permute-start(bf16[8,2,48,768]{3,2,0,1:T(8,128)(2,1)S(1)} %copy.38), channel_id=1, source_target_pairs={{0,32},{32,64},{64,96},{96,0},{1,33},{33,65},{65,97},{97,1},{2,34}... | collective-permute-start | bytes 3538952 | tf_op jit(solution)/shard_map/ppermute | solution.py:34
  99.7 24.0 %collective-permute-start.13 = (bf16[8,2,48,768]{3,2,0,1:T(8,128)(2,1)S(1)}, bf16[8,2,48,768]{3,2,0,1:T(8,128)(2,1)S(1)}, u32[]{:S(2)}, u32[]{:S(2)}) collective-permute-start(bf16[8,2,48,768]{3,2,0,1:T(8,128)(2,1)S(1)} %copy.38), channel_id=1, source_target_pairs={{0,96},{32,0},{64,32},{96,64},{1,97},{33,1},{65,33},{97,65},{2,98}... | collective-permute-start | bytes 3538952 | tf_op jit(solution)/shard_map/ppermute | solution.py:34
  101.2 17.0 %collective-permute-start.14 = (bf16[2,192,1024]{2,1,0:T(8,128)(2,1)}, bf16[2,192,1024]{2,1,0:T(8,128)(2,1)S(1)}, u32[]{:S(2)}, u32[]{:S(2)}) collective-permute-start(bf16[2,192,1024]{2,1,0:T(8,128)(2,1)} %collective-permute-done.5), channel_id=1, source_target_pairs={{4,0},{8,12},{5,1},{9,13},{6,2},{10,14},{7,3},{11,15},{20,16},{24,... | collective-permute-start | bytes 2359304 | tf_op jit(solution)/shard_map/ppermute | solution.py:197
  112.8 10.9 %collective-permute-start.16 = (bf16[192,1024]{1,0:T(8,128)(2,1)S(1)}, bf16[192,1024]{1,0:T(8,128)(2,1)S(1)}, u32[]{:S(2)}, u32[]{:S(2)}) collective-permute-start(bf16[192,1024]{1,0:T(8,128)(2,1)S(1)} %slice_bitcast_fusion.3), channel_id=1, source_target_pairs={{0,1},{1,2},{2,3},{3,0},{4,5},{5,6},{6,7},{7,4},{8,9},{9,10},{10,1... | collective-permute-start | bytes 1179656 | tf_op jit(solution)/shard_map/ppermute | solution.py:34
  112.9 10.8 %collective-permute-start.18 = (bf16[192,1024]{1,0:T(8,128)(2,1)S(1)}, bf16[192,1024]{1,0:T(8,128)(2,1)S(1)}, u32[]{:S(2)}, u32[]{:S(2)}) collective-permute-start(bf16[192,1024]{1,0:T(8,128)(2,1)S(1)} %slice_bitcast_fusion.2), channel_id=1, source_target_pairs={{0,3},{1,0},{2,1},{3,2},{4,7},{5,4},{6,5},{7,6},{8,11},{9,8},{10,9... | collective-permute-start | bytes 1179656 | tf_op jit(solution)/shard_map/ppermute | solution.py:34
  118.3 12.8 %collective-permute-start.21 = (bf16[8,2,48,768]{3,2,1,0:T(8,128)(2,1)S(1)}, bf16[8,2,48,768]{3,2,1,0:T(8,128)(2,1)S(1)}, u32[]{:S(2)}, u32[]{:S(2)}) collective-permute-start(bf16[8,2,48,768]{3,2,1,0:T(8,128)(2,1)S(1)} %all-to-all-done.1.refs_15_.refs_5_), channel_id=1, source_target_pairs={{0,16},{16,0},{1,17},{17,1},{2,18},{18,2},{3,19},{19,3},{4,20},{20... | collective-permute-start | bytes 3538952 | tf_op jit(solution)/shard_map/ppermute | solution.py:34
  123.7 7.4 %collective-permute-start.22 = (bf16[8,2,48,768]{3,2,0,1:T(8,128)(2,1)S(1)}, bf16[8,2,48,768]{3,2,0,1:T(8,128)(2,1)S(1)}, u32[]{:S(2)}, u32[]{:S(2)}) collective-permute-start(bf16[8,2,48,768]{3,2,0,1:T(8,128)(2,1)S(1)} %collective-permute-done.12), channel_id=1, source_target_pairs={{0,16},{16,0},{1,17},{17,1},{2,18},{18,2},{3,19},{19,3},{4,20},{20... | collective-permute-start | bytes 3538952 | tf_op jit(solution)/shard_map/ppermute | solution.py:34
  128.3 4.2 %collective-permute-start.23 = (bf16[8,2,48,768]{3,2,0,1:T(8,128)(2,1)S(1)}, bf16[8,2,48,768]{3,2,0,1:T(8,128)(2,1)S(1)}, u32[]{:S(2)}, u32[]{:S(2)}) collective-permute-start(bf16[8,2,48,768]{3,2,0,1:T(8,128)(2,1)S(1)} %collective-permute-done.13), channel_id=1, source_target_pairs={{0,16},{16,0},{1,17},{17,1},{2,18},{18,2},{3,19},{19,3},{4,20},{20... | collective-permute-start | bytes 3538952 | tf_op jit(solution)/shard_map/ppermute | solution.py:34
  128.4 19.9 %collective-permute-start.19 = (bf16[2,192,1024]{2,1,0:T(8,128)(2,1)S(1)}, bf16[2,192,1024]{2,1,0:T(8,128)(2,1)S(1)}, u32[]{:S(2)}, u32[]{:S(2)}) collective-permute-start(bf16[2,192,1024]{2,1,0:T(8,128)(2,1)S(1)} %broadcast_select_fusion.refs_0_), channel_id=1, source_target_pairs={{0,1},{1,2},{2,3},{3,0},{4,5},{5,6},{6,7},{7,4},{8,9},{9,10},{10,1... | collective-permute-start | bytes 2359304 | tf_op jit(solution)/shard_map/ppermute | solution.py:34
  128.4 19.9 %collective-permute-start.20 = (bf16[2,192,1024]{2,1,0:T(8,128)(2,1)S(1)}, bf16[2,192,1024]{2,1,0:T(8,128)(2,1)S(1)}, u32[]{:S(2)}, u32[]{:S(2)}) collective-permute-start(bf16[2,192,1024]{2,1,0:T(8,128)(2,1)S(1)} %broadcast_select_fusion.refs_0_), channel_id=1, source_target_pairs={{0,3},{1,0},{2,1},{3,2},{4,7},{5,4},{6,5},{7,6},{8,11},{9,8},{10,9... | collective-permute-start | bytes 2359304 | tf_op jit(solution)/shard_map/ppermute | solution.py:34
  132.4 15.9 %collective-permute-start.26 = (bf16[8,48,768]{2,1,0:T(8,128)(2,1)S(1)}, bf16[8,48,768]{2,1,0:T(8,128)(2,1)S(1)}, u32[]{:S(2)}, u32[]{:S(2)}) collective-permute-start(bf16[8,48,768]{2,1,0:T(8,128)(2,1)S(1)} %get-tuple-element.46), channel_id=1, source_target_pairs={{0,32},{32,64},{64,96},{96,0},{1,33},{33,65},{65,97},{97,1},{2,34}... | collective-permute-start | bytes 1769480 | tf_op jit(solution)/shard_map/ppermute | solution.py:34
  133.6 16.0 %collective-permute-start.27 = (bf16[8,48,768]{2,1,0:T(8,128)(2,1)S(1)}, bf16[8,48,768]{2,1,0:T(8,128)(2,1)S(1)}, u32[]{:S(2)}, u32[]{:S(2)}) collective-permute-start(bf16[8,48,768]{2,1,0:T(8,128)(2,1)S(1)} %get-tuple-element.47), channel_id=1, source_target_pairs={{0,96},{32,0},{64,32},{96,64},{1,97},{33,1},{65,33},{97,65},{2,98}... | collective-permute-start | bytes 1769480 | tf_op jit(solution)/shard_map/ppermute | solution.py:34
  135.4 1.1 copy-start.1
  135.4 1.2 copy-start.4
  135.4 1.3 copy-start.6
  135.4 1.4 copy-start.8
  135.4 1.6 copy-start.10
  148.3 4.3 %collective-permute-start.28 = (bf16[8,48,768]{2,1,0:T(8,128)(2,1)S(1)}, bf16[8,48,768]{2,1,0:T(8,128)(2,1)S(1)}, u32[]{:S(2)}, u32[]{:S(2)}) collective-permute-start(bf16[8,48,768]{2,1,0:T(8,128)(2,1)S(1)} %collective-permute-done.26.refs_15_.refs_11_), channel_id=1, source_target_pairs={{0,16},{16,0},{1,17},{17,1},{2,18},{18,2},{3,19},{19,3},{4,20},{20... | collective-permute-start | bytes 1769480 | tf_op jit(solution)/shard_map/ppermute | solution.py:34
  149.5 3.0 %collective-permute-start.29 = (bf16[8,48,768]{2,1,0:T(8,128)(2,1)S(1)}, bf16[8,48,768]{2,1,0:T(8,128)(2,1)S(1)}, u32[]{:S(2)}, u32[]{:S(2)}) collective-permute-start(bf16[8,48,768]{2,1,0:T(8,128)(2,1)S(1)} %collective-permute-done.27.refs_16_.refs_12_), channel_id=1, source_target_pairs={{0,16},{16,0},{1,17},{17,1},{2,18},{18,2},{3,19},{19,3},{4,20},{20... | collective-permute-start | bytes 1769480 | tf_op jit(solution)/shard_map/ppermute | solution.py:34
  149.7 11.6 %collective-permute-start.24 = (bf16[192,1024]{1,0:T(8,128)(2,1)S(1)}, bf16[192,1024]{1,0:T(8,128)(2,1)S(1)}, u32[]{:S(2)}, u32[]{:S(2)}) collective-permute-start(bf16[192,1024]{1,0:T(8,128)(2,1)S(1)} %slice_bitcast_fusion.7), channel_id=1, source_target_pairs={{0,1},{1,2},{2,3},{3,0},{4,5},{5,6},{6,7},{7,4},{8,9},{9,10},{10,1... | collective-permute-start | bytes 1179656 | tf_op jit(solution)/shard_map/ppermute | solution.py:34
  149.8 11.4 %collective-permute-start.25 = (bf16[192,1024]{1,0:T(8,128)(2,1)S(1)}, bf16[192,1024]{1,0:T(8,128)(2,1)S(1)}, u32[]{:S(2)}, u32[]{:S(2)}) collective-permute-start(bf16[192,1024]{1,0:T(8,128)(2,1)S(1)} %slice_bitcast_fusion.6), channel_id=1, source_target_pairs={{0,3},{1,0},{2,1},{3,2},{4,7},{5,4},{6,5},{7,6},{8,11},{9,8},{10,9... | collective-permute-start | bytes 1179656 | tf_op jit(solution)/shard_map/ppermute | solution.py:34

commit v4 on v3

--- a/solution.py
+++ b/solution.py
@@ -202,8 +202,8 @@
     side0 = sides(own)
     order = points.reshape(4, 4, SHARE).transpose(1, 0, 2).reshape(NPTS, 1)
     picked = gather_points(order, psi_region, phi_region).reshape(4, 4, SHARE, 2 * ORBS)
+    near, other, *side0, picked = together(near, other, *side0, picked)
     by_y = lax.all_to_all(picked, "y", 0, 0, tiled=True)
-    near, other, *side0, by_y = together(near, other, *side0, by_y)
     side1 = sides(near)
     third = passed_on(other)
     last = lax.ppermute(near, "zlo", MIDDLE)

time: 167 us -> 164 us (0.982)
  blocking collectives: 14.5 us -> 0 us
  waiting for transfers between devices: 49.4 us -> 61.6 us
  starting transfers between devices: 57.5 us -> 59.7 us
    all_to_all x0 -> x1, waiting for transfers between devices: none -> 17.5 us  [per_device(): by_y = lax.all_to_all(picked, 'y', 0, 0, tiled=True)]
    all_to_all x1 -> x0, blocking collectives: 14.5 us -> none  [per_device(): by_y = lax.all_to_all(picked, 'y', 0, 0, tiled=True)]
    ppermute x2, waiting for transfers between devices: 15.5 us -> 2.56 us  [passed_on(): return jnp.where(inner, value, lax.ppermute(value, 'zlo', OUTWARD))]
    ppermute x25, waiting for transfers between devices: 23.4 us -> 28.6 us  [shift(): return lax.ppermute(value, axis, [(i, (i + step) % n) for i in range(n)])]
    all_to_all x0 -> x1, starting transfers between devices: none -> 3.48 us  [per_device(): by_y = lax.all_to_all(picked, 'y', 0, 0, tiled=True)]
    ppermute x1, waiting for transfers between devices: 0.01 us -> 1.95 us  [per_device(): near = lax.ppermute(own, 'zlo', PAIRS)]
    unnamed x24 -> x32, local copies, waits for them, and re-layouts: 6.45 us -> 5.88 us
  transfers between devices with their start and end apart: 31 -> 32, of which waited for: 8 -> 11; matrix products, arithmetic and copies ran while one was open for 4% -> 3% of each run, Pallas kernels for 15% -> 15%
where the time goes in v4:
time: 164 us
  waiting for transfers between devices  61.6 us (38%)
  starting transfers between devices  59.7 us (36%)
  Pallas kernels  28.7 us (18%)
  local copies, waits for them, and re-layouts  9.55 us (6%)
  other arithmetic  3.88 us (2%)
    ppermute x25, starting transfers between devices, shift(): return lax.ppermute(value, axis, [(i, (i + step) % n) for i in range(n)])  39.1 us
    ppermute x25, waiting for transfers between devices, shift(): return lax.ppermute(value, axis, [(i, (i + step) % n) for i in range(n)])  28.6 us
    pallas_call x3, Pallas kernels, gram(): pl.pallas_call(functools.partial(gram_kernel, slots, rows, pieces, len(ar...  19 us
    all_to_all x1, waiting for transfers between devices, per_device(): by_y = lax.all_to_all(picked, 'y', 0, 0, tiled=True)  17.5 us
    all_to_all x1, waiting for transfers between devices, per_device(): lax.all_to_all(jnp.concatenate([cols, cols]), ('zhi', 'zlo'), 0, 0, tiled...  11.1 us
    pallas_call x1, Pallas kernels, gather_points(): pl.pallas_call(gather_kernel, grid=(steps,), in_specs=[pl.BlockSpec((NPTS...  8.97 us
    all_to_all x1, starting transfers between devices, per_device(): lax.all_to_all(jnp.concatenate([cols, cols]), ('zhi', 'zlo'), 0, 0, tiled...  8.71 us
    unnamed x32, local copies, waits for them, and re-layouts  5.88 us
  transfers between devices with their start and end apart: 32, of which 11 were waited for; matrix products, arithmetic and copies ran while one was open for 3% of the time, Pallas kernels for 15%

profile of v4, /device:TPU:1, one launch (start us, length us, event | category | flops | bytes accessed | tf_op | source)
XLA Modules:
  0.0 163.8 jit_solution(9196835740566732845)
XLA Ops:
  0.0 1.2 pad_maximum_fusion.1.refs_0_
  1.2 2.6 %collective-permute-start = (bf16[2,192,1024]{2,1,0:T(8,128)(2,1)S(1)}, bf16[2,192,1024]{2,1,0:T(8,128)(2,1)S(1)}, u32[]{:S(2)}, u32[]{:S(2)}) collective-permute-start(bf16[2,192,1024]{2,1,0:T(8,128)(2,1)S(1)} %pad_maximum_fusion.1.refs_0_), channel_id=1, source_target_pairs={{0,4},{4,0},{8,12},{12,8},{1,5},{5,1},{9,13},{13,9},{2,6},{6,2},{1... | collective-permute-start | bytes 2359304 | tf_op jit(solution)/shard_map/ppermute | solution.py:200
  3.8 1.5 collective-permute-start.1
  5.3 1.3 collective-permute-start.2
  6.6 1.4 collective-permute-start.3
  8.1 0.9 reshape.16.points_ref
  9.1 9.0 %gather_points.1 = bf16[768,384]{1,0:T(8,128)(2,1)} custom-call(s32[768,1]{1,0:T(8,128)} %reshape.16.points_ref, bf16[192,6144]{1,0:T(8,128)(2,1)} %psi_ref.1, bf16[192,6144]{1,0:T(8,128)(2,1)} %phi_ref.1), custom_call_target="tpu_custom_call" | custom-call | flops 3623878656 | bytes 4718592 | tf_op jit(solution)/shard_map/gather_points/pallas_call | solution.py:69
  18.0 1.9 %collective-permute-done.refs_5_ = bf16[2,192,1024]{2,1,0:T(8,128)(2,1)S(1)} collective-permute-done((bf16[2,192,1024]{2,1,0:T(8,128)(2,1)S(1)}, bf16[2,192,1024]{2,1,0:T(8,128)(2,1)S(1)}, u32[]{:S(2)}, u32[]{:S(2)}) %collective-permute-start) | collective-permute-done | bytes 786464 | tf_op jit(solution)/shard_map/ppermute | solution.py:200
  20.0 4.8 %collective-permute-done.2.refs_3_ = bf16[2,192,1024]{2,1,0:T(8,128)(2,1)S(1)} collective-permute-done((bf16[2,192,1024]{2,1,0:T(8,128)(2,1)S(1)}, bf16[2,192,1024]{2,1,0:T(8,128)(2,1)S(1)}, u32[]{:S(2)}, u32[]{:S(2)}) %collective-permute-start.2) | collective-permute-done | bytes 786464 | tf_op jit(solution)/shard_map/ppermute | solution.py:34
  24.7 0.9 copy-done
  25.6 1.3 collective-permute-start.4
  26.9 1.0 collective-permute-start.6
  28.0 1.7 %collective-permute-start.7 = (bf16[2,192,1024]{2,1,0:T(8,128)(2,1)}, bf16[2,192,1024]{2,1,0:T(8,128)(2,1)}, u32[]{:S(2)}, u32[]{:S(2)}) collective-permute-start(bf16[2,192,1024]{2,1,0:T(8,128)(2,1)} %copy-done.5), channel_id=1, source_target_pairs={{0,3},{1,0},{2,1},{3,2},{4,7},{5,4},{6,5},{7,6},{8,11},{9,8},{10,9... | collective-permute-start | bytes 2359304 | tf_op jit(solution)/shard_map/ppermute | solution.py:34
  29.7 1.5 collective-permute-start.5
  31.2 3.5 %all-to-all-start = ((bf16[4,4,48,384]{3,2,1,0:T(8,128)(2,1)}), bf16[4,4,48,384]{3,2,1,0:T(8,128)(2,1)S(1)}, u32[]{:S(2)}, u32[]{:S(2)}) async-start(bf16[4,4,48,384]{3,2,1,0:T(8,128)(2,1)} %bitcast.31), calls=%async_computation | async-start | bytes 1179648 | tf_op jit(solution)/shard_map/all_to_all | solution.py:206
  34.8 17.5 %all-to-all-done.in_ref = bf16[4,4,48,384]{3,2,1,0:T(8,128)(2,1)S(1)} async-done(((bf16[4,4,48,384]{3,2,1,0:T(8,128)(2,1)}), bf16[4,4,48,384]{3,2,1,0:T(8,128)(2,1)S(1)}, u32[]{:S(2)}, u32[]{:S(2)}) %all-to-all-start) | async-done | bytes 589856 | tf_op jit(solution)/shard_map/all_to_all | solution.py:206
  53.0 1.2 broadcast_select_fusion.1.refs_10_
  54.3 1.2 pad_maximum_fusion
  55.5 8.7 %all-to-all-start.1 = ((bf16[8,2,48,768]{3,2,1,0:T(8,128)(2,1)}), bf16[8,2,48,768]{3,2,1,0:T(8,128)(2,1)S(1)}, u32[]{:S(2)}, u32[]{:S(2)}) async-start(bf16[8,2,48,768]{3,2,1,0:T(8,128)(2,1)} %pad_maximum_fusion), calls=%async_computation.1 | async-start | bytes 2359296 | tf_op jit(solution)/shard_map/all_to_all | solution.py:213
  64.9 1.0 slice_bitcast_fusion.8
  66.0 2.2 %collective-permute-start.9 = (bf16[192,1024]{1,0:T(8,128)(2,1)S(1)}, bf16[192,1024]{1,0:T(8,128)(2,1)S(1)}, u32[]{:S(2)}, u32[]{:S(2)}) collective-permute-start(bf16[192,1024]{1,0:T(8,128)(2,1)S(1)} %slice_bitcast_fusion.8), channel_id=1, source_target_pairs={{0,3},{1,0},{2,1},{3,2},{4,7},{5,4},{6,5},{7,6},{8,11},{9,8},{10,9... | collective-permute-start | bytes 1179656 | tf_op jit(solution)/shard_map/ppermute | solution.py:34
  68.3 1.0 slice_bitcast_fusion.4
  69.3 2.7 %collective-permute-start.11 = (bf16[192,1024]{1,0:T(8,128)(2,1)S(1)}, bf16[192,1024]{1,0:T(8,128)(2,1)S(1)}, u32[]{:S(2)}, u32[]{:S(2)}) collective-permute-start(bf16[192,1024]{1,0:T(8,128)(2,1)S(1)} %slice_bitcast_fusion.4), channel_id=1, source_target_pairs={{0,3},{1,0},{2,1},{3,2},{4,7},{5,4},{6,5},{7,6},{8,11},{9,8},{10,9... | collective-permute-start | bytes 1179656 | tf_op jit(solution)/shard_map/ppermute | solution.py:34
  73.0 0.8 copy-done.9
  73.7 7.0 %collective-permute-done.10.refs_7_ = bf16[192,1024]{1,0:T(8,128)(2,1)S(1)} collective-permute-done((bf16[192,1024]{1,0:T(8,128)(2,1)S(1)}, bf16[192,1024]{1,0:T(8,128)(2,1)S(1)}, u32[]{:S(2)}, u32[]{:S(2)}) %collective-permute-start.10) | collective-permute-done | bytes 393248 | tf_op jit(solution)/shard_map/ppermute | solution.py:34
  80.7 0.8 copy-done.11
  82.3 11.1 %all-to-all-done.1.refs_15_.refs_5_ = bf16[8,2,48,768]{3,2,1,0:T(8,128)(2,1)S(1)} async-done(((bf16[8,2,48,768]{3,2,1,0:T(8,128)(2,1)}), bf16[8,2,48,768]{3,2,1,0:T(8,128)(2,1)S(1)}, u32[]{:S(2)}, u32[]{:S(2)}) %all-to-all-start.1) | async-done | bytes 1179680 | tf_op jit(solution)/shard_map/all_to_all | solution.py:213
  93.5 2.6 %collective-permute-start.17 = (bf16[2,192,1024]{2,1,0:T(8,128)(2,1)S(1)}, bf16[2,192,1024]{2,1,0:T(8,128)(2,1)S(1)}, u32[]{:S(2)}, u32[]{:S(2)}) collective-permute-start(bf16[2,192,1024]{2,1,0:T(8,128)(2,1)S(1)} %broadcast_select_fusion.1.refs_10_), channel_id=1, source_target_pairs={{0,3},{1,0},{2,1},{3,2},{4,7},{5,4},{6,5},{7,6},{8,11},{9,8},{10,9... | collective-permute-start | bytes 2359304 | tf_op jit(solution)/shard_map/ppermute | solution.py:34
  96.1 1.3 collective-permute-start.12
  97.4 1.5 collective-permute-start.13
  98.9 1.5 collective-permute-start.14
  100.3 9.8 %collective-permute-done.15.refs_13_ = bf16[2,192,1024]{2,1,0:T(8,128)(2,1)S(1)} collective-permute-done((bf16[2,192,1024]{2,1,0:T(8,128)(2,1)S(1)}, bf16[2,192,1024]{2,1,0:T(8,128)(2,1)S(1)}, u32[]{:S(2)}, u32[]{:S(2)}) %collective-permute-start.15) | collective-permute-done | bytes 786464 | tf_op jit(solution)/shard_map/ppermute | solution.py:34
  110.3 2.7 %collective-permute-start.18 = (bf16[192,1024]{1,0:T(8,128)(2,1)S(1)}, bf16[192,1024]{1,0:T(8,128)(2,1)S(1)}, u32[]{:S(2)}, u32[]{:S(2)}) collective-permute-start(bf16[192,1024]{1,0:T(8,128)(2,1)S(1)} %slice_bitcast_fusion.2), channel_id=1, source_target_pairs={{0,3},{1,0},{2,1},{3,2},{4,7},{5,4},{6,5},{7,6},{8,11},{9,8},{10,9... | collective-permute-start | bytes 1179656 | tf_op jit(solution)/shard_map/ppermute | solution.py:34
  113.0 2.6 %collective-permute-done.14 = bf16[2,192,1024]{2,1,0:T(8,128)(2,1)S(1)} collective-permute-done((bf16[2,192,1024]{2,1,0:T(8,128)(2,1)}, bf16[2,192,1024]{2,1,0:T(8,128)(2,1)S(1)}, u32[]{:S(2)}, u32[]{:S(2)}) %collective-permute-start.14) | collective-permute-done | bytes 786464 | tf_op jit(solution)/shard_map/ppermute | solution.py:197
  115.7 5.6 %collective-permute-start.21 = (bf16[8,2,48,768]{3,2,1,0:T(8,128)(2,1)S(1)}, bf16[8,2,48,768]{3,2,1,0:T(8,128)(2,1)S(1)}, u32[]{:S(2)}, u32[]{:S(2)}) collective-permute-start(bf16[8,2,48,768]{3,2,1,0:T(8,128)(2,1)S(1)} %all-to-all-done.1.refs_15_.refs_5_), channel_id=1, source_target_pairs={{0,16},{16,0},{1,17},{17,1},{2,18},{18,2},{3,19},{19,3},{4,20},{20... | collective-permute-start | bytes 3538952 | tf_op jit(solution)/shard_map/ppermute | solution.py:34
  121.3 4.5 %collective-permute-start.22 = (bf16[8,2,48,768]{3,2,0,1:T(8,128)(2,1)S(1)}, bf16[8,2,48,768]{3,2,0,1:T(8,128)(2,1)S(1)}, u32[]{:S(2)}, u32[]{:S(2)}) collective-permute-start(bf16[8,2,48,768]{3,2,0,1:T(8,128)(2,1)S(1)} %collective-permute-done.12), channel_id=1, source_target_pairs={{0,16},{16,0},{1,17},{17,1},{2,18},{18,2},{3,19},{19,3},{4,20},{20... | collective-permute-start | bytes 3538952 | tf_op jit(solution)/shard_map/ppermute | solution.py:34
  126.0 2.7 %collective-permute-start.20 = (bf16[2,192,1024]{2,1,0:T(8,128)(2,1)S(1)}, bf16[2,192,1024]{2,1,0:T(8,128)(2,1)S(1)}, u32[]{:S(2)}, u32[]{:S(2)}) collective-permute-start(bf16[2,192,1024]{2,1,0:T(8,128)(2,1)S(1)} %broadcast_select_fusion.refs_0_), channel_id=1, source_target_pairs={{0,3},{1,0},{2,1},{3,2},{4,7},{5,4},{6,5},{7,6},{8,11},{9,8},{10,9... | collective-permute-start | bytes 2359304 | tf_op jit(solution)/shard_map/ppermute | solution.py:34
  128.8 1.3 collective-permute-done.23
  130.0 1.1 collective-permute-start.26
  131.2 1.6 collective-permute-start.27
  133.1 0.8 copy-done.8
  135.0 8.8 %gram_near.1.refs_15_ = f32[2,576,1024]{2,1,0:T(8,128)S(1)} custom-call(s32[4]{0:T(128)S(1)} %pad_add_fusion.pos_ref, bf16[2,192,1024]{2,1,0:T(8,128)(2,1)S(1)} %pad_maximum_fusion.1.refs_0_, bf16[2,192,1024]{2,1,0:T(8,128)(2,1)S(1)} %copy-done.1, bf16[192,1024]{1,0:T(8,128)(2,1)S(1)} %copy-done.8, bf16[2,192,1024]{2,1,0:T(8,128)(2,1)S(1)} %collective-permute-done.2.refs_3_, ...), custom_call_target="tpu_custom_call" | custom-call | flops 5435817984 | bytes 8388608 | tf_op jit(solution)/shard_map/gram_near/pallas_call | solution.py:172
  143.8 2.0 %collective-permute-done.19.refs_3_ = bf16[2,192,1024]{2,1,0:T(8,128)(2,1)S(1)} collective-permute-done((bf16[2,192,1024]{2,1,0:T(8,128)(2,1)S(1)}, bf16[2,192,1024]{2,1,0:T(8,128)(2,1)S(1)}, u32[]{:S(2)}, u32[]{:S(2)}) %collective-permute-start.19) | collective-permute-done | bytes 786464 | tf_op jit(solution)/shard_map/ppermute | solution.py:34
  145.9 1.2 collective-permute-start.28
  147.4 2.7 %collective-permute-start.25 = (bf16[192,1024]{1,0:T(8,128)(2,1)S(1)}, bf16[192,1024]{1,0:T(8,128)(2,1)S(1)}, u32[]{:S(2)}, u32[]{:S(2)}) collective-permute-start(bf16[192,1024]{1,0:T(8,128)(2,1)S(1)} %slice_bitcast_fusion.6), channel_id=1, source_target_pairs={{0,3},{1,0},{2,1},{3,2},{4,7},{5,4},{6,5},{7,6},{8,11},{9,8},{10,9... | collective-permute-start | bytes 1179656 | tf_op jit(solution)/shard_map/ppermute | solution.py:34
  150.2 5.3 %gram_far.1.refs_16_ = f32[2,192,1024]{2,1,0:T(8,128)S(1)} custom-call(s32[4]{0:T(128)S(1)} %pad_add_fusion.pos_ref, bf16[2,192,1024]{2,1,0:T(8,128)(2,1)S(1)} %pad_maximum_fusion.1.refs_0_, bf16[2,192,1024]{2,1,0:T(8,128)(2,1)S(1)} %copy-done.1, bf16[192,1024]{1,0:T(8,128)(2,1)S(1)} %copy-done.8, bf16[2,192,1024]{2,1,0:T(8,128)(2,1)S(1)} %collective-permute-done.2.refs_3_, ...), custom_call_target="tpu_custom_call" | custom-call | flops 1811939328 | bytes 8388608 | tf_op jit(solution)/shard_map/gram_far/pallas_call | solution.py:172
  155.4 3.4 %collective-permute-done.24.refs_2_ = bf16[192,1024]{1,0:T(8,128)(2,1)S(1)} collective-permute-done((bf16[192,1024]{1,0:T(8,128)(2,1)S(1)}, bf16[192,1024]{1,0:T(8,128)(2,1)S(1)}, u32[]{:S(2)}, u32[]{:S(2)}) %collective-permute-start.24) | collective-permute-done | bytes 393248 | tf_op jit(solution)/shard_map/ppermute | solution.py:34
  158.9 4.9 %gram_last.1 = bf16[2,4,2,48,1024]{4,3,2,1,0:T(8,128)(2,1)} custom-call(s32[4]{0:T(128)S(1)} %pad_add_fusion.pos_ref, bf16[2,192,1024]{2,1,0:T(8,128)(2,1)S(1)} %broadcast_select_fusion.refs_0_, bf16[2,192,1024]{2,1,0:T(8,128)(2,1)S(1)} %collective-permute-done.20.refs_1_, bf16[192,1024]{1,0:T(8,128)(2,1)S(1)} %collective-permute-done.24.refs_2_, ...), custom_call_target="tpu_custom_call" | custom-call | flops 2415919104 | bytes 8388608 | tf_op jit(solution)/shard_map/gram_last/pallas_call | solution.py:172
  (75 shorter events, 5.8 us)
Async XLA Ops:
  0.0 8.0 %copy-start.15 = (s32[768]{0:T(1024)S(1)}, s32[768]{0:T(1024)}, u32[]{:S(2)}) copy-start(s32[768]{0:T(1024)} %param.9) | copy-start | bytes 9220
  1.2 18.8 %collective-permute-start = (bf16[2,192,1024]{2,1,0:T(8,128)(2,1)S(1)}, bf16[2,192,1024]{2,1,0:T(8,128)(2,1)S(1)}, u32[]{:S(2)}, u32[]{:S(2)}) collective-permute-start(bf16[2,192,1024]{2,1,0:T(8,128)(2,1)S(1)} %pad_maximum_fusion.1.refs_0_), channel_id=1, source_target_pairs={{0,4},{4,0},{8,12},{12,8},{1,5},{5,1},{9,13},{13,9},{2,6},{6,2},{1... | collective-permute-start | bytes 2359304 | tf_op jit(solution)/shard_map/ppermute | solution.py:200
  3.8 16.2 %collective-permute-start.1 = (bf16[2,192,1024]{2,1,0:T(8,128)(2,1)S(1)}, bf16[2,192,1024]{2,1,0:T(8,128)(2,1)}, u32[]{:S(2)}, u32[]{:S(2)}) collective-permute-start(bf16[2,192,1024]{2,1,0:T(8,128)(2,1)S(1)} %pad_maximum_fusion.1.refs_0_), channel_id=1, source_target_pairs={{4,8},{8,4},{5,9},{9,5},{6,10},{10,6},{7,11},{11,7},{20,24},{24,20... | collective-permute-start | bytes 2359304 | tf_op jit(solution)/shard_map/ppermute | solution.py:201
  5.3 19.4 %collective-permute-start.2 = (bf16[2,192,1024]{2,1,0:T(8,128)(2,1)S(1)}, bf16[2,192,1024]{2,1,0:T(8,128)(2,1)S(1)}, u32[]{:S(2)}, u32[]{:S(2)}) collective-permute-start(bf16[2,192,1024]{2,1,0:T(8,128)(2,1)S(1)} %pad_maximum_fusion.1.refs_0_), channel_id=1, source_target_pairs={{0,1},{1,2},{2,3},{3,0},{4,5},{5,6},{6,7},{7,4},{8,9},{9,10},{10,1... | collective-permute-start | bytes 2359304 | tf_op jit(solution)/shard_map/ppermute | solution.py:34
  6.6 18.1 %collective-permute-start.3 = (bf16[2,192,1024]{2,1,0:T(8,128)(2,1)S(1)}, bf16[2,192,1024]{2,1,0:T(8,128)(2,1)S(1)}, u32[]{:S(2)}, u32[]{:S(2)}) collective-permute-start(bf16[2,192,1024]{2,1,0:T(8,128)(2,1)S(1)} %pad_maximum_fusion.1.refs_0_), channel_id=1, source_target_pairs={{0,3},{1,0},{2,1},{3,2},{4,7},{5,4},{6,5},{7,6},{8,11},{9,8},{10,9... | collective-permute-start | bytes 2359304 | tf_op jit(solution)/shard_map/ppermute | solution.py:34
  20.0 5.7 %copy-start.5 = (bf16[2,192,1024]{2,1,0:T(8,128)(2,1)}, bf16[2,192,1024]{2,1,0:T(8,128)(2,1)S(1)}, u32[]{:S(2)}) copy-start(bf16[2,192,1024]{2,1,0:T(8,128)(2,1)S(1)} %collective-permute-done.refs_5_) | copy-start | bytes 2359300
  24.7 0.9 copy-start
  25.6 27.4 %collective-permute-start.4 = (bf16[2,192,1024]{2,1,0:T(8,128)(2,1)}, bf16[2,192,1024]{2,1,0:T(8,128)(2,1)}, u32[]{:S(2)}, u32[]{:S(2)}) collective-permute-start(bf16[2,192,1024]{2,1,0:T(8,128)(2,1)} %collective-permute-done.1), channel_id=1, source_target_pairs={{4,0},{8,12},{5,1},{9,13},{6,2},{10,14},{7,3},{11,15},{20,16},{24,... | collective-permute-start | bytes 2359304 | tf_op jit(solution)/shard_map/ppermute | solution.py:197
  26.9 27.3 %collective-permute-start.6 = (bf16[2,192,1024]{2,1,0:T(8,128)(2,1)}, bf16[2,192,1024]{2,1,0:T(8,128)(2,1)S(1)}, u32[]{:S(2)}, u32[]{:S(2)}) collective-permute-start(bf16[2,192,1024]{2,1,0:T(8,128)(2,1)} %copy-done.5), channel_id=1, source_target_pairs={{0,1},{1,2},{2,3},{3,0},{4,5},{5,6},{6,7},{7,4},{8,9},{9,10},{10,1... | collective-permute-start | bytes 2359304 | tf_op jit(solution)/shard_map/ppermute | solution.py:34
  28.0 26.3 %collective-permute-start.7 = (bf16[2,192,1024]{2,1,0:T(8,128)(2,1)}, bf16[2,192,1024]{2,1,0:T(8,128)(2,1)}, u32[]{:S(2)}, u32[]{:S(2)}) collective-permute-start(bf16[2,192,1024]{2,1,0:T(8,128)(2,1)} %copy-done.5), channel_id=1, source_target_pairs={{0,3},{1,0},{2,1},{3,2},{4,7},{5,4},{6,5},{7,6},{8,11},{9,8},{10,9... | collective-permute-start | bytes 2359304 | tf_op jit(solution)/shard_map/ppermute | solution.py:34
  29.7 24.6 %collective-permute-start.5 = (bf16[2,192,1024]{2,1,0:T(8,128)(2,1)}, bf16[2,192,1024]{2,1,0:T(8,128)(2,1)}, u32[]{:S(2)}, u32[]{:S(2)}) collective-permute-start(bf16[2,192,1024]{2,1,0:T(8,128)(2,1)} %copy-done.5), channel_id=1, source_target_pairs={{4,8},{8,4},{5,9},{9,5},{6,10},{10,6},{7,11},{11,7},{20,24},{24,20... | collective-permute-start | bytes 2359304 | tf_op jit(solution)/shard_map/ppermute | solution.py:209
  31.2 21.1 %all-to-all-start = ((bf16[4,4,48,384]{3,2,1,0:T(8,128)(2,1)}), bf16[4,4,48,384]{3,2,1,0:T(8,128)(2,1)S(1)}, u32[]{:S(2)}, u32[]{:S(2)}) async-start(bf16[4,4,48,384]{3,2,1,0:T(8,128)(2,1)} %bitcast.31), calls=%async_computation | async-start | bytes 1179648 | tf_op jit(solution)/shard_map/all_to_all | solution.py:206
  54.2 1.3 copy-start.2
  55.5 37.8 %all-to-all-start.1 = ((bf16[8,2,48,768]{3,2,1,0:T(8,128)(2,1)}), bf16[8,2,48,768]{3,2,1,0:T(8,128)(2,1)S(1)}, u32[]{:S(2)}, u32[]{:S(2)}) async-start(bf16[8,2,48,768]{3,2,1,0:T(8,128)(2,1)} %pad_maximum_fusion), calls=%async_computation.1 | async-start | bytes 2359296 | tf_op jit(solution)/shard_map/all_to_all | solution.py:213
  64.2 3.9 %copy-start.3 = (bf16[2,192,1024]{2,1,0:T(8,128)(2,1)S(1)}, bf16[2,192,1024]{2,1,0:T(8,128)(2,1)}, u32[]{:S(2)}) copy-start(bf16[2,192,1024]{2,1,0:T(8,128)(2,1)} %copy-done.2) | copy-start | bytes 2359300
  64.3 7.9 %collective-permute-start.8 = (bf16[192,1024]{1,0:T(8,128)(2,1)S(1)}, bf16[192,1024]{1,0:T(8,128)(2,1)S(1)}, u32[]{:S(2)}, u32[]{:S(2)}) collective-permute-start(bf16[192,1024]{1,0:T(8,128)(2,1)S(1)} %slice_bitcast_fusion.9), channel_id=1, source_target_pairs={{0,1},{1,2},{2,3},{3,0},{4,5},{5,6},{6,7},{7,4},{8,9},{9,10},{10,1... | collective-permute-start | bytes 1179656 | tf_op jit(solution)/shard_map/ppermute | solution.py:34
  66.0 7.0 %collective-permute-start.9 = (bf16[192,1024]{1,0:T(8,128)(2,1)S(1)}, bf16[192,1024]{1,0:T(8,128)(2,1)S(1)}, u32[]{:S(2)}, u32[]{:S(2)}) collective-permute-start(bf16[192,1024]{1,0:T(8,128)(2,1)S(1)} %slice_bitcast_fusion.8), channel_id=1, source_target_pairs={{0,3},{1,0},{2,1},{3,2},{4,7},{5,4},{6,5},{7,6},{8,11},{9,8},{10,9... | collective-permute-start | bytes 1179656 | tf_op jit(solution)/shard_map/ppermute | solution.py:34
  68.2 12.6 %collective-permute-start.10 = (bf16[192,1024]{1,0:T(8,128)(2,1)S(1)}, bf16[192,1024]{1,0:T(8,128)(2,1)S(1)}, u32[]{:S(2)}, u32[]{:S(2)}) collective-permute-start(bf16[192,1024]{1,0:T(8,128)(2,1)S(1)} %slice_bitcast_fusion.5), channel_id=1, source_target_pairs={{0,1},{1,2},{2,3},{3,0},{4,5},{5,6},{6,7},{7,4},{8,9},{9,10},{10,1... | collective-permute-start | bytes 1179656 | tf_op jit(solution)/shard_map/ppermute | solution.py:34
  69.3 12.2 %collective-permute-start.11 = (bf16[192,1024]{1,0:T(8,128)(2,1)S(1)}, bf16[192,1024]{1,0:T(8,128)(2,1)S(1)}, u32[]{:S(2)}, u32[]{:S(2)}) collective-permute-start(bf16[192,1024]{1,0:T(8,128)(2,1)S(1)} %slice_bitcast_fusion.4), channel_id=1, source_target_pairs={{0,3},{1,0},{2,1},{3,2},{4,7},{5,4},{6,5},{7,6},{8,11},{9,8},{10,9... | collective-permute-start | bytes 1179656 | tf_op jit(solution)/shard_map/ppermute | solution.py:34
  72.2 0.8 copy-start.7
  73.0 0.8 copy-start.9
  80.7 0.8 copy-start.11
  81.5 0.8 copy-start.13
  93.3 16.8 %collective-permute-start.15 = (bf16[2,192,1024]{2,1,0:T(8,128)(2,1)S(1)}, bf16[2,192,1024]{2,1,0:T(8,128)(2,1)S(1)}, u32[]{:S(2)}, u32[]{:S(2)}) collective-permute-start(bf16[2,192,1024]{2,1,0:T(8,128)(2,1)S(1)} %broadcast_select_fusion.1.refs_10_), channel_id=1, source_target_pairs={{0,1},{1,2},{2,3},{3,0},{4,5},{5,6},{6,7},{7,4},{8,9},{9,10},{10,1... | collective-permute-start | bytes 2359304 | tf_op jit(solution)/shard_map/ppermute | solution.py:34
  93.5 16.8 %collective-permute-start.17 = (bf16[2,192,1024]{2,1,0:T(8,128)(2,1)S(1)}, bf16[2,192,1024]{2,1,0:T(8,128)(2,1)S(1)}, u32[]{:S(2)}, u32[]{:S(2)}) collective-permute-start(bf16[2,192,1024]{2,1,0:T(8,128)(2,1)S(1)} %broadcast_select_fusion.1.refs_10_), channel_id=1, source_target_pairs={{0,3},{1,0},{2,1},{3,2},{4,7},{5,4},{6,5},{7,6},{8,11},{9,8},{10,9... | collective-permute-start | bytes 2359304 | tf_op jit(solution)/shard_map/ppermute | solution.py:34
  96.1 25.2 %collective-permute-start.12 = (bf16[8,2,48,768]{3,2,0,1:T(8,128)(2,1)S(1)}, bf16[8,2,48,768]{3,2,0,1:T(8,128)(2,1)S(1)}, u32[]{:S(2)}, u32[]{:S(2)}) collective-permute-start(bf16[8,2,48,768]{3,2,0,1:T(8,128)(2,1)S(1)} %copy.38), channel_id=1, source_target_pairs={{0,32},{32,64},{64,96},{96,0},{1,33},{33,65},{65,97},{97,1},{2,34}... | collective-permute-start | bytes 3538952 | tf_op jit(solution)/shard_map/ppermute | solution.py:34
  97.4 23.9 %collective-permute-start.13 = (bf16[8,2,48,768]{3,2,0,1:T(8,128)(2,1)S(1)}, bf16[8,2,48,768]{3,2,0,1:T(8,128)(2,1)S(1)}, u32[]{:S(2)}, u32[]{:S(2)}) collective-permute-start(bf16[8,2,48,768]{3,2,0,1:T(8,128)(2,1)S(1)} %copy.38), channel_id=1, source_target_pairs={{0,96},{32,0},{64,32},{96,64},{1,97},{33,1},{65,33},{97,65},{2,98}... | collective-permute-start | bytes 3538952 | tf_op jit(solution)/shard_map/ppermute | solution.py:34
  98.9 16.7 %collective-permute-start.14 = (bf16[2,192,1024]{2,1,0:T(8,128)(2,1)}, bf16[2,192,1024]{2,1,0:T(8,128)(2,1)S(1)}, u32[]{:S(2)}, u32[]{:S(2)}) collective-permute-start(bf16[2,192,1024]{2,1,0:T(8,128)(2,1)} %collective-permute-done.5), channel_id=1, source_target_pairs={{4,0},{8,12},{5,1},{9,13},{6,2},{10,14},{7,3},{11,15},{20,16},{24,... | collective-permute-start | bytes 2359304 | tf_op jit(solution)/shard_map/ppermute | solution.py:197
  110.2 11.1 %collective-permute-start.16 = (bf16[192,1024]{1,0:T(8,128)(2,1)S(1)}, bf16[192,1024]{1,0:T(8,128)(2,1)S(1)}, u32[]{:S(2)}, u32[]{:S(2)}) collective-permute-start(bf16[192,1024]{1,0:T(8,128)(2,1)S(1)} %slice_bitcast_fusion.3), channel_id=1, source_target_pairs={{0,1},{1,2},{2,3},{3,0},{4,5},{5,6},{6,7},{7,4},{8,9},{9,10},{10,1... | collective-permute-start | bytes 1179656 | tf_op jit(solution)/shard_map/ppermute | solution.py:34
  110.3 11.0 %collective-permute-start.18 = (bf16[192,1024]{1,0:T(8,128)(2,1)S(1)}, bf16[192,1024]{1,0:T(8,128)(2,1)S(1)}, u32[]{:S(2)}, u32[]{:S(2)}) collective-permute-start(bf16[192,1024]{1,0:T(8,128)(2,1)S(1)} %slice_bitcast_fusion.2), channel_id=1, source_target_pairs={{0,3},{1,0},{2,1},{3,2},{4,7},{5,4},{6,5},{7,6},{8,11},{9,8},{10,9... | collective-permute-start | bytes 1179656 | tf_op jit(solution)/shard_map/ppermute | solution.py:34
  115.7 13.0 %collective-permute-start.21 = (bf16[8,2,48,768]{3,2,1,0:T(8,128)(2,1)S(1)}, bf16[8,2,48,768]{3,2,1,0:T(8,128)(2,1)S(1)}, u32[]{:S(2)}, u32[]{:S(2)}) collective-permute-start(bf16[8,2,48,768]{3,2,1,0:T(8,128)(2,1)S(1)} %all-to-all-done.1.refs_15_.refs_5_), channel_id=1, source_target_pairs={{0,16},{16,0},{1,17},{17,1},{2,18},{18,2},{3,19},{19,3},{4,20},{20... | collective-permute-start | bytes 3538952 | tf_op jit(solution)/shard_map/ppermute | solution.py:34
  121.3 7.4 %collective-permute-start.22 = (bf16[8,2,48,768]{3,2,0,1:T(8,128)(2,1)S(1)}, bf16[8,2,48,768]{3,2,0,1:T(8,128)(2,1)S(1)}, u32[]{:S(2)}, u32[]{:S(2)}) collective-permute-start(bf16[8,2,48,768]{3,2,0,1:T(8,128)(2,1)S(1)} %collective-permute-done.12), channel_id=1, source_target_pairs={{0,16},{16,0},{1,17},{17,1},{2,18},{18,2},{3,19},{19,3},{4,20},{20... | collective-permute-start | bytes 3538952 | tf_op jit(solution)/shard_map/ppermute | solution.py:34
  125.9 4.2 %collective-permute-start.23 = (bf16[8,2,48,768]{3,2,0,1:T(8,128)(2,1)S(1)}, bf16[8,2,48,768]{3,2,0,1:T(8,128)(2,1)S(1)}, u32[]{:S(2)}, u32[]{:S(2)}) collective-permute-start(bf16[8,2,48,768]{3,2,0,1:T(8,128)(2,1)S(1)} %collective-permute-done.13), channel_id=1, source_target_pairs={{0,16},{16,0},{1,17},{17,1},{2,18},{18,2},{3,19},{19,3},{4,20},{20... | collective-permute-start | bytes 3538952 | tf_op jit(solution)/shard_map/ppermute | solution.py:34
  126.0 19.9 %collective-permute-start.19 = (bf16[2,192,1024]{2,1,0:T(8,128)(2,1)S(1)}, bf16[2,192,1024]{2,1,0:T(8,128)(2,1)S(1)}, u32[]{:S(2)}, u32[]{:S(2)}) collective-permute-start(bf16[2,192,1024]{2,1,0:T(8,128)(2,1)S(1)} %broadcast_select_fusion.refs_0_), channel_id=1, source_target_pairs={{0,1},{1,2},{2,3},{3,0},{4,5},{5,6},{6,7},{7,4},{8,9},{9,10},{10,1... | collective-permute-start | bytes 2359304 | tf_op jit(solution)/shard_map/ppermute | solution.py:34
  126.0 19.9 %collective-permute-start.20 = (bf16[2,192,1024]{2,1,0:T(8,128)(2,1)S(1)}, bf16[2,192,1024]{2,1,0:T(8,128)(2,1)S(1)}, u32[]{:S(2)}, u32[]{:S(2)}) collective-permute-start(bf16[2,192,1024]{2,1,0:T(8,128)(2,1)S(1)} %broadcast_select_fusion.refs_0_), channel_id=1, source_target_pairs={{0,3},{1,0},{2,1},{3,2},{4,7},{5,4},{6,5},{7,6},{8,11},{9,8},{10,9... | collective-permute-start | bytes 2359304 | tf_op jit(solution)/shard_map/ppermute | solution.py:34
  130.0 15.9 %collective-permute-start.26 = (bf16[8,48,768]{2,1,0:T(8,128)(2,1)S(1)}, bf16[8,48,768]{2,1,0:T(8,128)(2,1)S(1)}, u32[]{:S(2)}, u32[]{:S(2)}) collective-permute-start(bf16[8,48,768]{2,1,0:T(8,128)(2,1)S(1)} %get-tuple-element.46), channel_id=1, source_target_pairs={{0,32},{32,64},{64,96},{96,0},{1,33},{33,65},{65,97},{97,1},{2,34}... | collective-permute-start | bytes 1769480 | tf_op jit(solution)/shard_map/ppermute | solution.py:34
  131.2 16.0 %collective-permute-start.27 = (bf16[8,48,768]{2,1,0:T(8,128)(2,1)S(1)}, bf16[8,48,768]{2,1,0:T(8,128)(2,1)S(1)}, u32[]{:S(2)}, u32[]{:S(2)}) collective-permute-start(bf16[8,48,768]{2,1,0:T(8,128)(2,1)S(1)} %get-tuple-element.47), channel_id=1, source_target_pairs={{0,96},{32,0},{64,32},{96,64},{1,97},{33,1},{65,33},{97,65},{2,98}... | collective-permute-start | bytes 1769480 | tf_op jit(solution)/shard_map/ppermute | solution.py:34
  132.9 1.0 copy-start.8
  132.9 1.1 copy-start.10
  132.9 1.2 copy-start.12
  132.9 1.3 copy-start.14
  133.0 1.5 copy-start.1
  133.0 1.7 %copy-start.4 = (bf16[2,192,1024]{2,1,0:T(8,128)(2,1)S(1)}, bf16[2,192,1024]{2,1,0:T(8,128)(2,1)}, u32[]{:S(2)}) copy-start(bf16[2,192,1024]{2,1,0:T(8,128)(2,1)} %copy-done.2) | copy-start | bytes 2359300
  133.0 2.0 %copy-start.6 = (bf16[2,192,1024]{2,1,0:T(8,128)(2,1)S(1)}, bf16[2,192,1024]{2,1,0:T(8,128)(2,1)}, u32[]{:S(2)}) copy-start(bf16[2,192,1024]{2,1,0:T(8,128)(2,1)} %copy-done.5) | copy-start | bytes 2359300
  145.9 4.3 %collective-permute-start.28 = (bf16[8,48,768]{2,1,0:T(8,128)(2,1)S(1)}, bf16[8,48,768]{2,1,0:T(8,128)(2,1)S(1)}, u32[]{:S(2)}, u32[]{:S(2)}) collective-permute-start(bf16[8,48,768]{2,1,0:T(8,128)(2,1)S(1)} %collective-permute-done.26.refs_15_.refs_11_), channel_id=1, source_target_pairs={{0,16},{16,0},{1,17},{17,1},{2,18},{18,2},{3,19},{19,3},{4,20},{20... | collective-permute-start | bytes 1769480 | tf_op jit(solution)/shard_map/ppermute | solution.py:34
  147.2 3.0 %collective-permute-start.29 = (bf16[8,48,768]{2,1,0:T(8,128)(2,1)S(1)}, bf16[8,48,768]{2,1,0:T(8,128)(2,1)S(1)}, u32[]{:S(2)}, u32[]{:S(2)}) collective-permute-start(bf16[8,48,768]{2,1,0:T(8,128)(2,1)S(1)} %collective-permute-done.27.refs_16_.refs_12_), channel_id=1, source_target_pairs={{0,16},{16,0},{1,17},{17,1},{2,18},{18,2},{3,19},{19,3},{4,20},{20... | collective-permute-start | bytes 1769480 | tf_op jit(solution)/shard_map/ppermute | solution.py:34
  147.3 11.6 %collective-permute-start.24 = (bf16[192,1024]{1,0:T(8,128)(2,1)S(1)}, bf16[192,1024]{1,0:T(8,128)(2,1)S(1)}, u32[]{:S(2)}, u32[]{:S(2)}) collective-permute-start(bf16[192,1024]{1,0:T(8,128)(2,1)S(1)} %slice_bitcast_fusion.7), channel_id=1, source_target_pairs={{0,1},{1,2},{2,3},{3,0},{4,5},{5,6},{6,7},{7,4},{8,9},{9,10},{10,1... | collective-permute-start | bytes 1179656 | tf_op jit(solution)/shard_map/ppermute | solution.py:34
  147.4 11.4 %collective-permute-start.25 = (bf16[192,1024]{1,0:T(8,128)(2,1)S(1)}, bf16[192,1024]{1,0:T(8,128)(2,1)S(1)}, u32[]{:S(2)}, u32[]{:S(2)}) collective-permute-start(bf16[192,1024]{1,0:T(8,128)(2,1)S(1)} %slice_bitcast_fusion.6), channel_id=1, source_target_pairs={{0,3},{1,0},{2,1},{3,2},{4,7},{5,4},{6,5},{7,6},{8,11},{9,8},{10,9... | collective-permute-start | bytes 1179656 | tf_op jit(solution)/shard_map/ppermute | solution.py:34

commit v5 on v4

--- a/solution.py
+++ b/solution.py
@@ -20,8 +20,8 @@
 ROWS = 1024
 KSLOT = 4 * ORBS
 CHUNK = 1024
-TILE = 256
-GRAM_VMEM = 24
+TILE = 512
+GRAM_VMEM = 32
 MIB = 1024 * 1024
 
 PAIRS = [(0, 1), (1, 0), (2, 3), (3, 2)]

time: 164 us -> 164 us (level)
  Pallas kernels: 28.7 us -> 26.4 us
  waiting for transfers between devices: 61.6 us -> 63.9 us
    pallas_call x3, Pallas kernels: 19 us -> 16.7 us  [gram(): pl.pallas_call(functools.partial(gram_kernel, slots, rows, pieces, len(ar...]
    ppermute x25, waiting for transfers between devices: 28.6 us -> 30.8 us  [shift(): return lax.ppermute(value, axis, [(i, (i + step) % n) for i in range(n)])]
  transfers between devices with their start and end apart: 32 -> 32, of which waited for: 11 -> 11; matrix products, arithmetic and copies ran while one was open for 3% -> 3% of each run, Pallas kernels for 15% -> 13%
where the time goes in v5:
time: 164 us
  waiting for transfers between devices  63.9 us (39%)
  starting transfers between devices  59.7 us (36%)
  Pallas kernels  26.4 us (16%)
  local copies, waits for them, and re-layouts  9.55 us (6%)
  other arithmetic  3.88 us (2%)
    ppermute x25, starting transfers between devices, shift(): return lax.ppermute(value, axis, [(i, (i + step) % n) for i in range(n)])  39.1 us
    ppermute x25, waiting for transfers between devices, shift(): return lax.ppermute(value, axis, [(i, (i + step) % n) for i in range(n)])  30.8 us
    all_to_all x1, waiting for transfers between devices, per_device(): by_y = lax.all_to_all(picked, 'y', 0, 0, tiled=True)  17.5 us
    pallas_call x3, Pallas kernels, gram(): pl.pallas_call(functools.partial(gram_kernel, slots, rows, pieces, len(ar...  16.7 us
    all_to_all x1, waiting for transfers between devices, per_device(): lax.all_to_all(jnp.concatenate([cols, cols]), ('zhi', 'zlo'), 0, 0, tiled...  11.1 us
    pallas_call x1, Pallas kernels, gather_points(): pl.pallas_call(gather_kernel, grid=(steps,), in_specs=[pl.BlockSpec((NPTS...  8.97 us
    all_to_all x1, starting transfers between devices, per_device(): lax.all_to_all(jnp.concatenate([cols, cols]), ('zhi', 'zlo'), 0, 0, tiled...  8.71 us
    unnamed x32, local copies, waits for them, and re-layouts  5.87 us
  transfers between devices with their start and end apart: 32, of which 11 were waited for; matrix products, arithmetic and copies ran while one was open for 3% of the time, Pallas kernels for 13%

profile of v5, /device:TPU:1, one launch (start us, length us, event | category | flops | bytes accessed | tf_op | source)
XLA Modules:
  0.0 163.7 jit_solution(9281882722369752867)
XLA Ops:
  0.0 1.2 pad_maximum_fusion.1.refs_0_
  1.2 2.6 %collective-permute-start = (bf16[2,192,1024]{2,1,0:T(8,128)(2,1)S(1)}, bf16[2,192,1024]{2,1,0:T(8,128)(2,1)S(1)}, u32[]{:S(2)}, u32[]{:S(2)}) collective-permute-start(bf16[2,192,1024]{2,1,0:T(8,128)(2,1)S(1)} %pad_maximum_fusion.1.refs_0_), channel_id=1, source_target_pairs={{0,4},{4,0},{8,12},{12,8},{1,5},{5,1},{9,13},{13,9},{2,6},{6,2},{1... | collective-permute-start | bytes 2359304 | tf_op jit(solution)/shard_map/ppermute | solution.py:200
  3.8 1.5 collective-permute-start.1
  5.3 1.3 collective-permute-start.2
  6.6 1.4 collective-permute-start.3
  8.1 0.9 reshape.16.points_ref
  9.1 9.0 %gather_points.1 = bf16[768,384]{1,0:T(8,128)(2,1)} custom-call(s32[768,1]{1,0:T(8,128)} %reshape.16.points_ref, bf16[192,6144]{1,0:T(8,128)(2,1)} %psi_ref.1, bf16[192,6144]{1,0:T(8,128)(2,1)} %phi_ref.1), custom_call_target="tpu_custom_call" | custom-call | flops 3623878656 | bytes 4718592 | tf_op jit(solution)/shard_map/gather_points/pallas_call | solution.py:69
  18.0 1.9 %collective-permute-done.refs_5_ = bf16[2,192,1024]{2,1,0:T(8,128)(2,1)S(1)} collective-permute-done((bf16[2,192,1024]{2,1,0:T(8,128)(2,1)S(1)}, bf16[2,192,1024]{2,1,0:T(8,128)(2,1)S(1)}, u32[]{:S(2)}, u32[]{:S(2)}) %collective-permute-start) | collective-permute-done | bytes 786464 | tf_op jit(solution)/shard_map/ppermute | solution.py:200
  20.0 4.8 %collective-permute-done.2.refs_3_ = bf16[2,192,1024]{2,1,0:T(8,128)(2,1)S(1)} collective-permute-done((bf16[2,192,1024]{2,1,0:T(8,128)(2,1)S(1)}, bf16[2,192,1024]{2,1,0:T(8,128)(2,1)S(1)}, u32[]{:S(2)}, u32[]{:S(2)}) %collective-permute-start.2) | collective-permute-done | bytes 786464 | tf_op jit(solution)/shard_map/ppermute | solution.py:34
  24.7 0.9 copy-done
  25.6 1.3 collective-permute-start.4
  26.9 1.0 collective-permute-start.6
  28.0 1.7 %collective-permute-start.7 = (bf16[2,192,1024]{2,1,0:T(8,128)(2,1)}, bf16[2,192,1024]{2,1,0:T(8,128)(2,1)}, u32[]{:S(2)}, u32[]{:S(2)}) collective-permute-start(bf16[2,192,1024]{2,1,0:T(8,128)(2,1)} %copy-done.5), channel_id=1, source_target_pairs={{0,3},{1,0},{2,1},{3,2},{4,7},{5,4},{6,5},{7,6},{8,11},{9,8},{10,9... | collective-permute-start | bytes 2359304 | tf_op jit(solution)/shard_map/ppermute | solution.py:34
  29.7 1.5 collective-permute-start.5
  31.2 3.5 %all-to-all-start = ((bf16[4,4,48,384]{3,2,1,0:T(8,128)(2,1)}), bf16[4,4,48,384]{3,2,1,0:T(8,128)(2,1)S(1)}, u32[]{:S(2)}, u32[]{:S(2)}) async-start(bf16[4,4,48,384]{3,2,1,0:T(8,128)(2,1)} %bitcast.31), calls=%async_computation | async-start | bytes 1179648 | tf_op jit(solution)/shard_map/all_to_all | solution.py:206
  34.8 17.5 %all-to-all-done.in_ref = bf16[4,4,48,384]{3,2,1,0:T(8,128)(2,1)S(1)} async-done(((bf16[4,4,48,384]{3,2,1,0:T(8,128)(2,1)}), bf16[4,4,48,384]{3,2,1,0:T(8,128)(2,1)S(1)}, u32[]{:S(2)}, u32[]{:S(2)}) %all-to-all-start) | async-done | bytes 589856 | tf_op jit(solution)/shard_map/all_to_all | solution.py:206
  53.0 1.2 broadcast_select_fusion.1.refs_10_
  54.3 1.2 pad_maximum_fusion
  55.5 8.7 %all-to-all-start.1 = ((bf16[8,2,48,768]{3,2,1,0:T(8,128)(2,1)}), bf16[8,2,48,768]{3,2,1,0:T(8,128)(2,1)S(1)}, u32[]{:S(2)}, u32[]{:S(2)}) async-start(bf16[8,2,48,768]{3,2,1,0:T(8,128)(2,1)} %pad_maximum_fusion), calls=%async_computation.1 | async-start | bytes 2359296 | tf_op jit(solution)/shard_map/all_to_all | solution.py:213
  65.0 1.0 slice_bitcast_fusion.8
  66.0 2.2 %collective-permute-start.9 = (bf16[192,1024]{1,0:T(8,128)(2,1)S(1)}, bf16[192,1024]{1,0:T(8,128)(2,1)S(1)}, u32[]{:S(2)}, u32[]{:S(2)}) collective-permute-start(bf16[192,1024]{1,0:T(8,128)(2,1)S(1)} %slice_bitcast_fusion.8), channel_id=1, source_target_pairs={{0,3},{1,0},{2,1},{3,2},{4,7},{5,4},{6,5},{7,6},{8,11},{9,8},{10,9... | collective-permute-start | bytes 1179656 | tf_op jit(solution)/shard_map/ppermute | solution.py:34
  68.3 1.0 slice_bitcast_fusion.4
  69.3 2.7 %collective-permute-start.11 = (bf16[192,1024]{1,0:T(8,128)(2,1)S(1)}, bf16[192,1024]{1,0:T(8,128)(2,1)S(1)}, u32[]{:S(2)}, u32[]{:S(2)}) collective-permute-start(bf16[192,1024]{1,0:T(8,128)(2,1)S(1)} %slice_bitcast_fusion.4), channel_id=1, source_target_pairs={{0,3},{1,0},{2,1},{3,2},{4,7},{5,4},{6,5},{7,6},{8,11},{9,8},{10,9... | collective-permute-start | bytes 1179656 | tf_op jit(solution)/shard_map/ppermute | solution.py:34
  72.2 0.8 copy-done.7
  73.0 0.8 copy-done.9
  73.7 7.0 %collective-permute-done.10.refs_7_ = bf16[192,1024]{1,0:T(8,128)(2,1)S(1)} collective-permute-done((bf16[192,1024]{1,0:T(8,128)(2,1)S(1)}, bf16[192,1024]{1,0:T(8,128)(2,1)S(1)}, u32[]{:S(2)}, u32[]{:S(2)}) %collective-permute-start.10) | collective-permute-done | bytes 393248 | tf_op jit(solution)/shard_map/ppermute | solution.py:34
  80.7 0.8 copy-done.11
  82.3 11.1 %all-to-all-done.1.refs_15_.refs_5_ = bf16[8,2,48,768]{3,2,1,0:T(8,128)(2,1)S(1)} async-done(((bf16[8,2,48,768]{3,2,1,0:T(8,128)(2,1)}), bf16[8,2,48,768]{3,2,1,0:T(8,128)(2,1)S(1)}, u32[]{:S(2)}, u32[]{:S(2)}) %all-to-all-start.1) | async-done | bytes 1179680 | tf_op jit(solution)/shard_map/all_to_all | solution.py:213
  93.5 2.6 %collective-permute-start.17 = (bf16[2,192,1024]{2,1,0:T(8,128)(2,1)S(1)}, bf16[2,192,1024]{2,1,0:T(8,128)(2,1)S(1)}, u32[]{:S(2)}, u32[]{:S(2)}) collective-permute-start(bf16[2,192,1024]{2,1,0:T(8,128)(2,1)S(1)} %broadcast_select_fusion.1.refs_10_), channel_id=1, source_target_pairs={{0,3},{1,0},{2,1},{3,2},{4,7},{5,4},{6,5},{7,6},{8,11},{9,8},{10,9... | collective-permute-start | bytes 2359304 | tf_op jit(solution)/shard_map/ppermute | solution.py:34
  96.1 1.3 collective-permute-start.12
  97.4 1.5 collective-permute-start.13
  98.9 1.5 collective-permute-start.14
  100.3 9.8 %collective-permute-done.15.refs_13_ = bf16[2,192,1024]{2,1,0:T(8,128)(2,1)S(1)} collective-permute-done((bf16[2,192,1024]{2,1,0:T(8,128)(2,1)S(1)}, bf16[2,192,1024]{2,1,0:T(8,128)(2,1)S(1)}, u32[]{:S(2)}, u32[]{:S(2)}) %collective-permute-start.15) | collective-permute-done | bytes 786464 | tf_op jit(solution)/shard_map/ppermute | solution.py:34
  110.3 2.7 %collective-permute-start.18 = (bf16[192,1024]{1,0:T(8,128)(2,1)S(1)}, bf16[192,1024]{1,0:T(8,128)(2,1)S(1)}, u32[]{:S(2)}, u32[]{:S(2)}) collective-permute-start(bf16[192,1024]{1,0:T(8,128)(2,1)S(1)} %slice_bitcast_fusion.2), channel_id=1, source_target_pairs={{0,3},{1,0},{2,1},{3,2},{4,7},{5,4},{6,5},{7,6},{8,11},{9,8},{10,9... | collective-permute-start | bytes 1179656 | tf_op jit(solution)/shard_map/ppermute | solution.py:34
  113.0 2.6 %collective-permute-done.14 = bf16[2,192,1024]{2,1,0:T(8,128)(2,1)S(1)} collective-permute-done((bf16[2,192,1024]{2,1,0:T(8,128)(2,1)}, bf16[2,192,1024]{2,1,0:T(8,128)(2,1)S(1)}, u32[]{:S(2)}, u32[]{:S(2)}) %collective-permute-start.14) | collective-permute-done | bytes 786464 | tf_op jit(solution)/shard_map/ppermute | solution.py:197
  115.7 5.6 %collective-permute-start.21 = (bf16[8,2,48,768]{3,2,1,0:T(8,128)(2,1)S(1)}, bf16[8,2,48,768]{3,2,1,0:T(8,128)(2,1)S(1)}, u32[]{:S(2)}, u32[]{:S(2)}) collective-permute-start(bf16[8,2,48,768]{3,2,1,0:T(8,128)(2,1)S(1)} %all-to-all-done.1.refs_15_.refs_5_), channel_id=1, source_target_pairs={{0,16},{16,0},{1,17},{17,1},{2,18},{18,2},{3,19},{19,3},{4,20},{20... | collective-permute-start | bytes 3538952 | tf_op jit(solution)/shard_map/ppermute | solution.py:34
  121.3 4.5 %collective-permute-start.22 = (bf16[8,2,48,768]{3,2,0,1:T(8,128)(2,1)S(1)}, bf16[8,2,48,768]{3,2,0,1:T(8,128)(2,1)S(1)}, u32[]{:S(2)}, u32[]{:S(2)}) collective-permute-start(bf16[8,2,48,768]{3,2,0,1:T(8,128)(2,1)S(1)} %collective-permute-done.12), channel_id=1, source_target_pairs={{0,16},{16,0},{1,17},{17,1},{2,18},{18,2},{3,19},{19,3},{4,20},{20... | collective-permute-start | bytes 3538952 | tf_op jit(solution)/shard_map/ppermute | solution.py:34
  126.0 2.7 %collective-permute-start.20 = (bf16[2,192,1024]{2,1,0:T(8,128)(2,1)S(1)}, bf16[2,192,1024]{2,1,0:T(8,128)(2,1)S(1)}, u32[]{:S(2)}, u32[]{:S(2)}) collective-permute-start(bf16[2,192,1024]{2,1,0:T(8,128)(2,1)S(1)} %broadcast_select_fusion.refs_0_), channel_id=1, source_target_pairs={{0,3},{1,0},{2,1},{3,2},{4,7},{5,4},{6,5},{7,6},{8,11},{9,8},{10,9... | collective-permute-start | bytes 2359304 | tf_op jit(solution)/shard_map/ppermute | solution.py:34
  128.8 1.3 collective-permute-done.23
  130.0 1.1 collective-permute-start.26
  131.2 1.6 collective-permute-start.27
  135.0 7.7 %gram_near.1.refs_15_ = f32[2,576,1024]{2,1,0:T(8,128)S(1)} custom-call(s32[4]{0:T(128)S(1)} %pad_add_fusion.pos_ref, bf16[2,192,1024]{2,1,0:T(8,128)(2,1)S(1)} %pad_maximum_fusion.1.refs_0_, bf16[2,192,1024]{2,1,0:T(8,128)(2,1)S(1)} %copy-done.1, bf16[192,1024]{1,0:T(8,128)(2,1)S(1)} %copy-done.8, bf16[2,192,1024]{2,1,0:T(8,128)(2,1)S(1)} %collective-permute-done.2.refs_3_, ...), custom_call_target="tpu_custom_call" | custom-call | flops 5435817984 | bytes 8388608 | tf_op jit(solution)/shard_map/gram_near/pallas_call | solution.py:172
  142.7 3.2 %collective-permute-done.19.refs_3_ = bf16[2,192,1024]{2,1,0:T(8,128)(2,1)S(1)} collective-permute-done((bf16[2,192,1024]{2,1,0:T(8,128)(2,1)S(1)}, bf16[2,192,1024]{2,1,0:T(8,128)(2,1)S(1)}, u32[]{:S(2)}, u32[]{:S(2)}) %collective-permute-start.19) | collective-permute-done | bytes 786464 | tf_op jit(solution)/shard_map/ppermute | solution.py:34
  145.9 1.2 collective-permute-start.28
  147.4 2.7 %collective-permute-start.25 = (bf16[192,1024]{1,0:T(8,128)(2,1)S(1)}, bf16[192,1024]{1,0:T(8,128)(2,1)S(1)}, u32[]{:S(2)}, u32[]{:S(2)}) collective-permute-start(bf16[192,1024]{1,0:T(8,128)(2,1)S(1)} %slice_bitcast_fusion.6), channel_id=1, source_target_pairs={{0,3},{1,0},{2,1},{3,2},{4,7},{5,4},{6,5},{7,6},{8,11},{9,8},{10,9... | collective-permute-start | bytes 1179656 | tf_op jit(solution)/shard_map/ppermute | solution.py:34
  150.2 4.1 %gram_far.1.refs_16_ = f32[2,192,1024]{2,1,0:T(8,128)S(1)} custom-call(s32[4]{0:T(128)S(1)} %pad_add_fusion.pos_ref, bf16[2,192,1024]{2,1,0:T(8,128)(2,1)S(1)} %pad_maximum_fusion.1.refs_0_, bf16[2,192,1024]{2,1,0:T(8,128)(2,1)S(1)} %copy-done.1, bf16[192,1024]{1,0:T(8,128)(2,1)S(1)} %copy-done.8, bf16[2,192,1024]{2,1,0:T(8,128)(2,1)S(1)} %collective-permute-done.2.refs_3_, ...), custom_call_target="tpu_custom_call" | custom-call | flops 1811939328 | bytes 8388608 | tf_op jit(solution)/shard_map/gram_far/pallas_call | solution.py:172
  154.3 4.6 %collective-permute-done.24.refs_2_ = bf16[192,1024]{1,0:T(8,128)(2,1)S(1)} collective-permute-done((bf16[192,1024]{1,0:T(8,128)(2,1)S(1)}, bf16[192,1024]{1,0:T(8,128)(2,1)S(1)}, u32[]{:S(2)}, u32[]{:S(2)}) %collective-permute-start.24) | collective-permute-done | bytes 393248 | tf_op jit(solution)/shard_map/ppermute | solution.py:34
  158.9 4.8 %gram_last.1 = bf16[2,4,2,48,1024]{4,3,2,1,0:T(8,128)(2,1)} custom-call(s32[4]{0:T(128)S(1)} %pad_add_fusion.pos_ref, bf16[2,192,1024]{2,1,0:T(8,128)(2,1)S(1)} %broadcast_select_fusion.refs_0_, bf16[2,192,1024]{2,1,0:T(8,128)(2,1)S(1)} %collective-permute-done.20.refs_1_, bf16[192,1024]{1,0:T(8,128)(2,1)S(1)} %collective-permute-done.24.refs_2_, ...), custom_call_target="tpu_custom_call" | custom-call | flops 2415919104 | bytes 8388608 | tf_op jit(solution)/shard_map/gram_last/pallas_call | solution.py:172
  (75 shorter events, 5.8 us)
Async XLA Ops:
  0.0 8.0 %copy-start.15 = (s32[768]{0:T(1024)S(1)}, s32[768]{0:T(1024)}, u32[]{:S(2)}) copy-start(s32[768]{0:T(1024)} %param.9) | copy-start | bytes 9220
  1.2 18.8 %collective-permute-start = (bf16[2,192,1024]{2,1,0:T(8,128)(2,1)S(1)}, bf16[2,192,1024]{2,1,0:T(8,128)(2,1)S(1)}, u32[]{:S(2)}, u32[]{:S(2)}) collective-permute-start(bf16[2,192,1024]{2,1,0:T(8,128)(2,1)S(1)} %pad_maximum_fusion.1.refs_0_), channel_id=1, source_target_pairs={{0,4},{4,0},{8,12},{12,8},{1,5},{5,1},{9,13},{13,9},{2,6},{6,2},{1... | collective-permute-start | bytes 2359304 | tf_op jit(solution)/shard_map/ppermute | solution.py:200
  3.8 16.2 %collective-permute-start.1 = (bf16[2,192,1024]{2,1,0:T(8,128)(2,1)S(1)}, bf16[2,192,1024]{2,1,0:T(8,128)(2,1)}, u32[]{:S(2)}, u32[]{:S(2)}) collective-permute-start(bf16[2,192,1024]{2,1,0:T(8,128)(2,1)S(1)} %pad_maximum_fusion.1.refs_0_), channel_id=1, source_target_pairs={{4,8},{8,4},{5,9},{9,5},{6,10},{10,6},{7,11},{11,7},{20,24},{24,20... | collective-permute-start | bytes 2359304 | tf_op jit(solution)/shard_map/ppermute | solution.py:201
  5.3 19.4 %collective-permute-start.2 = (bf16[2,192,1024]{2,1,0:T(8,128)(2,1)S(1)}, bf16[2,192,1024]{2,1,0:T(8,128)(2,1)S(1)}, u32[]{:S(2)}, u32[]{:S(2)}) collective-permute-start(bf16[2,192,1024]{2,1,0:T(8,128)(2,1)S(1)} %pad_maximum_fusion.1.refs_0_), channel_id=1, source_target_pairs={{0,1},{1,2},{2,3},{3,0},{4,5},{5,6},{6,7},{7,4},{8,9},{9,10},{10,1... | collective-permute-start | bytes 2359304 | tf_op jit(solution)/shard_map/ppermute | solution.py:34
  6.6 18.1 %collective-permute-start.3 = (bf16[2,192,1024]{2,1,0:T(8,128)(2,1)S(1)}, bf16[2,192,1024]{2,1,0:T(8,128)(2,1)S(1)}, u32[]{:S(2)}, u32[]{:S(2)}) collective-permute-start(bf16[2,192,1024]{2,1,0:T(8,128)(2,1)S(1)} %pad_maximum_fusion.1.refs_0_), channel_id=1, source_target_pairs={{0,3},{1,0},{2,1},{3,2},{4,7},{5,4},{6,5},{7,6},{8,11},{9,8},{10,9... | collective-permute-start | bytes 2359304 | tf_op jit(solution)/shard_map/ppermute | solution.py:34
  20.0 5.7 %copy-start.5 = (bf16[2,192,1024]{2,1,0:T(8,128)(2,1)}, bf16[2,192,1024]{2,1,0:T(8,128)(2,1)S(1)}, u32[]{:S(2)}) copy-start(bf16[2,192,1024]{2,1,0:T(8,128)(2,1)S(1)} %collective-permute-done.refs_5_) | copy-start | bytes 2359300
  24.7 0.9 copy-start
  25.6 27.4 %collective-permute-start.4 = (bf16[2,192,1024]{2,1,0:T(8,128)(2,1)}, bf16[2,192,1024]{2,1,0:T(8,128)(2,1)}, u32[]{:S(2)}, u32[]{:S(2)}) collective-permute-start(bf16[2,192,1024]{2,1,0:T(8,128)(2,1)} %collective-permute-done.1), channel_id=1, source_target_pairs={{4,0},{8,12},{5,1},{9,13},{6,2},{10,14},{7,3},{11,15},{20,16},{24,... | collective-permute-start | bytes 2359304 | tf_op jit(solution)/shard_map/ppermute | solution.py:197
  26.9 27.3 %collective-permute-start.6 = (bf16[2,192,1024]{2,1,0:T(8,128)(2,1)}, bf16[2,192,1024]{2,1,0:T(8,128)(2,1)S(1)}, u32[]{:S(2)}, u32[]{:S(2)}) collective-permute-start(bf16[2,192,1024]{2,1,0:T(8,128)(2,1)} %copy-done.5), channel_id=1, source_target_pairs={{0,1},{1,2},{2,3},{3,0},{4,5},{5,6},{6,7},{7,4},{8,9},{9,10},{10,1... | collective-permute-start | bytes 2359304 | tf_op jit(solution)/shard_map/ppermute | solution.py:34
  28.0 26.3 %collective-permute-start.7 = (bf16[2,192,1024]{2,1,0:T(8,128)(2,1)}, bf16[2,192,1024]{2,1,0:T(8,128)(2,1)}, u32[]{:S(2)}, u32[]{:S(2)}) collective-permute-start(bf16[2,192,1024]{2,1,0:T(8,128)(2,1)} %copy-done.5), channel_id=1, source_target_pairs={{0,3},{1,0},{2,1},{3,2},{4,7},{5,4},{6,5},{7,6},{8,11},{9,8},{10,9... | collective-permute-start | bytes 2359304 | tf_op jit(solution)/shard_map/ppermute | solution.py:34
  29.7 24.6 %collective-permute-start.5 = (bf16[2,192,1024]{2,1,0:T(8,128)(2,1)}, bf16[2,192,1024]{2,1,0:T(8,128)(2,1)}, u32[]{:S(2)}, u32[]{:S(2)}) collective-permute-start(bf16[2,192,1024]{2,1,0:T(8,128)(2,1)} %copy-done.5), channel_id=1, source_target_pairs={{4,8},{8,4},{5,9},{9,5},{6,10},{10,6},{7,11},{11,7},{20,24},{24,20... | collective-permute-start | bytes 2359304 | tf_op jit(solution)/shard_map/ppermute | solution.py:209
  31.2 21.1 %all-to-all-start = ((bf16[4,4,48,384]{3,2,1,0:T(8,128)(2,1)}), bf16[4,4,48,384]{3,2,1,0:T(8,128)(2,1)S(1)}, u32[]{:S(2)}, u32[]{:S(2)}) async-start(bf16[4,4,48,384]{3,2,1,0:T(8,128)(2,1)} %bitcast.31), calls=%async_computation | async-start | bytes 1179648 | tf_op jit(solution)/shard_map/all_to_all | solution.py:206
  54.2 1.3 copy-start.2
  55.5 37.8 %all-to-all-start.1 = ((bf16[8,2,48,768]{3,2,1,0:T(8,128)(2,1)}), bf16[8,2,48,768]{3,2,1,0:T(8,128)(2,1)S(1)}, u32[]{:S(2)}, u32[]{:S(2)}) async-start(bf16[8,2,48,768]{3,2,1,0:T(8,128)(2,1)} %pad_maximum_fusion), calls=%async_computation.1 | async-start | bytes 2359296 | tf_op jit(solution)/shard_map/all_to_all | solution.py:213
  64.3 3.9 %copy-start.3 = (bf16[2,192,1024]{2,1,0:T(8,128)(2,1)S(1)}, bf16[2,192,1024]{2,1,0:T(8,128)(2,1)}, u32[]{:S(2)}) copy-start(bf16[2,192,1024]{2,1,0:T(8,128)(2,1)} %copy-done.2) | copy-start | bytes 2359300
  64.3 7.9 %collective-permute-start.8 = (bf16[192,1024]{1,0:T(8,128)(2,1)S(1)}, bf16[192,1024]{1,0:T(8,128)(2,1)S(1)}, u32[]{:S(2)}, u32[]{:S(2)}) collective-permute-start(bf16[192,1024]{1,0:T(8,128)(2,1)S(1)} %slice_bitcast_fusion.9), channel_id=1, source_target_pairs={{0,1},{1,2},{2,3},{3,0},{4,5},{5,6},{6,7},{7,4},{8,9},{9,10},{10,1... | collective-permute-start | bytes 1179656 | tf_op jit(solution)/shard_map/ppermute | solution.py:34
  66.0 7.0 %collective-permute-start.9 = (bf16[192,1024]{1,0:T(8,128)(2,1)S(1)}, bf16[192,1024]{1,0:T(8,128)(2,1)S(1)}, u32[]{:S(2)}, u32[]{:S(2)}) collective-permute-start(bf16[192,1024]{1,0:T(8,128)(2,1)S(1)} %slice_bitcast_fusion.8), channel_id=1, source_target_pairs={{0,3},{1,0},{2,1},{3,2},{4,7},{5,4},{6,5},{7,6},{8,11},{9,8},{10,9... | collective-permute-start | bytes 1179656 | tf_op jit(solution)/shard_map/ppermute | solution.py:34
  68.2 12.6 %collective-permute-start.10 = (bf16[192,1024]{1,0:T(8,128)(2,1)S(1)}, bf16[192,1024]{1,0:T(8,128)(2,1)S(1)}, u32[]{:S(2)}, u32[]{:S(2)}) collective-permute-start(bf16[192,1024]{1,0:T(8,128)(2,1)S(1)} %slice_bitcast_fusion.5), channel_id=1, source_target_pairs={{0,1},{1,2},{2,3},{3,0},{4,5},{5,6},{6,7},{7,4},{8,9},{9,10},{10,1... | collective-permute-start | bytes 1179656 | tf_op jit(solution)/shard_map/ppermute | solution.py:34
  69.3 12.2 %collective-permute-start.11 = (bf16[192,1024]{1,0:T(8,128)(2,1)S(1)}, bf16[192,1024]{1,0:T(8,128)(2,1)S(1)}, u32[]{:S(2)}, u32[]{:S(2)}) collective-permute-start(bf16[192,1024]{1,0:T(8,128)(2,1)S(1)} %slice_bitcast_fusion.4), channel_id=1, source_target_pairs={{0,3},{1,0},{2,1},{3,2},{4,7},{5,4},{6,5},{7,6},{8,11},{9,8},{10,9... | collective-permute-start | bytes 1179656 | tf_op jit(solution)/shard_map/ppermute | solution.py:34
  72.2 0.8 copy-start.7
  73.0 0.8 copy-start.9
  80.7 0.8 copy-start.11
  81.5 0.8 copy-start.13
  93.3 16.8 %collective-permute-start.15 = (bf16[2,192,1024]{2,1,0:T(8,128)(2,1)S(1)}, bf16[2,192,1024]{2,1,0:T(8,128)(2,1)S(1)}, u32[]{:S(2)}, u32[]{:S(2)}) collective-permute-start(bf16[2,192,1024]{2,1,0:T(8,128)(2,1)S(1)} %broadcast_select_fusion.1.refs_10_), channel_id=1, source_target_pairs={{0,1},{1,2},{2,3},{3,0},{4,5},{5,6},{6,7},{7,4},{8,9},{9,10},{10,1... | collective-permute-start | bytes 2359304 | tf_op jit(solution)/shard_map/ppermute | solution.py:34
  93.5 16.8 %collective-permute-start.17 = (bf16[2,192,1024]{2,1,0:T(8,128)(2,1)S(1)}, bf16[2,192,1024]{2,1,0:T(8,128)(2,1)S(1)}, u32[]{:S(2)}, u32[]{:S(2)}) collective-permute-start(bf16[2,192,1024]{2,1,0:T(8,128)(2,1)S(1)} %broadcast_select_fusion.1.refs_10_), channel_id=1, source_target_pairs={{0,3},{1,0},{2,1},{3,2},{4,7},{5,4},{6,5},{7,6},{8,11},{9,8},{10,9... | collective-permute-start | bytes 2359304 | tf_op jit(solution)/shard_map/ppermute | solution.py:34
  96.1 25.2 %collective-permute-start.12 = (bf16[8,2,48,768]{3,2,0,1:T(8,128)(2,1)S(1)}, bf16[8,2,48,768]{3,2,0,1:T(8,128)(2,1)S(1)}, u32[]{:S(2)}, u32[]{:S(2)}) collective-permute-start(bf16[8,2,48,768]{3,2,0,1:T(8,128)(2,1)S(1)} %copy.38), channel_id=1, source_target_pairs={{0,32},{32,64},{64,96},{96,0},{1,33},{33,65},{65,97},{97,1},{2,34}... | collective-permute-start | bytes 3538952 | tf_op jit(solution)/shard_map/ppermute | solution.py:34
  97.4 23.9 %collective-permute-start.13 = (bf16[8,2,48,768]{3,2,0,1:T(8,128)(2,1)S(1)}, bf16[8,2,48,768]{3,2,0,1:T(8,128)(2,1)S(1)}, u32[]{:S(2)}, u32[]{:S(2)}) collective-permute-start(bf16[8,2,48,768]{3,2,0,1:T(8,128)(2,1)S(1)} %copy.38), channel_id=1, source_target_pairs={{0,96},{32,0},{64,32},{96,64},{1,97},{33,1},{65,33},{97,65},{2,98}... | collective-permute-start | bytes 3538952 | tf_op jit(solution)/shard_map/ppermute | solution.py:34
  98.9 16.7 %collective-permute-start.14 = (bf16[2,192,1024]{2,1,0:T(8,128)(2,1)}, bf16[2,192,1024]{2,1,0:T(8,128)(2,1)S(1)}, u32[]{:S(2)}, u32[]{:S(2)}) collective-permute-start(bf16[2,192,1024]{2,1,0:T(8,128)(2,1)} %collective-permute-done.5), channel_id=1, source_target_pairs={{4,0},{8,12},{5,1},{9,13},{6,2},{10,14},{7,3},{11,15},{20,16},{24,... | collective-permute-start | bytes 2359304 | tf_op jit(solution)/shard_map/ppermute | solution.py:197
  110.2 11.1 %collective-permute-start.16 = (bf16[192,1024]{1,0:T(8,128)(2,1)S(1)}, bf16[192,1024]{1,0:T(8,128)(2,1)S(1)}, u32[]{:S(2)}, u32[]{:S(2)}) collective-permute-start(bf16[192,1024]{1,0:T(8,128)(2,1)S(1)} %slice_bitcast_fusion.3), channel_id=1, source_target_pairs={{0,1},{1,2},{2,3},{3,0},{4,5},{5,6},{6,7},{7,4},{8,9},{9,10},{10,1... | collective-permute-start | bytes 1179656 | tf_op jit(solution)/shard_map/ppermute | solution.py:34
  110.3 11.0 %collective-permute-start.18 = (bf16[192,1024]{1,0:T(8,128)(2,1)S(1)}, bf16[192,1024]{1,0:T(8,128)(2,1)S(1)}, u32[]{:S(2)}, u32[]{:S(2)}) collective-permute-start(bf16[192,1024]{1,0:T(8,128)(2,1)S(1)} %slice_bitcast_fusion.2), channel_id=1, source_target_pairs={{0,3},{1,0},{2,1},{3,2},{4,7},{5,4},{6,5},{7,6},{8,11},{9,8},{10,9... | collective-permute-start | bytes 1179656 | tf_op jit(solution)/shard_map/ppermute | solution.py:34
  115.7 13.0 %collective-permute-start.21 = (bf16[8,2,48,768]{3,2,1,0:T(8,128)(2,1)S(1)}, bf16[8,2,48,768]{3,2,1,0:T(8,128)(2,1)S(1)}, u32[]{:S(2)}, u32[]{:S(2)}) collective-permute-start(bf16[8,2,48,768]{3,2,1,0:T(8,128)(2,1)S(1)} %all-to-all-done.1.refs_15_.refs_5_), channel_id=1, source_target_pairs={{0,16},{16,0},{1,17},{17,1},{2,18},{18,2},{3,19},{19,3},{4,20},{20... | collective-permute-start | bytes 3538952 | tf_op jit(solution)/shard_map/ppermute | solution.py:34
  121.3 7.4 %collective-permute-start.22 = (bf16[8,2,48,768]{3,2,0,1:T(8,128)(2,1)S(1)}, bf16[8,2,48,768]{3,2,0,1:T(8,128)(2,1)S(1)}, u32[]{:S(2)}, u32[]{:S(2)}) collective-permute-start(bf16[8,2,48,768]{3,2,0,1:T(8,128)(2,1)S(1)} %collective-permute-done.12), channel_id=1, source_target_pairs={{0,16},{16,0},{1,17},{17,1},{2,18},{18,2},{3,19},{19,3},{4,20},{20... | collective-permute-start | bytes 3538952 | tf_op jit(solution)/shard_map/ppermute | solution.py:34
  125.9 4.2 %collective-permute-start.23 = (bf16[8,2,48,768]{3,2,0,1:T(8,128)(2,1)S(1)}, bf16[8,2,48,768]{3,2,0,1:T(8,128)(2,1)S(1)}, u32[]{:S(2)}, u32[]{:S(2)}) collective-permute-start(bf16[8,2,48,768]{3,2,0,1:T(8,128)(2,1)S(1)} %collective-permute-done.13), channel_id=1, source_target_pairs={{0,16},{16,0},{1,17},{17,1},{2,18},{18,2},{3,19},{19,3},{4,20},{20... | collective-permute-start | bytes 3538952 | tf_op jit(solution)/shard_map/ppermute | solution.py:34
  126.0 19.9 %collective-permute-start.19 = (bf16[2,192,1024]{2,1,0:T(8,128)(2,1)S(1)}, bf16[2,192,1024]{2,1,0:T(8,128)(2,1)S(1)}, u32[]{:S(2)}, u32[]{:S(2)}) collective-permute-start(bf16[2,192,1024]{2,1,0:T(8,128)(2,1)S(1)} %broadcast_select_fusion.refs_0_), channel_id=1, source_target_pairs={{0,1},{1,2},{2,3},{3,0},{4,5},{5,6},{6,7},{7,4},{8,9},{9,10},{10,1... | collective-permute-start | bytes 2359304 | tf_op jit(solution)/shard_map/ppermute | solution.py:34
  126.0 19.9 %collective-permute-start.20 = (bf16[2,192,1024]{2,1,0:T(8,128)(2,1)S(1)}, bf16[2,192,1024]{2,1,0:T(8,128)(2,1)S(1)}, u32[]{:S(2)}, u32[]{:S(2)}) collective-permute-start(bf16[2,192,1024]{2,1,0:T(8,128)(2,1)S(1)} %broadcast_select_fusion.refs_0_), channel_id=1, source_target_pairs={{0,3},{1,0},{2,1},{3,2},{4,7},{5,4},{6,5},{7,6},{8,11},{9,8},{10,9... | collective-permute-start | bytes 2359304 | tf_op jit(solution)/shard_map/ppermute | solution.py:34
  130.0 15.9 %collective-permute-start.26 = (bf16[8,48,768]{2,1,0:T(8,128)(2,1)S(1)}, bf16[8,48,768]{2,1,0:T(8,128)(2,1)S(1)}, u32[]{:S(2)}, u32[]{:S(2)}) collective-permute-start(bf16[8,48,768]{2,1,0:T(8,128)(2,1)S(1)} %get-tuple-element.46), channel_id=1, source_target_pairs={{0,32},{32,64},{64,96},{96,0},{1,33},{33,65},{65,97},{97,1},{2,34}... | collective-permute-start | bytes 1769480 | tf_op jit(solution)/shard_map/ppermute | solution.py:34
  131.2 16.0 %collective-permute-start.27 = (bf16[8,48,768]{2,1,0:T(8,128)(2,1)S(1)}, bf16[8,48,768]{2,1,0:T(8,128)(2,1)S(1)}, u32[]{:S(2)}, u32[]{:S(2)}) collective-permute-start(bf16[8,48,768]{2,1,0:T(8,128)(2,1)S(1)} %get-tuple-element.47), channel_id=1, source_target_pairs={{0,96},{32,0},{64,32},{96,64},{1,97},{33,1},{65,33},{97,65},{2,98}... | collective-permute-start | bytes 1769480 | tf_op jit(solution)/shard_map/ppermute | solution.py:34
  132.9 1.0 copy-start.8
  132.9 1.1 copy-start.10
  132.9 1.2 copy-start.12
  132.9 1.3 copy-start.14
  133.0 1.5 copy-start.1
  133.0 1.7 %copy-start.4 = (bf16[2,192,1024]{2,1,0:T(8,128)(2,1)S(1)}, bf16[2,192,1024]{2,1,0:T(8,128)(2,1)}, u32[]{:S(2)}) copy-start(bf16[2,192,1024]{2,1,0:T(8,128)(2,1)} %copy-done.2) | copy-start | bytes 2359300
  133.0 2.0 %copy-start.6 = (bf16[2,192,1024]{2,1,0:T(8,128)(2,1)S(1)}, bf16[2,192,1024]{2,1,0:T(8,128)(2,1)}, u32[]{:S(2)}) copy-start(bf16[2,192,1024]{2,1,0:T(8,128)(2,1)} %copy-done.5) | copy-start | bytes 2359300
  145.9 4.3 %collective-permute-start.28 = (bf16[8,48,768]{2,1,0:T(8,128)(2,1)S(1)}, bf16[8,48,768]{2,1,0:T(8,128)(2,1)S(1)}, u32[]{:S(2)}, u32[]{:S(2)}) collective-permute-start(bf16[8,48,768]{2,1,0:T(8,128)(2,1)S(1)} %collective-permute-done.26.refs_15_.refs_11_), channel_id=1, source_target_pairs={{0,16},{16,0},{1,17},{17,1},{2,18},{18,2},{3,19},{19,3},{4,20},{20... | collective-permute-start | bytes 1769480 | tf_op jit(solution)/shard_map/ppermute | solution.py:34
  147.2 3.0 %collective-permute-start.29 = (bf16[8,48,768]{2,1,0:T(8,128)(2,1)S(1)}, bf16[8,48,768]{2,1,0:T(8,128)(2,1)S(1)}, u32[]{:S(2)}, u32[]{:S(2)}) collective-permute-start(bf16[8,48,768]{2,1,0:T(8,128)(2,1)S(1)} %collective-permute-done.27.refs_16_.refs_12_), channel_id=1, source_target_pairs={{0,16},{16,0},{1,17},{17,1},{2,18},{18,2},{3,19},{19,3},{4,20},{20... | collective-permute-start | bytes 1769480 | tf_op jit(solution)/shard_map/ppermute | solution.py:34
  147.3 11.6 %collective-permute-start.24 = (bf16[192,1024]{1,0:T(8,128)(2,1)S(1)}, bf16[192,1024]{1,0:T(8,128)(2,1)S(1)}, u32[]{:S(2)}, u32[]{:S(2)}) collective-permute-start(bf16[192,1024]{1,0:T(8,128)(2,1)S(1)} %slice_bitcast_fusion.7), channel_id=1, source_target_pairs={{0,1},{1,2},{2,3},{3,0},{4,5},{5,6},{6,7},{7,4},{8,9},{9,10},{10,1... | collective-permute-start | bytes 1179656 | tf_op jit(solution)/shard_map/ppermute | solution.py:34
  147.4 11.4 %collective-permute-start.25 = (bf16[192,1024]{1,0:T(8,128)(2,1)S(1)}, bf16[192,1024]{1,0:T(8,128)(2,1)S(1)}, u32[]{:S(2)}, u32[]{:S(2)}) collective-permute-start(bf16[192,1024]{1,0:T(8,128)(2,1)S(1)} %slice_bitcast_fusion.6), channel_id=1, source_target_pairs={{0,3},{1,0},{2,1},{3,2},{4,7},{5,4},{6,5},{7,6},{8,11},{9,8},{10,9... | collective-permute-start | bytes 1179656 | tf_op jit(solution)/shard_map/ppermute | solution.py:34
